TPU v7x, 32 devices: a whole 2x2x4 slice. The times are simulated.
32 devices in a mesh: samp: 4 (over z), row: 4 (over y, x), col: 2 (over core).
Axes of the slice: x: 2, y: 2, z: 4, core: 2. Of those that a mesh axis runs over, the one named last changes fastest.
Arguments:
- genotypes: int32 [2048, 2048], P('samp', 'row'), may hold values from 0 to 2, as said below
- frequencies: float32 [2048], P('row'), may hold values from 0.25 to 0.5, as said below
- trait_scores: float32 [64, 2048], P(None, 'row'), may hold values from -6 to 6
- typed_mask: int32 [2048], P('row'), may hold values 0 or 1
- panel_index: int32 [1], replicated, may hold values from 0 to 127
Outputs:
- conditioned: float32 [2048, 2048], P('row', 'col')
- whitened: float32 [64, 1024], replicated
- residual: float32 [64, 2048], P(None, 'row')
Inputs may be any that keep to these rules, and one draw needn't show every extreme that they name: `genotypes`: each sample's dosage at a variant is its number of the variant's allele over two haplotypes, with the allele's chance the variant's frequency. frequencies are multiples of 1/64.
All inputs are finite; a program needn't handle non-finite values. No bound on the sum of `typed_mask` on one device may be relied on, other than what follows from the above.
Results may differ from a plain program's by a relative error of at most 0.0045.
Values may be sent and summed in bfloat16 or wider, within the bound.
No kernel may reach another device: no remote copies, remote signals or barrier semaphores. Data moves between devices by JAX's collectives and lax.ppermute only.
A program may use at most 64 MiB of HBM per device.

v0:
```python
import functools

import jax
import jax.numpy as jnp
from jax import lax
from jax.experimental import pallas as pl
from jax.experimental.pallas import tpu as pltpu
from jax.sharding import Mesh
from jax.sharding import PartitionSpec as P

ridge = 0.1
F32 = jnp.float32
BF16 = jnp.bfloat16
NN = (((1,), (0,)), ((), ()))
NT = (((1,), (1,)), ((), ()))
block = 128
sublanes = 8
vmem_bytes = 58 * 2**20


def dot1(a, b, dims):
    return lax.dot_general(a, b, dims, preferred_element_type=F32)


def split(x):
    high = x.astype(BF16)
    return high, (x - high.astype(F32)).astype(BF16)


def dot3(a, b, dims):
    (along_a,), (along_b,) = dims[0]
    left = jnp.concatenate([a[0], a[0], a[1]], axis=along_a)
    right = jnp.concatenate([b[0], b[1], b[0]], axis=along_b)
    return dot1(left, right, dims)


def row_to_all(v, i):
    return jnp.broadcast_to(v[i : i + 1, :], v.shape)


def lane_to_all(v, j):
    return jnp.take_along_axis(v, jnp.full(v.shape, j, jnp.int32), axis=1)


def take_away(base, coefs, rows):
    t = [c * r for c, r in zip(coefs, rows)]
    return base - (((t[0] + t[1]) + (t[2] + t[3])) + ((t[4] + t[5]) + (t[6] + t[7])))


def inverse_factor(rows):
    count = block // sublanes
    sub = lax.broadcasted_iota(jnp.int32, (sublanes, block), 0)
    lane = lax.broadcasted_iota(jnp.int32, (sublanes, block), 1)
    rows = list(rows)
    out = []
    diag = [lane_to_all(rows[0], j) for j in range(sublanes)]
    for p in range(count):
        first = sublanes * p
        inside = (lane >= first) & (lane < first + sublanes)
        work = jnp.where(inside, jnp.where(lane - first == sub, 1.0, 0.0), rows[p])
        near = range(p + 1, min(count, p + (4 if p % 2 == 0 else 3)))
        below = {g: [lane_to_all(rows[g], first + j) for j in range(sublanes)] for g in near}
        more = p + 1 < count
        if more:
            after = [lane_to_all(rows[p + 1], first + sublanes + m) for m in range(sublanes)]
            entry_next = list(below[p + 1])
        scaled = []
        done = jnp.zeros((sublanes, block), F32)
        raw = diag[0]
        for j in range(sublanes):
            pivot = row_to_all(raw, j)
            inv = 1.0 / pivot
            ratio = diag[j] * inv
            here = sub == j
            row = row_to_all(work, j)
            done = jnp.where(here, row * lax.rsqrt(pivot), done)
            work = jnp.where(here, row * inv, work - ratio * row)
            if more:
                scaled.append(entry_next[j] * inv)
            for m in range(j + 1, sublanes):
                entry = row_to_all(diag[m], j)
                left = diag[m] - ratio * entry
                if m == j + 1:
                    raw = left
                diag[m] = jnp.where(here, entry * inv, left)
                if more:
                    entry_next[m] = entry_next[m] - scaled[j] * entry
        out.append(jnp.where(lane <= first + sub, done, 0.0))
        if more:
            diag = [
                take_away(after[m], scaled, [row_to_all(entry_next[j], m) for j in range(sublanes)])
                for m in range(sublanes)
            ]
        work_rows = [row_to_all(work, j) for j in range(sublanes)]
        for g in near:
            rows[g] = take_away(jnp.where(inside, 0.0, rows[g]), below[g], work_rows)
        if p % 2 == 0:
            before, inside_before = work, inside
            continue
        far = range(p + 3, count)
        if not far:
            continue
        tie = [lane_to_all(before, first + m) for m in range(sublanes)]
        before = take_away(jnp.where(inside, 0.0, before), tie, work_rows)
        pair = split(jnp.concatenate([before, work], axis=0))
        top, bottom = first - sublanes, block - first - sublanes
        pair = tuple(
            jnp.concatenate(
                [jnp.zeros((h, block), BF16) if v is None else v for h, v in ((top, None), (0, w), (bottom, None)) if h or v is not None],
                axis=0,
            )
            for w in pair
        )
        change = dot3(split(jnp.concatenate([rows[g] for g in far], axis=0)), pair, NN)
        for i, g in enumerate(far):
            kept = jnp.where(inside | inside_before, 0.0, rows[g])
            rows[g] = kept - change[sublanes * i : sublanes * (i + 1)]
    return out


def invert_in_place(a, n, high, low, finish):
    def rest_of(k):
        here = slice(k * block, (k + 1) * block)
        start = (k + 1) * block
        small = (high[here, here], low[here, here])
        if k > 0:
            left = split(dot3(small, split(a[here, 0 : k * block]), NN))
            high[here, 0 : k * block], low[here, 0 : k * block] = left
        if start < n:
            for v in (high, low):
                v[here, start:n] = jnp.zeros((block, n - start), BF16)
        finish(k)
        if start == n:
            return
        rest = slice(start, n)
        column = split(dot3(split(a[rest, here]), small, NT))
        for i0 in range(start, n, 2 * block):
            i1 = min(i0 + 2 * block, n)
            left = tuple(v[i0 - start : i1 - start] for v in column)
            right = tuple(v[0 : i1 - start] for v in column)
            a[i0:i1, start:i1] = a[i0:i1, start:i1] - dot3(left, right, NT)
        a[rest, here] = -dot3(column, small, NN)
        if k > 0:
            done = (high[here, 0 : k * block], low[here, 0 : k * block])
            a[rest, 0 : k * block] = a[rest, 0 : k * block] - dot3(column, done, NN)

    def step(k, carry):
        first = pl.multiple_of(k * block, block)
        here = pl.ds(first, block)
        groups = [
            a[pl.ds(pl.multiple_of(first + sublanes * g, sublanes), sublanes), here] for g in range(block // sublanes)
        ]
        high[here, here], low[here, here] = split(jnp.concatenate(inverse_factor(groups), axis=0))
        for i in range(n // block):
            pl.when(k == i)(functools.partial(rest_of, i))
        return carry

    lax.fori_loop(0, n // block, step, 0)


def panel_kernel(plan, samples_all, places, *refs):
    count = len(plan)
    pieces, (high_ref, low_ref, panel_ref, data, a, high, low, in_sem, out_sem) = refs[:count], refs[count:]
    width, samples = data.shape
    copies = []
    for i, (piece, slots) in enumerate(zip(pieces, plan)):
        tall, depth = piece.shape[1:]
        place = pl.multiple_of(places[i], block)
        for t, slot in enumerate(slots):
            at = pl.multiple_of(places[count + slot] * depth, block)
            copies.append(
                pltpu.make_async_copy(piece.at[t], data.at[pl.ds(place, tall), pl.ds(at, depth)], in_sem)
            )
    for c in copies:
        c.start()
    for c in copies:
        c.wait()
    keep = pltpu.make_async_copy(data, panel_ref, out_sem)
    keep.start()
    step = 2 * block
    for i0 in range(0, width, step):
        i1 = i0 + step
        part = dot1(data[i0:i1, :], data[0:i1, :], NT) / samples_all
        at = lax.broadcasted_iota(jnp.int32, (step, i1), 0) + i0
        across = lax.broadcasted_iota(jnp.int32, (step, i1), 1)
        a[i0:i1, 0:i1] = part + jnp.where(at == across, ridge, 0.0)

    def out_copies(k):
        here = pl.ds(k * block, block)
        return [
            pltpu.make_async_copy(source.at[here, :], target.at[here, :], out_sem)
            for source, target in ((high, high_ref), (low, low_ref))
        ]

    def finish(k):
        for c in out_copies(k):
            c.start()

    invert_in_place(a, width, high, low, finish)
    for k in range(width // block):
        for c in out_copies(k):
            c.wait()
    keep.wait()


def panel_step(pieces, plan, places, width, samples, samples_all):
    return pl.pallas_call(
        functools.partial(panel_kernel, plan, samples_all),
        out_shape=(
            jax.ShapeDtypeStruct((width, width), BF16),
            jax.ShapeDtypeStruct((width, width), BF16),
            jax.ShapeDtypeStruct((width, samples), BF16),
        ),
        in_specs=[pl.BlockSpec(memory_space=pltpu.SMEM)] + [pl.BlockSpec(memory_space=pl.ANY)] * len(pieces),
        out_specs=(pl.BlockSpec(memory_space=pl.ANY),) * 3,
        scratch_shapes=[
            pltpu.VMEM((width, samples), BF16),
            pltpu.VMEM((width, width), F32),
            pltpu.VMEM((width, width), BF16),
            pltpu.VMEM((width, width), BF16),
            pltpu.SemaphoreType.DMA,
            pltpu.SemaphoreType.DMA,
        ],
        compiler_params=pltpu.CompilerParams(vmem_limit_bytes=vmem_bytes),
        cost_estimate=pl.CostEstimate(flops=40 * 10**9, bytes_accessed=20 * 2**20, transcendentals=0),
    )(places, *pieces)


def tile_kernel(samples_all, n_places, n_scores, col_plan, row_plan, facts, panel_ref, high_ref, low_ref, own_ref, *refs):
    score_refs, refs = refs[:n_scores], refs[n_scores:]
    pieces = refs[: len(col_plan)]
    cond_ref, whitened_ref, residual_ref, panel, cols, rows, high, low, change, sems = refs[-10:]
    extra = refs[len(col_plan) : -10]
    width, samples = panel.shape
    local_rows = rows.shape[0]
    row_place_panel = pl.multiple_of(facts[2], block)
    n_facts, slot_at = 5, 5 + n_places
    cols_own, rows_own = facts[0] == 1, facts[1] == 1
    load_panel = pltpu.make_async_copy(panel_ref, panel, sems.at[0])

    def copies(piece, target, first, plan, sem):
        tall, depth = piece.shape[1:]
        found = []
        for t, place, slot in plan:
            at = pl.multiple_of((facts[n_facts + place] if place >= 0 else 0) - first, block)
            across = pl.multiple_of(facts[slot_at + slot] * depth, block)
            found.append(
                pltpu.make_async_copy(piece.at[t], target.at[pl.ds(at, tall), pl.ds(across, depth)], sem)
            )
        return found

    def col_copies():
        return [c for p, plan in zip(pieces, col_plan) for c in copies(p, cols, 0, plan, sems.at[1])]

    def row_copies():
        if extra:
            return copies(extra[0], rows, 0, row_plan[0], sems.at[2])
        return [c for p, plan in zip(pieces, row_plan) for c in copies(p, rows, facts[2], plan, sems.at[2])]

    cols_from_panel = pltpu.make_async_copy(panel_ref, cols, sems.at[1])
    rows_from_panel = pltpu.make_async_copy(
        panel_ref.at[pl.ds(row_place_panel, local_rows), :], rows, sems.at[2]
    )

    @pl.when(rows_own)
    def _():
        rows_from_panel.start()

    @pl.when(jnp.logical_not(rows_own))
    def _():
        for c in row_copies():
            c.start()

    load_panel.start()
    loads = [
        pltpu.make_async_copy(source, target, sems.at[3]) for source, target in ((high_ref, high), (low_ref, low))
    ]
    for c in loads:
        c.start()
    @pl.when(cols_own)
    def _():
        cols_from_panel.start()

    @pl.when(jnp.logical_not(cols_own))
    def _():
        for c in col_copies():
            c.start()

    inverse = (high, low)
    step = 2 * block
    load_panel.wait()

    @pl.when(rows_own)
    def _():
        rows_from_panel.wait()

    @pl.when(jnp.logical_not(rows_own))
    def _():
        for c in row_copies():
            c.wait()

    slabs = []
    for r0 in range(0, local_rows, step):
        slab = dot1(rows[r0 : r0 + step, :], panel[...], NT) / samples_all
        at = lax.broadcasted_iota(jnp.int32, slab.shape, 0) + (row_place_panel + r0)
        across = lax.broadcasted_iota(jnp.int32, slab.shape, 1)
        slabs.append(split(slab + jnp.where((at == across) & rows_own, ridge, 0.0)))
    for c in loads:
        c.wait()
    scores = score_refs[0][...]
    if n_scores == 2:
        beside = score_refs[1][...]
        first = row_place_panel == 0
        scores = jnp.concatenate([jnp.where(first, scores, beside), jnp.where(first, beside, scores)], axis=1)
    scores = split(scores)
    for j0 in range(0, width, step):
        j1 = j0 + step
        whitened_ref[:, j0:j1] = dot3(
            tuple(v[:, :j1] for v in scores), tuple(v[j0:j1, :j1] for v in inverse), NT
        )
    whitened = split(whitened_ref[...])
    for slab, r0 in zip(slabs, range(0, local_rows, step)):
        r1 = r0 + step
        factor = jnp.concatenate(
            [
                dot3(
                    tuple(v[:, : j0 + step] for v in slab),
                    tuple(v[j0 : j0 + step, : j0 + step] for v in inverse),
                    NT,
                )
                for j0 in range(0, width, step)
            ],
            axis=1,
        )
        factor = split(factor)
        residual_ref[:, r0:r1] = own_ref[:, r0:r1] - dot3(whitened, factor, NT)
        weights = jnp.concatenate(
            [
                dot3(
                    tuple(v[:, j0:] for v in factor),
                    tuple(v[j0:, j0 : j0 + step] for v in inverse),
                    NN,
                )
                for j0 in range(0, width, step)
            ],
            axis=1,
        )
        parts = split(weights)
        both = jnp.concatenate([panel[...], panel[...]], axis=0)
        explained = dot1(jnp.concatenate(parts, axis=1), both, NN)
        change[r0:r1, :] = (rows[r0:r1, :].astype(F32) - explained).astype(BF16)
        cond_ref[r0:r1, :] = weights

    @pl.when(cols_own)
    def _():
        cols_from_panel.wait()

    @pl.when(jnp.logical_not(cols_own))
    def _():
        for c in col_copies():
            c.wait()

    row_first, col_first = facts[3], facts[4]
    for r0 in range(0, local_rows, step):
        r1 = r0 + step
        part = dot1(change[r0:r1, :], cols[...], NT) / samples_all
        at = lax.broadcasted_iota(jnp.int32, part.shape, 0) + (row_first + r0)
        across = lax.broadcasted_iota(jnp.int32, part.shape, 1) + col_first
        unit = jnp.where(at == across, 1.0, 0.0)
        cond_ref[r0:r1, :] = part + ridge * (unit - jnp.where(cols_own, cond_ref[r0:r1, :], 0.0))


def tile_step(facts, panel, high, low, scores, own, pieces, n_places, col_plan, row_plan, extra, samples_all):
    width, samples = panel.shape
    traits, local_rows = own.shape
    smem = pl.BlockSpec(memory_space=pltpu.SMEM)
    vmem = pl.BlockSpec(memory_space=pltpu.VMEM)
    anywhere = pl.BlockSpec(memory_space=pl.ANY)
    return pl.pallas_call(
        functools.partial(tile_kernel, samples_all, n_places, len(scores), col_plan, row_plan),
        out_shape=(
            jax.ShapeDtypeStruct((local_rows, width), F32),
            jax.ShapeDtypeStruct((traits, width), F32),
            jax.ShapeDtypeStruct((traits, local_rows), F32),
        ),
        in_specs=[smem] + [anywhere] * 3 + [vmem] * (1 + len(scores)) + [anywhere] * (len(pieces) + len(extra)),
        out_specs=(vmem, vmem, vmem),
        scratch_shapes=[
            pltpu.VMEM((width, samples), BF16),
            pltpu.VMEM((width, samples), BF16),
            pltpu.VMEM((local_rows, samples), BF16),
            pltpu.VMEM((width, width), BF16),
            pltpu.VMEM((width, width), BF16),
            pltpu.VMEM((local_rows, samples), BF16),
            pltpu.SemaphoreType.DMA((4,)),
        ],
        compiler_params=pltpu.CompilerParams(vmem_limit_bytes=vmem_bytes),
        cost_estimate=pl.CostEstimate(flops=20 * 10**9, bytes_accessed=20 * 2**20, transcendentals=0),
    )(facts, panel, high, low, own, *scores, *pieces, *extra)


swap = [(0, 1), (1, 0)]


def on_device(genotypes, frequencies, trait_scores, typed_mask, panel_index):
    n_samp, n_pan, n_mem, n_col = (lax.axis_size(a) for a in ("samp", "pan", "mem", "col"))
    samp, pan, mem, col = (lax.axis_index(a) for a in ("samp", "pan", "mem", "col"))
    depth, local_rows = genotypes.shape
    width = local_rows * n_mem
    samples_all = depth * n_samp
    q = panel_index[0] % n_col
    spread = jnp.sqrt(2.0 * frequencies * (1.0 - frequencies))
    standard = ((genotypes.astype(F32) - 2.0 * frequencies) / spread).astype(BF16).T
    masked = trait_scores * typed_mask.astype(F32)
    own_panel = pan == q
    rest = []
    if n_pan == 2 and n_mem == 2 and n_col == 2 and n_samp == 4:
        quarter = local_rows // 4

        def part(i, j):
            return lax.dynamic_slice_in_dim(standard, (2 * i + j) * quarter, quarter, 0)

        mine, other = part(pan, col), lax.ppermute(part(1 - pan, col), "pan", swap)
        piece = jnp.where(own_panel, mine, other)
        rest_piece = jnp.where(own_panel, other, mine)

        def along_samp(v):
            steps = [[(s, (s + d) % n_samp) for s in range(n_samp)] for d in (1, 2, 3)]
            return [lax.ppermute(v, "samp", pairs) for pairs in steps]

        own = jnp.stack([piece] + along_samp(piece))
        panel_masked = jnp.where(own_panel, masked, lax.ppermute(masked, "pan", swap))
        own, panel_masked = lax.optimization_barrier((own, panel_masked))
        beside = lax.ppermute(panel_masked, "mem", swap)
        by_mem, by_pan = lax.ppermute(own, "mem", swap), lax.ppermute(own, "pan", swap)
        far_a = lax.ppermute(by_pan[:2], "mem", swap)
        far_b = lax.ppermute(by_mem[2:], "pan", swap)
        near = [own, by_mem, by_pan, far_a, far_b]
        twin = [lax.ppermute(v, "col", swap) for v in near]
        pieces = near + twin
        plan = [(0, 1, 2, 3)] * 3 + [(0, 1), (2, 3)]
        plan = plan + plan

        def place(m, a, c):
            return (m * 4 + a * 2 + c) * quarter

        slots = [(samp - d) % n_samp for d in range(n_samp)]
        corners = ((mem, pan), (1 - mem, pan), (mem, 1 - pan), (1 - mem, 1 - pan))
        places = [place(m, a, c) for c in (col, 1 - col) for m, a in corners + corners[3:]] + slots
        rest_piece, _ = lax.optimization_barrier((rest_piece, own))
        rest_own = jnp.stack([rest_piece] + along_samp(rest_piece))
        rest_own, _, _, beside = lax.optimization_barrier((rest_own, by_mem, by_pan, beside))
        cross = [(2 * i + j, 2 * (1 - i) + 1 - j) for i in range(2) for j in range(2)]
        rest = [
            rest_own,
            lax.ppermute(rest_own, "mem", swap),
            lax.ppermute(rest_own, "pan", swap),
            lax.ppermute(rest_own, ("pan", "mem"), cross),
        ]
        rest_twin = lax.ppermute(rest_own, "col", swap)
        col_plan = [[(d, t + 4 * c, d) for d in range(4)] for c in range(2) for t in range(4)]
        row_plan = [plan if i % 2 == 0 else [] for i, plan in enumerate(col_plan)]
        extra, n_places = [], 8
        col_places = [place(m, a, c) for c in (col, 1 - col) for m, a in corners] + slots
        panel_scores = [panel_masked, beside]
    else:
        chosen = lax.psum(jnp.where(own_panel, standard, jnp.zeros_like(standard)), "pan")
        gathered = lax.all_gather(chosen, ("samp", "mem")).reshape(n_samp, width, depth)
        pieces, plan = [gathered], [tuple(range(n_samp))]
        places = [0, *range(n_samp)]
        cross = [(i * n_col + j, j * n_col + i) for i in range(n_pan) for j in range(n_col)]
        col_block = lax.ppermute(standard, ("pan", "col"), cross)
        col_pieces = [lax.all_gather(col_block, ("samp", "mem")).reshape(n_samp, width, depth)]
        extra, n_places = [lax.all_gather(standard, "samp")], 1
        col_plan = [[(s, 0, s) for s in range(n_samp)]]
        row_plan = [[(s, -1, s) for s in range(n_samp)]]
        col_places = places
        panel_masked = lax.psum(jnp.where(own_panel, masked, jnp.zeros_like(masked)), "pan")
        panel_scores = [lax.all_gather(panel_masked, "mem", axis=1, tiled=True)]
    places = jnp.stack([jnp.asarray(v).astype(jnp.int32) for v in places])
    facts = [col == q, own_panel, mem * local_rows, (pan * n_mem + mem) * local_rows, col * width, *col_places]
    facts = jnp.stack([jnp.asarray(f).astype(jnp.int32) for f in facts])
    facts, places = lax.optimization_barrier((facts, places))
    high, low, panel_data = panel_step(pieces, plan, places, width, samples_all, samples_all)
    if rest:
        held = lax.optimization_barrier((high, *rest[1:]))
        high = held[0]
        rest = [rest[0], *held[1:]]
        col_pieces = rest + [rest_twin] + [lax.ppermute(v, "col", swap) for v in rest[1:]]
    return tile_step(
        facts, panel_data, high, low, panel_scores, masked, col_pieces, n_places, col_plan, row_plan, extra, samples_all
    )


def solution(mesh):
    n_samp, n_row, n_col = (mesh.shape[a] for a in ("samp", "row", "col"))
    inner = Mesh(mesh.devices.reshape(n_samp, n_col, n_row // n_col, n_col), ("samp", "pan", "mem", "col"))
    row = ("pan", "mem")
    return jax.shard_map(
        on_device,
        mesh=inner,
        in_specs=(P("samp", row), P(row), P(None, row), P(row), P()),
        out_specs=(P(row, "col"), P(), P(None, row)),
        check_vma=False,
    )
```

profile of v0, /device:TPU:0, one launch (start us, length us, event | category | flops | bytes accessed | tf_op | source)
XLA Modules:
  0.0 113.1 jit_solution(5201232628105450991)
XLA Ops:
  0.7 0.7 broadcast_multiply_fusion.1
  1.4 1.6 %copy.8 = s32[512,512]{0,1:T(8,128)S(1)} copy(s32[512,512]{1,0:T(8,128)} %param.5) | data formatting | bytes 2097152 | tf_op args[0]
  3.0 0.2 divide_convert_fusion
  3.2 3.0 %collective-permute-start = (bf16[128,512]{1,0:T(8,128)(2,1)S(1)}, bf16[128,512]{1,0:T(8,128)(2,1)S(1)}, u32[]{:S(2)}, u32[]{:S(2)}) collective-permute-start(bf16[128,512]{1,0:T(8,128)(2,1)S(1)} %dynamic-slice_bitcast_fusion), channel_id=1, source_target_pairs={{0,4},{4,0},{1,5},{5,1},{2,6},{6,2},{3,7},{7,3},{8,12},{12,8},{9,1... | collective-permute-start | bytes 393224 | tf_op jit(solution)/shard_map/ppermute | solution.py:423
  6.3 0.1 collective-permute-start.4
  7.1 3.5 %collective-permute-done = bf16[128,512]{1,0:T(8,128)(2,1)S(1)} collective-permute-done((bf16[128,512]{1,0:T(8,128)(2,1)S(1)}, bf16[128,512]{1,0:T(8,128)(2,1)S(1)}, u32[]{:S(2)}, u32[]{:S(2)}) %collective-permute-start) | collective-permute-done | bytes 131104 | tf_op jit(solution)/shard_map/ppermute | solution.py:423
  10.6 0.1 bitcast_select_fusion
  10.6 2.2 %collective-permute-start.1 = (bf16[128,512]{1,0:T(8,128)(2,1)S(1)}, bf16[128,512]{1,0:T(8,128)(2,1)S(1)}, u32[]{:S(2)}, u32[]{:S(2)}) collective-permute-start(bf16[128,512]{1,0:T(8,128)(2,1)S(1)} %get-tuple-element.32), channel_id=1, source_target_pairs={{0,8},{8,16},{16,24},{24,0},{1,9},{9,17},{17,25},{25,1},{2,10},{10... | collective-permute-start | bytes 393224 | tf_op jit(solution)/shard_map/ppermute | solution.py:429
  12.8 2.6 %collective-permute-start.2 = (bf16[128,512]{1,0:T(8,128)(2,1)S(1)}, bf16[128,512]{1,0:T(8,128)(2,1)S(1)}, u32[]{:S(2)}, u32[]{:S(2)}) collective-permute-start(bf16[128,512]{1,0:T(8,128)(2,1)S(1)} %get-tuple-element.32), channel_id=1, source_target_pairs={{0,16},{8,24},{16,0},{24,8},{1,17},{9,25},{17,1},{25,9},{2,18},{10... | collective-permute-start | bytes 393224 | tf_op jit(solution)/shard_map/ppermute | solution.py:429
  15.4 1.3 %collective-permute-start.3 = (bf16[128,512]{1,0:T(8,128)(2,1)S(1)}, bf16[128,512]{1,0:T(8,128)(2,1)S(1)}, u32[]{:S(2)}, u32[]{:S(2)}) collective-permute-start(bf16[128,512]{1,0:T(8,128)(2,1)S(1)} %get-tuple-element.32), channel_id=1, source_target_pairs={{0,24},{8,0},{16,8},{24,16},{1,25},{9,1},{17,9},{25,17},{2,26},{10... | collective-permute-start | bytes 393224 | tf_op jit(solution)/shard_map/ppermute | solution.py:429
  16.7 0.0 collective-permute-done.4
  16.8 2.5 %collective-permute-done.1 = bf16[128,512]{1,0:T(8,128)(2,1)S(1)} collective-permute-done((bf16[128,512]{1,0:T(8,128)(2,1)S(1)}, bf16[128,512]{1,0:T(8,128)(2,1)S(1)}, u32[]{:S(2)}, u32[]{:S(2)}) %collective-permute-start.1) | collective-permute-done | bytes 131104 | tf_op jit(solution)/shard_map/ppermute | solution.py:429
  19.3 3.3 %collective-permute-done.2 = bf16[128,512]{1,0:T(8,128)(2,1)S(1)} collective-permute-done((bf16[128,512]{1,0:T(8,128)(2,1)S(1)}, bf16[128,512]{1,0:T(8,128)(2,1)S(1)}, u32[]{:S(2)}, u32[]{:S(2)}) %collective-permute-start.2) | collective-permute-done | bytes 131104 | tf_op jit(solution)/shard_map/ppermute | solution.py:429
  22.6 0.0 collective-permute-done.3
  22.6 0.1 pad_maximum_fusion.refs_0_
  22.6 0.0 copy-start
  22.7 1.7 %collective-permute-start.6 = (bf16[4,128,512]{2,1,0:T(8,128)(2,1)S(1)}, bf16[4,128,512]{2,1,0:T(8,128)(2,1)S(1)}, u32[]{:S(2)}, u32[]{:S(2)}) collective-permute-start(bf16[4,128,512]{2,1,0:T(8,128)(2,1)S(1)} %pad_maximum_fusion.refs_0_), channel_id=1, source_target_pairs={{0,4},{4,0},{1,5},{5,1},{2,6},{6,2},{3,7},{7,3},{8,12},{12,8},{9,1... | collective-permute-start | bytes 1572872 | tf_op jit(solution)/shard_map/ppermute | solution.py:435
  24.3 1.5 %collective-permute-start.5 = (bf16[4,128,512]{2,1,0:T(8,128)(2,1)S(1)}, bf16[4,128,512]{2,1,0:T(8,128)(2,1)S(1)}, u32[]{:S(2)}, u32[]{:S(2)}) collective-permute-start(bf16[4,128,512]{2,1,0:T(8,128)(2,1)S(1)} %pad_maximum_fusion.refs_0_), channel_id=1, source_target_pairs={{0,2},{2,0},{1,3},{3,1},{4,6},{6,4},{5,7},{7,5},{8,10},{10,8},{9,1... | collective-permute-start | bytes 1572872 | tf_op jit(solution)/shard_map/ppermute | solution.py:435
  25.8 2.7 %collective-permute-start.14 = (bf16[128,512]{1,0:T(8,128)(2,1)S(1)}, bf16[128,512]{1,0:T(8,128)(2,1)S(1)}, u32[]{:S(2)}, u32[]{:S(2)}) collective-permute-start(bf16[128,512]{1,0:T(8,128)(2,1)S(1)} %get-tuple-element.22), channel_id=1, source_target_pairs={{0,8},{8,16},{16,24},{24,0},{1,9},{9,17},{17,25},{25,1},{2,10},{10... | collective-permute-start | bytes 393224 | tf_op jit(solution)/shard_map/ppermute | solution.py:429
  28.5 1.6 %collective-permute-start.15 = (bf16[128,512]{1,0:T(8,128)(2,1)S(1)}, bf16[128,512]{1,0:T(8,128)(2,1)S(1)}, u32[]{:S(2)}, u32[]{:S(2)}) collective-permute-start(bf16[128,512]{1,0:T(8,128)(2,1)S(1)} %get-tuple-element.22), channel_id=1, source_target_pairs={{0,16},{8,24},{16,0},{24,8},{1,17},{9,25},{17,1},{25,9},{2,18},{10... | collective-permute-start | bytes 393224 | tf_op jit(solution)/shard_map/ppermute | solution.py:429
  30.1 0.8 collective-permute-start.16
  30.9 4.7 %collective-permute-done.6.refs_2_ = bf16[4,128,512]{2,1,0:T(8,128)(2,1)S(1)} collective-permute-done((bf16[4,128,512]{2,1,0:T(8,128)(2,1)S(1)}, bf16[4,128,512]{2,1,0:T(8,128)(2,1)S(1)}, u32[]{:S(2)}, u32[]{:S(2)}) %collective-permute-start.6) | collective-permute-done | bytes 524320 | tf_op jit(solution)/shard_map/ppermute | solution.py:435
  35.5 1.3 %collective-permute-start.17 = (f32[64,512]{1,0:T(8,128)S(1)}, f32[64,512]{1,0:T(8,128)S(1)}, u32[]{:S(2)}, u32[]{:S(2)}) collective-permute-start(f32[64,512]{1,0:T(8,128)S(1)} %broadcast_select_fusion.refs_0_), channel_id=1, source_target_pairs={{0,2},{2,0},{1,3},{3,1},{4,6},{6,4},{5,7},{7,5},{8,10},{10,8},{9,1... | collective-permute-start | bytes 393224 | tf_op jit(solution)/shard_map/ppermute | solution.py:434
  36.9 0.1 collective-permute-done.5.refs_1_
  36.9 0.0 collective-permute-start.9
  37.0 0.0 collective-permute-done.14
  37.0 2.0 %collective-permute-start.7 = (bf16[2,128,512]{2,1,0:T(8,128)(2,1)S(1)}, bf16[2,128,512]{2,1,0:T(8,128)(2,1)}, u32[]{:S(2)}, u32[]{:S(2)}) collective-permute-start(bf16[2,128,512]{2,1,0:T(8,128)(2,1)S(1)} %slice.8), channel_id=1, source_target_pairs={{0,2},{2,0},{1,3},{3,1},{4,6},{6,4},{5,7},{7,5},{8,10},{10,8},{9,1... | collective-permute-start | bytes 786440 | tf_op jit(solution)/shard_map/ppermute | solution.py:436
  39.0 0.0 collective-permute-done.15
  39.0 0.1 collective-permute-start.8
  39.1 0.0 collective-permute-done.16
  39.1 0.2 collective-permute-start.10
  39.3 1.3 %collective-permute-done.17.refs_1_ = f32[64,512]{1,0:T(8,128)S(1)} collective-permute-done((f32[64,512]{1,0:T(8,128)S(1)}, f32[64,512]{1,0:T(8,128)S(1)}, u32[]{:S(2)}, u32[]{:S(2)}) %collective-permute-start.17) | collective-permute-done | bytes 131104 | tf_op jit(solution)/shard_map/ppermute | solution.py:434
  40.6 0.0 collective-permute-start.11
  40.6 5.6 %collective-permute-done.7.refs_3_ = bf16[2,128,512]{2,1,0:T(8,128)(2,1)} collective-permute-done((bf16[2,128,512]{2,1,0:T(8,128)(2,1)S(1)}, bf16[2,128,512]{2,1,0:T(8,128)(2,1)}, u32[]{:S(2)}, u32[]{:S(2)}) %collective-permute-start.7) | collective-permute-done | bytes 262176 | tf_op jit(solution)/shard_map/ppermute | solution.py:436
  46.2 0.0 collective-permute-start.12
  46.2 1.3 %collective-permute-done.8.refs_4_ = bf16[2,128,512]{2,1,0:T(8,128)(2,1)} collective-permute-done((bf16[2,128,512]{2,1,0:T(8,128)(2,1)S(1)}, bf16[2,128,512]{2,1,0:T(8,128)(2,1)}, u32[]{:S(2)}, u32[]{:S(2)}) %collective-permute-start.8) | collective-permute-done | bytes 262176 | tf_op jit(solution)/shard_map/ppermute | solution.py:437
  47.5 0.0 collective-permute-start.13
  47.5 0.6 stack.127.places
  48.1 0.7 stack.126.facts
  48.8 0.1 pad_maximum_fusion.1.refs_2_
  48.9 0.0 collective-permute-done.9.refs_5_
  48.9 0.9 collective-permute-start.18
  49.8 0.0 collective-permute-done.12.refs_8_
  49.8 1.2 %collective-permute-start.19 = (bf16[4,128,512]{2,1,0:T(8,128)(2,1)S(1)}, bf16[4,128,512]{2,1,0:T(8,128)(2,1)S(1)}, u32[]{:S(2)}, u32[]{:S(2)}) collective-permute-start(bf16[4,128,512]{2,1,0:T(8,128)(2,1)S(1)} %pad_maximum_fusion.1.refs_2_), channel_id=1, source_target_pairs={{0,4},{4,0},{1,5},{5,1},{2,6},{6,2},{3,7},{7,3},{8,12},{12,8},{9,1... | collective-permute-start | bytes 1572872 | tf_op jit(solution)/shard_map/ppermute | solution.py:457
  51.0 0.0 collective-permute-done.13.refs_9_
  51.0 1.5 %collective-permute-start.20 = (bf16[4,128,512]{2,1,0:T(8,128)(2,1)S(1)}, bf16[4,128,512]{2,1,0:T(8,128)(2,1)S(1)}, u32[]{:S(2)}, u32[]{:S(2)}) collective-permute-start(bf16[4,128,512]{2,1,0:T(8,128)(2,1)S(1)} %pad_maximum_fusion.1.refs_2_), channel_id=1, source_target_pairs={{0,6},{2,4},{4,2},{6,0},{1,7},{3,5},{5,3},{7,1},{8,14},{10,12},{12... | collective-permute-start | bytes 1572872 | tf_op jit(solution)/shard_map/ppermute | solution.py:458
  52.5 0.0 collective-permute-done.10.refs_6_
  52.5 0.0 collective-permute-start.21
  52.5 0.0 collective-permute-done.11.refs_7_
  52.5 0.8 copy-done.9
  53.3 32.6 %shard_map.76 = (bf16[1024,1024]{1,0:T(8,128)(2,1)}, bf16[1024,1024]{1,0:T(8,128)(2,1)}, bf16[1024,2048]{1,0:T(8,128)(2,1)}) custom-call(s32[14]{0:T(128)} %stack.127.places, bf16[4,128,512]{2,1,0:T(8,128)(2,1)} %copy-done, bf16[4,128,512]{2,1,0:T(8,128)(2,1)} %copy-done.4, bf16[4,128,512]{2,1,0:T(8,128)(2,1)} %copy-done.3, ...), custom_call_target="tpu_custom_call" | custom-call | flops 40000000000 | bytes 20971520 | tf_op jit(solution)/shard_map/pallas_call | solution.py:207
  85.9 0.0 collective-permute-done.18.refs_3_
  86.0 0.0 collective-permute-done.19.refs_4_
  86.0 0.0 collective-permute-done.20.refs_5_
  86.0 0.1 collective-permute-start.22
  86.1 0.5 collective-permute-start.23
  86.6 0.1 collective-permute-start.24
  86.7 0.0 collective-permute-done.21.refs_6_
  86.7 1.3 %collective-permute-done.22.refs_7_ = bf16[4,128,512]{2,1,0:T(8,128)(2,1)S(1)} collective-permute-done((bf16[4,128,512]{2,1,0:T(8,128)(2,1)S(1)}, bf16[4,128,512]{2,1,0:T(8,128)(2,1)S(1)}, u32[]{:S(2)}, u32[]{:S(2)}) %collective-permute-start.22) | collective-permute-done | bytes 524320 | tf_op jit(solution)/shard_map/ppermute | solution.py:489
  88.0 0.7 collective-permute-done.23.refs_8_
  88.7 0.7 collective-permute-done.24.refs_9_
  89.5 0.0 copy-done.15
  89.5 0.8 copy-done.16
  90.3 22.6 %shard_map.77 = (f32[512,1024]{1,0:T(8,128)}, f32[64,1024]{1,0:T(8,128)}, f32[64,512]{1,0:T(8,128)}) custom-call(s32[17]{0:T(128)} %stack.126.facts, bf16[1024,2048]{1,0:T(8,128)(2,1)} %get-tuple-element.20.panel_ref, bf16[1024,1024]{1,0:T(8,128)(2,1)} %get-tuple-element.25.high_ref, bf16[1024,1024]{1,0:T(8,128)(2,1)} %get-tuple-element.26.low_ref, ...), custom_call_target="tpu_custom_call" | custom-call | flops 20000000000 | bytes 20971520 | tf_op jit(solution)/shard_map/pallas_call | solution.py:379
  (38 shorter events, 0.2 us)
Async XLA Ops:
  0.6 5.6 %copy-start.7 = (s32[512]{0:T(512)S(1)}, s32[512]{0:T(512)}, u32[]{:S(2)}) copy-start(s32[512]{0:T(512)} %param.8) | copy-start | bytes 6148
  0.6 5.6 %copy-start.2 = (f32[64,512]{1,0:T(8,128)S(1)}, f32[64,512]{1,0:T(8,128)}, u32[]{:S(2)}) copy-start(f32[64,512]{1,0:T(8,128)} %param.7) | copy-start | bytes 393220
  3.2 7.4 %collective-permute-start = (bf16[128,512]{1,0:T(8,128)(2,1)S(1)}, bf16[128,512]{1,0:T(8,128)(2,1)S(1)}, u32[]{:S(2)}, u32[]{:S(2)}) collective-permute-start(bf16[128,512]{1,0:T(8,128)(2,1)S(1)} %dynamic-slice_bitcast_fusion), channel_id=1, source_target_pairs={{0,4},{4,0},{1,5},{5,1},{2,6},{6,2},{3,7},{7,3},{8,12},{12,8},{9,1... | collective-permute-start | bytes 393224 | tf_op jit(solution)/shard_map/ppermute | solution.py:423
  6.3 42.6 %copy-start.5 = (f32[64,512]{1,0:T(8,128)}, f32[64,512]{1,0:T(8,128)S(1)}, u32[]{:S(2)}) copy-start(f32[64,512]{1,0:T(8,128)S(1)} %broadcast_multiply_fusion.own_ref) | copy-start | bytes 393220
  6.3 10.5 %collective-permute-start.4 = (f32[64,512]{1,0:T(8,128)S(1)}, f32[64,512]{1,0:T(8,128)S(1)}, u32[]{:S(2)}, u32[]{:S(2)}) collective-permute-start(f32[64,512]{1,0:T(8,128)S(1)} %broadcast_multiply_fusion.own_ref), channel_id=1, source_target_pairs={{0,4},{4,0},{1,5},{5,1},{2,6},{6,2},{3,7},{7,3},{8,12},{12,8},{9,1... | collective-permute-start | bytes 393224 | tf_op jit(solution)/shard_map/ppermute | solution.py:432
  10.6 8.6 %collective-permute-start.1 = (bf16[128,512]{1,0:T(8,128)(2,1)S(1)}, bf16[128,512]{1,0:T(8,128)(2,1)S(1)}, u32[]{:S(2)}, u32[]{:S(2)}) collective-permute-start(bf16[128,512]{1,0:T(8,128)(2,1)S(1)} %get-tuple-element.32), channel_id=1, source_target_pairs={{0,8},{8,16},{16,24},{24,0},{1,9},{9,17},{17,25},{25,1},{2,10},{10... | collective-permute-start | bytes 393224 | tf_op jit(solution)/shard_map/ppermute | solution.py:429
  12.8 9.8 %collective-permute-start.2 = (bf16[128,512]{1,0:T(8,128)(2,1)S(1)}, bf16[128,512]{1,0:T(8,128)(2,1)S(1)}, u32[]{:S(2)}, u32[]{:S(2)}) collective-permute-start(bf16[128,512]{1,0:T(8,128)(2,1)S(1)} %get-tuple-element.32), channel_id=1, source_target_pairs={{0,16},{8,24},{16,0},{24,8},{1,17},{9,25},{17,1},{25,9},{2,18},{10... | collective-permute-start | bytes 393224 | tf_op jit(solution)/shard_map/ppermute | solution.py:429
  15.4 7.2 %collective-permute-start.3 = (bf16[128,512]{1,0:T(8,128)(2,1)S(1)}, bf16[128,512]{1,0:T(8,128)(2,1)S(1)}, u32[]{:S(2)}, u32[]{:S(2)}) collective-permute-start(bf16[128,512]{1,0:T(8,128)(2,1)S(1)} %get-tuple-element.32), channel_id=1, source_target_pairs={{0,24},{8,0},{16,8},{24,16},{1,25},{9,1},{17,9},{25,17},{2,26},{10... | collective-permute-start | bytes 393224 | tf_op jit(solution)/shard_map/ppermute | solution.py:429
  16.8 69.1 %copy-start.6 = (f32[64,512]{1,0:T(8,128)}, f32[64,512]{1,0:T(8,128)S(1)}, u32[]{:S(2)}) copy-start(f32[64,512]{1,0:T(8,128)S(1)} %broadcast_select_fusion.refs_0_) | copy-start | bytes 393220
  22.6 29.9 %copy-start = (bf16[4,128,512]{2,1,0:T(8,128)(2,1)}, bf16[4,128,512]{2,1,0:T(8,128)(2,1)S(1)}, u32[]{:S(2)}) copy-start(bf16[4,128,512]{2,1,0:T(8,128)(2,1)S(1)} %pad_maximum_fusion.refs_0_) | copy-start | bytes 1572868
  22.7 12.9 %collective-permute-start.6 = (bf16[4,128,512]{2,1,0:T(8,128)(2,1)S(1)}, bf16[4,128,512]{2,1,0:T(8,128)(2,1)S(1)}, u32[]{:S(2)}, u32[]{:S(2)}) collective-permute-start(bf16[4,128,512]{2,1,0:T(8,128)(2,1)S(1)} %pad_maximum_fusion.refs_0_), channel_id=1, source_target_pairs={{0,4},{4,0},{1,5},{5,1},{2,6},{6,2},{3,7},{7,3},{8,12},{12,8},{9,1... | collective-permute-start | bytes 1572872 | tf_op jit(solution)/shard_map/ppermute | solution.py:435
  24.3 12.6 %collective-permute-start.5 = (bf16[4,128,512]{2,1,0:T(8,128)(2,1)S(1)}, bf16[4,128,512]{2,1,0:T(8,128)(2,1)S(1)}, u32[]{:S(2)}, u32[]{:S(2)}) collective-permute-start(bf16[4,128,512]{2,1,0:T(8,128)(2,1)S(1)} %pad_maximum_fusion.refs_0_), channel_id=1, source_target_pairs={{0,2},{2,0},{1,3},{3,1},{4,6},{6,4},{5,7},{7,5},{8,10},{10,8},{9,1... | collective-permute-start | bytes 1572872 | tf_op jit(solution)/shard_map/ppermute | solution.py:435
  25.8 11.1 %collective-permute-start.14 = (bf16[128,512]{1,0:T(8,128)(2,1)S(1)}, bf16[128,512]{1,0:T(8,128)(2,1)S(1)}, u32[]{:S(2)}, u32[]{:S(2)}) collective-permute-start(bf16[128,512]{1,0:T(8,128)(2,1)S(1)} %get-tuple-element.22), channel_id=1, source_target_pairs={{0,8},{8,16},{16,24},{24,0},{1,9},{9,17},{17,25},{25,1},{2,10},{10... | collective-permute-start | bytes 393224 | tf_op jit(solution)/shard_map/ppermute | solution.py:429
  28.5 10.5 %collective-permute-start.15 = (bf16[128,512]{1,0:T(8,128)(2,1)S(1)}, bf16[128,512]{1,0:T(8,128)(2,1)S(1)}, u32[]{:S(2)}, u32[]{:S(2)}) collective-permute-start(bf16[128,512]{1,0:T(8,128)(2,1)S(1)} %get-tuple-element.22), channel_id=1, source_target_pairs={{0,16},{8,24},{16,0},{24,8},{1,17},{9,25},{17,1},{25,9},{2,18},{10... | collective-permute-start | bytes 393224 | tf_op jit(solution)/shard_map/ppermute | solution.py:429
  30.1 9.0 %collective-permute-start.16 = (bf16[128,512]{1,0:T(8,128)(2,1)S(1)}, bf16[128,512]{1,0:T(8,128)(2,1)S(1)}, u32[]{:S(2)}, u32[]{:S(2)}) collective-permute-start(bf16[128,512]{1,0:T(8,128)(2,1)S(1)} %get-tuple-element.22), channel_id=1, source_target_pairs={{0,24},{8,0},{16,8},{24,16},{1,25},{9,1},{17,9},{25,17},{2,26},{10... | collective-permute-start | bytes 393224 | tf_op jit(solution)/shard_map/ppermute | solution.py:429
  35.5 17.0 %copy-start.3 = (bf16[4,128,512]{2,1,0:T(8,128)(2,1)}, bf16[4,128,512]{2,1,0:T(8,128)(2,1)S(1)}, u32[]{:S(2)}) copy-start(bf16[4,128,512]{2,1,0:T(8,128)(2,1)S(1)} %collective-permute-done.6.refs_2_) | copy-start | bytes 1572868
  35.5 5.1 %collective-permute-start.17 = (f32[64,512]{1,0:T(8,128)S(1)}, f32[64,512]{1,0:T(8,128)S(1)}, u32[]{:S(2)}, u32[]{:S(2)}) collective-permute-start(f32[64,512]{1,0:T(8,128)S(1)} %broadcast_select_fusion.refs_0_), channel_id=1, source_target_pairs={{0,2},{2,0},{1,3},{3,1},{4,6},{6,4},{5,7},{7,5},{8,10},{10,8},{9,1... | collective-permute-start | bytes 393224 | tf_op jit(solution)/shard_map/ppermute | solution.py:434
  36.9 15.6 %copy-start.4 = (bf16[4,128,512]{2,1,0:T(8,128)(2,1)}, bf16[4,128,512]{2,1,0:T(8,128)(2,1)S(1)}, u32[]{:S(2)}) copy-start(bf16[4,128,512]{2,1,0:T(8,128)(2,1)S(1)} %collective-permute-done.5.refs_1_) | copy-start | bytes 1572868
  36.9 12.0 %collective-permute-start.9 = (bf16[4,128,512]{2,1,0:T(8,128)(2,1)S(1)}, bf16[4,128,512]{2,1,0:T(8,128)(2,1)S(1)}, u32[]{:S(2)}, u32[]{:S(2)}) collective-permute-start(bf16[4,128,512]{2,1,0:T(8,128)(2,1)S(1)} %pad_maximum_fusion.refs_0_), channel_id=1, source_target_pairs={{0,1},{1,0},{2,3},{3,2},{4,5},{5,4},{6,7},{7,6},{8,9},{9,8},{10,11... | collective-permute-start | bytes 1572872 | tf_op jit(solution)/shard_map/ppermute | solution.py:439
  37.0 9.2 %collective-permute-start.7 = (bf16[2,128,512]{2,1,0:T(8,128)(2,1)S(1)}, bf16[2,128,512]{2,1,0:T(8,128)(2,1)}, u32[]{:S(2)}, u32[]{:S(2)}) collective-permute-start(bf16[2,128,512]{2,1,0:T(8,128)(2,1)S(1)} %slice.8), channel_id=1, source_target_pairs={{0,2},{2,0},{1,3},{3,1},{4,6},{6,4},{5,7},{7,5},{8,10},{10,8},{9,1... | collective-permute-start | bytes 786440 | tf_op jit(solution)/shard_map/ppermute | solution.py:436
  39.0 8.5 %collective-permute-start.8 = (bf16[2,128,512]{2,1,0:T(8,128)(2,1)S(1)}, bf16[2,128,512]{2,1,0:T(8,128)(2,1)}, u32[]{:S(2)}, u32[]{:S(2)}) collective-permute-start(bf16[2,128,512]{2,1,0:T(8,128)(2,1)S(1)} %slice.9), channel_id=1, source_target_pairs={{0,4},{4,0},{1,5},{5,1},{2,6},{6,2},{3,7},{7,3},{8,12},{12,8},{9,1... | collective-permute-start | bytes 786440 | tf_op jit(solution)/shard_map/ppermute | solution.py:437
  39.1 13.4 %collective-permute-start.10 = (bf16[4,128,512]{2,1,0:T(8,128)(2,1)S(1)}, bf16[4,128,512]{2,1,0:T(8,128)(2,1)S(1)}, u32[]{:S(2)}, u32[]{:S(2)}) collective-permute-start(bf16[4,128,512]{2,1,0:T(8,128)(2,1)S(1)} %collective-permute-done.5.refs_1_), channel_id=1, source_target_pairs={{0,1},{1,0},{2,3},{3,2},{4,5},{5,4},{6,7},{7,6},{8,9},{9,8},{10,11... | collective-permute-start | bytes 1572872 | tf_op jit(solution)/shard_map/ppermute | solution.py:439
  40.6 45.3 %copy-start.17 = (f32[64,512]{1,0:T(8,128)}, f32[64,512]{1,0:T(8,128)S(1)}, u32[]{:S(2)}) copy-start(f32[64,512]{1,0:T(8,128)S(1)} %collective-permute-done.17.refs_1_) | copy-start | bytes 393220
  40.6 11.9 %collective-permute-start.11 = (bf16[4,128,512]{2,1,0:T(8,128)(2,1)S(1)}, bf16[4,128,512]{2,1,0:T(8,128)(2,1)}, u32[]{:S(2)}, u32[]{:S(2)}) collective-permute-start(bf16[4,128,512]{2,1,0:T(8,128)(2,1)S(1)} %collective-permute-done.6.refs_2_), channel_id=1, source_target_pairs={{0,1},{1,0},{2,3},{3,2},{4,5},{5,4},{6,7},{7,6},{8,9},{9,8},{10,11... | collective-permute-start | bytes 1572872 | tf_op jit(solution)/shard_map/ppermute | solution.py:439
  46.2 3.6 %collective-permute-start.12 = (bf16[2,128,512]{2,1,0:T(8,128)(2,1)}, bf16[2,128,512]{2,1,0:T(8,128)(2,1)}, u32[]{:S(2)}, u32[]{:S(2)}) collective-permute-start(bf16[2,128,512]{2,1,0:T(8,128)(2,1)} %collective-permute-done.7.refs_3_), channel_id=1, source_target_pairs={{0,1},{1,0},{2,3},{3,2},{4,5},{5,4},{6,7},{7,6},{8,9},{9,8},{10,11... | collective-permute-start | bytes 786440 | tf_op jit(solution)/shard_map/ppermute | solution.py:439
  47.5 3.5 %collective-permute-start.13 = (bf16[2,128,512]{2,1,0:T(8,128)(2,1)}, bf16[2,128,512]{2,1,0:T(8,128)(2,1)}, u32[]{:S(2)}, u32[]{:S(2)}) collective-permute-start(bf16[2,128,512]{2,1,0:T(8,128)(2,1)} %collective-permute-done.8.refs_4_), channel_id=1, source_target_pairs={{0,1},{1,0},{2,3},{3,2},{4,5},{5,4},{6,7},{7,6},{8,9},{9,8},{10,11... | collective-permute-start | bytes 786440 | tf_op jit(solution)/shard_map/ppermute | solution.py:439
  48.9 37.0 %copy-start.1 = (bf16[4,128,512]{2,1,0:T(8,128)(2,1)}, bf16[4,128,512]{2,1,0:T(8,128)(2,1)S(1)}, u32[]{:S(2)}) copy-start(bf16[4,128,512]{2,1,0:T(8,128)(2,1)S(1)} %pad_maximum_fusion.1.refs_2_) | copy-start | bytes 1572868
  48.9 3.6 %copy-start.8 = (bf16[4,128,512]{2,1,0:T(8,128)(2,1)}, bf16[4,128,512]{2,1,0:T(8,128)(2,1)S(1)}, u32[]{:S(2)}) copy-start(bf16[4,128,512]{2,1,0:T(8,128)(2,1)S(1)} %collective-permute-done.9.refs_5_) | copy-start | bytes 1572868
  48.9 37.0 %collective-permute-start.18 = (bf16[4,128,512]{2,1,0:T(8,128)(2,1)S(1)}, bf16[4,128,512]{2,1,0:T(8,128)(2,1)S(1)}, u32[]{:S(2)}, u32[]{:S(2)}) collective-permute-start(bf16[4,128,512]{2,1,0:T(8,128)(2,1)S(1)} %pad_maximum_fusion.1.refs_2_), channel_id=1, source_target_pairs={{0,2},{2,0},{1,3},{3,1},{4,6},{6,4},{5,7},{7,5},{8,10},{10,8},{9,1... | collective-permute-start | bytes 1572872 | tf_op jit(solution)/shard_map/ppermute | solution.py:456
  49.8 36.2 %collective-permute-start.19 = (bf16[4,128,512]{2,1,0:T(8,128)(2,1)S(1)}, bf16[4,128,512]{2,1,0:T(8,128)(2,1)S(1)}, u32[]{:S(2)}, u32[]{:S(2)}) collective-permute-start(bf16[4,128,512]{2,1,0:T(8,128)(2,1)S(1)} %pad_maximum_fusion.1.refs_2_), channel_id=1, source_target_pairs={{0,4},{4,0},{1,5},{5,1},{2,6},{6,2},{3,7},{7,3},{8,12},{12,8},{9,1... | collective-permute-start | bytes 1572872 | tf_op jit(solution)/shard_map/ppermute | solution.py:457
  51.0 35.0 %collective-permute-start.20 = (bf16[4,128,512]{2,1,0:T(8,128)(2,1)S(1)}, bf16[4,128,512]{2,1,0:T(8,128)(2,1)S(1)}, u32[]{:S(2)}, u32[]{:S(2)}) collective-permute-start(bf16[4,128,512]{2,1,0:T(8,128)(2,1)S(1)} %pad_maximum_fusion.1.refs_2_), channel_id=1, source_target_pairs={{0,6},{2,4},{4,2},{6,0},{1,7},{3,5},{5,3},{7,1},{8,14},{10,12},{12... | collective-permute-start | bytes 1572872 | tf_op jit(solution)/shard_map/ppermute | solution.py:458
  52.5 0.8 copy-start.9
  52.5 34.2 %collective-permute-start.21 = (bf16[4,128,512]{2,1,0:T(8,128)(2,1)S(1)}, bf16[4,128,512]{2,1,0:T(8,128)(2,1)S(1)}, u32[]{:S(2)}, u32[]{:S(2)}) collective-permute-start(bf16[4,128,512]{2,1,0:T(8,128)(2,1)S(1)} %pad_maximum_fusion.1.refs_2_), channel_id=1, source_target_pairs={{0,1},{1,0},{2,3},{3,2},{4,5},{5,4},{6,7},{7,6},{8,9},{9,8},{10,11... | collective-permute-start | bytes 1572872 | tf_op jit(solution)/shard_map/ppermute | solution.py:460
  86.0 3.5 %copy-start.10 = (bf16[4,128,512]{2,1,0:T(8,128)(2,1)}, bf16[4,128,512]{2,1,0:T(8,128)(2,1)S(1)}, u32[]{:S(2)}) copy-start(bf16[4,128,512]{2,1,0:T(8,128)(2,1)S(1)} %collective-permute-done.18.refs_3_) | copy-start | bytes 1572868
  86.0 3.5 %copy-start.11 = (bf16[4,128,512]{2,1,0:T(8,128)(2,1)}, bf16[4,128,512]{2,1,0:T(8,128)(2,1)S(1)}, u32[]{:S(2)}) copy-start(bf16[4,128,512]{2,1,0:T(8,128)(2,1)S(1)} %collective-permute-done.19.refs_4_) | copy-start | bytes 1572868
  86.0 3.5 %copy-start.12 = (bf16[4,128,512]{2,1,0:T(8,128)(2,1)}, bf16[4,128,512]{2,1,0:T(8,128)(2,1)S(1)}, u32[]{:S(2)}) copy-start(bf16[4,128,512]{2,1,0:T(8,128)(2,1)S(1)} %collective-permute-done.20.refs_5_) | copy-start | bytes 1572868
  86.0 2.0 %collective-permute-start.22 = (bf16[4,128,512]{2,1,0:T(8,128)(2,1)S(1)}, bf16[4,128,512]{2,1,0:T(8,128)(2,1)S(1)}, u32[]{:S(2)}, u32[]{:S(2)}) collective-permute-start(bf16[4,128,512]{2,1,0:T(8,128)(2,1)S(1)} %collective-permute-done.18.refs_3_), channel_id=1, source_target_pairs={{0,1},{1,0},{2,3},{3,2},{4,5},{5,4},{6,7},{7,6},{8,9},{9,8},{10,11... | collective-permute-start | bytes 1572872 | tf_op jit(solution)/shard_map/ppermute | solution.py:489
  86.1 2.6 %collective-permute-start.23 = (bf16[4,128,512]{2,1,0:T(8,128)(2,1)S(1)}, bf16[4,128,512]{2,1,0:T(8,128)(2,1)S(1)}, u32[]{:S(2)}, u32[]{:S(2)}) collective-permute-start(bf16[4,128,512]{2,1,0:T(8,128)(2,1)S(1)} %collective-permute-done.19.refs_4_), channel_id=1, source_target_pairs={{0,1},{1,0},{2,3},{3,2},{4,5},{5,4},{6,7},{7,6},{8,9},{9,8},{10,11... | collective-permute-start | bytes 1572872 | tf_op jit(solution)/shard_map/ppermute | solution.py:489
  86.6 2.9 %collective-permute-start.24 = (bf16[4,128,512]{2,1,0:T(8,128)(2,1)S(1)}, bf16[4,128,512]{2,1,0:T(8,128)(2,1)S(1)}, u32[]{:S(2)}, u32[]{:S(2)}) collective-permute-start(bf16[4,128,512]{2,1,0:T(8,128)(2,1)S(1)} %collective-permute-done.20.refs_5_), channel_id=1, source_target_pairs={{0,1},{1,0},{2,3},{3,2},{4,5},{5,4},{6,7},{7,6},{8,9},{9,8},{10,11... | collective-permute-start | bytes 1572872 | tf_op jit(solution)/shard_map/ppermute | solution.py:489
  86.7 2.8 %copy-start.13 = (bf16[4,128,512]{2,1,0:T(8,128)(2,1)}, bf16[4,128,512]{2,1,0:T(8,128)(2,1)S(1)}, u32[]{:S(2)}) copy-start(bf16[4,128,512]{2,1,0:T(8,128)(2,1)S(1)} %collective-permute-done.21.refs_6_) | copy-start | bytes 1572868
  88.0 1.5 %copy-start.14 = (bf16[4,128,512]{2,1,0:T(8,128)(2,1)}, bf16[4,128,512]{2,1,0:T(8,128)(2,1)S(1)}, u32[]{:S(2)}) copy-start(bf16[4,128,512]{2,1,0:T(8,128)(2,1)S(1)} %collective-permute-done.22.refs_7_) | copy-start | bytes 1572868
  88.7 0.8 copy-start.15
  89.5 0.8 copy-start.16
where the time goes:
time: 114 us; the launch traced here: 113 us
  Pallas kernels  55.2 us (48%)
  starting transfers between devices  25.3 us (22%)
  waiting for transfers between devices  25.1 us (22%)
  local copies, waits for them, and re-layouts  4.48 us (4%)
  between operations  1.8 us (2%)
  other arithmetic  1.18 us (1%)
    pallas_call x1, Pallas kernels, panel_step(): pl.pallas_call(functools.partial(panel_kernel, plan, samples_all), out_sh...  32.6 us
    pallas_call x1, Pallas kernels, tile_step(): pl.pallas_call(functools.partial(tile_kernel, samples_all, n_places, len(...  22.6 us
    ppermute x6, starting transfers between devices, along_samp(): return [lax.ppermute(v, 'samp', pairs) for pairs in steps]  11.1 us
    ppermute x6, waiting for transfers between devices, along_samp(): return [lax.ppermute(v, 'samp', pairs) for pairs in steps]  5.81 us
    ppermute x1, waiting for transfers between devices, on_device(): far_a = lax.ppermute(by_pan[:2], 'mem', swap)  5.61 us
    ppermute x1, waiting for transfers between devices, on_device(): lax.ppermute(own, 'pan', swap)  4.66 us
    ppermute x1, waiting for transfers between devices, on_device(): lax.ppermute(part(1 - pan, col), 'pan', swap)  3.51 us
    unnamed x37, local copies, waits for them, and re-layouts  3.16 us
  transfers between devices with their start and end apart: 25, of which 11 were waited for; matrix products, arithmetic and copies ran while one was open for 1% of the time, Pallas kernels for 29%

commit v1 on v0

--- a/solution.py
+++ b/solution.py
@@ -47,7 +47,7 @@
     return base - (((t[0] + t[1]) + (t[2] + t[3])) + ((t[4] + t[5]) + (t[6] + t[7])))
 
 
-def inverse_factor(rows):
+def inverse_factor(rows, beside=None):
     count = block // sublanes
     sub = lax.broadcasted_iota(jnp.int32, (sublanes, block), 0)
     lane = lax.broadcasted_iota(jnp.int32, (sublanes, block), 1)
@@ -86,6 +86,8 @@
                 if more:
                     entry_next[m] = entry_next[m] - scaled[j] * entry
         out.append(jnp.where(lane <= first + sub, done, 0.0))
+        if beside is not None:
+            beside(p)
         if more:
             diag = [
                 take_away(after[m], scaled, [row_to_all(entry_next[j], m) for j in range(sublanes)])
@@ -118,49 +120,60 @@
     return out
 
 
-def invert_in_place(a, n, high, low, finish):
-    def rest_of(k):
-        here = slice(k * block, (k + 1) * block)
-        start = (k + 1) * block
+def invert_in_place(a, n, corner, fill, high, low, columns, line, finish):
+    def factor_of(value, beside=None):
+        return split(
+            jnp.concatenate(
+                inverse_factor([value[sublanes * g : sublanes * (g + 1)] for g in range(block // sublanes)], beside), axis=0
+            )
+        )
+
+    def make_line(k):
+        first = pl.multiple_of(k * block, block)
+        here = pl.ds(first, block)
         small = (high[here, here], low[here, here])
-        if k > 0:
-            left = split(dot3(small, split(a[here, 0 : k * block]), NN))
-            high[here, 0 : k * block], low[here, 0 : k * block] = left
-        if start < n:
-            for v in (high, low):
-                v[here, start:n] = jnp.zeros((block, n - start), BF16)
+        at = lax.broadcasted_iota(jnp.int32, (block, n), 0)
+        across = lax.broadcasted_iota(jnp.int32, (block, n), 1) - first
+        inside = (across >= 0) & (across < block)
+        given = jnp.where(inside, jnp.where(at == across, 1.0, 0.0), a[here, :])
+        found = dot3(small, split(given), NN)
+        high[here, :], low[here, :] = split(jnp.where(across < block, found, 0.0))
         finish(k)
-        if start == n:
-            return
-        rest = slice(start, n)
-        column = split(dot3(split(a[rest, here]), small, NT))
-        for i0 in range(start, n, 2 * block):
-            i1 = min(i0 + 2 * block, n)
-            left = tuple(v[i0 - start : i1 - start] for v in column)
-            right = tuple(v[0 : i1 - start] for v in column)
-            a[i0:i1, start:i1] = a[i0:i1, start:i1] - dot3(left, right, NT)
-        a[rest, here] = -dot3(column, small, NN)
-        if k > 0:
-            done = (high[here, 0 : k * block], low[here, 0 : k * block])
-            a[rest, 0 : k * block] = a[rest, 0 : k * block] - dot3(column, done, NN)
+        return found
 
     def step(k, carry):
         first = pl.multiple_of(k * block, block)
+        after = pl.ds(pl.multiple_of(first + block, block), block)
         here = pl.ds(first, block)
-        groups = [
-            a[pl.ds(pl.multiple_of(first + sublanes * g, sublanes), sublanes), here] for g in range(block // sublanes)
-        ]
-        high[here, here], low[here, here] = split(jnp.concatenate(inverse_factor(groups), axis=0))
-        for i in range(n // block):
-            pl.when(k == i)(functools.partial(rest_of, i))
+        small = (high[here, here], low[here, here])
+        left = split(dot3(split(a[after, here]), small, NT))
+        corner = a[after, after] - dot3(left, left, NT)
+        across = lax.broadcasted_iota(jnp.int32, (128, n), 1) - first
+        inside = (across >= 0) & (across < block)
+        turns = [2 * i for i in range(1, n // block)] + [n // block * 2 - 1]
+
+        def beside(p):
+            if p == 0:
+                line[0], line[1] = split(make_line(k))
+            if p == 1:
+                columns[0], columns[1] = split(dot3(split(a[:, here]), small, NT))
+            if p in turns:
+                i0 = turns.index(p) * 128
+                i1 = i0 + 128
+                change = dot3((columns[0, i0:i1, :], columns[1, i0:i1, :]), (line[0], line[1]), NN)
+                a[i0:i1, :] = jnp.where(inside, 0.0, a[i0:i1, :]) - change
+
+        high[after, after], low[after, after] = factor_of(corner, beside)
         return carry
 
-    lax.fori_loop(0, n // block, step, 0)
+    high[0:block, 0:block], low[0:block, 0:block] = factor_of(corner, fill)
+    lax.fori_loop(0, n // block - 1, step, 0)
+    make_line(n // block - 1)
 
 
 def panel_kernel(plan, samples_all, places, *refs):
     count = len(plan)
-    pieces, (high_ref, low_ref, panel_ref, data, a, high, low, in_sem, out_sem) = refs[:count], refs[count:]
+    pieces, (high_ref, low_ref, panel_ref, data, a, high, low, columns, line, in_sem, out_sem) = refs[:count], refs[count:]
     width, samples = data.shape
     copies = []
     for i, (piece, slots) in enumerate(zip(pieces, plan)):
@@ -178,15 +191,21 @@
     keep = pltpu.make_async_copy(data, panel_ref, out_sem)
     keep.start()
     step = 2 * block
-    for i0 in range(0, width, step):
-        i1 = i0 + step
-        part = dot1(data[i0:i1, :], data[0:i1, :], NT) / samples_all
-        at = lax.broadcasted_iota(jnp.int32, (step, i1), 0) + i0
-        across = lax.broadcasted_iota(jnp.int32, (step, i1), 1)
-        a[i0:i1, 0:i1] = part + jnp.where(at == across, ridge, 0.0)
+
+    def linkage_rows(i0, tall, wide):
+        part = dot1(data[i0 : i0 + tall, :], data[0:wide, :], NT) / samples_all
+        at = lax.broadcasted_iota(jnp.int32, part.shape, 0) + i0
+        across = lax.broadcasted_iota(jnp.int32, part.shape, 1)
+        return part + jnp.where(at == across, ridge, 0.0)
+
+    def fill(p):
+        turns = block // sublanes * step // width
+        if p % turns == 0:
+            i0 = p // turns * step
+            a[i0 : i0 + step, :] = linkage_rows(i0, step, width)
 
     def out_copies(k):
-        here = pl.ds(k * block, block)
+        here = pl.ds(pl.multiple_of(k * block, block), block)
         return [
             pltpu.make_async_copy(source.at[here, :], target.at[here, :], out_sem)
             for source, target in ((high, high_ref), (low, low_ref))
@@ -196,7 +215,7 @@
         for c in out_copies(k):
             c.start()
 
-    invert_in_place(a, width, high, low, finish)
+    invert_in_place(a, width, linkage_rows(0, block, block), fill, high, low, columns, line, finish)
     for k in range(width // block):
         for c in out_copies(k):
             c.wait()
@@ -218,6 +237,8 @@
             pltpu.VMEM((width, width), F32),
             pltpu.VMEM((width, width), BF16),
             pltpu.VMEM((width, width), BF16),
+            pltpu.VMEM((2, width, block), BF16),
+            pltpu.VMEM((2, block, width), BF16),
             pltpu.SemaphoreType.DMA,
             pltpu.SemaphoreType.DMA,
         ],
@@ -299,57 +320,48 @@
         for c in row_copies():
             c.wait()
 
+    tall = min(256, local_rows)
+    chunks = [(r0, r0 + tall) for r0 in range(0, local_rows, tall)]
+    tiles = [(j0, j0 + step) for j0 in range(0, width, step)]
     slabs = []
-    for r0 in range(0, local_rows, step):
-        slab = dot1(rows[r0 : r0 + step, :], panel[...], NT) / samples_all
+    for r0, r1 in chunks:
+        slab = dot1(rows[r0:r1, :], panel[...], NT) / samples_all
         at = lax.broadcasted_iota(jnp.int32, slab.shape, 0) + (row_place_panel + r0)
         across = lax.broadcasted_iota(jnp.int32, slab.shape, 1)
         slabs.append(split(slab + jnp.where((at == across) & rows_own, ridge, 0.0)))
     for c in loads:
         c.wait()
+    factors = []
+    for slab in slabs:
+        parts = [
+            dot3(tuple(v[:, :j1] for v in slab), tuple(v[j0:j1, :j1] for v in inverse), NT) for j0, j1 in tiles
+        ]
+        factors.append(split(jnp.concatenate(parts, axis=1)))
+    weights = []
+    for (r0, r1), factor in zip(chunks, factors):
+        parts = [
+            dot3(tuple(v[:, j0:] for v in factor), tuple(v[j0:, j0:j1] for v in inverse), NN) for j0, j1 in tiles
+        ]
+        value = jnp.concatenate(parts, axis=1)
+        cond_ref[r0:r1, :] = value
+        weights.append(split(value))
     scores = score_refs[0][...]
     if n_scores == 2:
         beside = score_refs[1][...]
         first = row_place_panel == 0
         scores = jnp.concatenate([jnp.where(first, scores, beside), jnp.where(first, beside, scores)], axis=1)
     scores = split(scores)
-    for j0 in range(0, width, step):
-        j1 = j0 + step
+    for j0, j1 in tiles:
         whitened_ref[:, j0:j1] = dot3(
             tuple(v[:, :j1] for v in scores), tuple(v[j0:j1, :j1] for v in inverse), NT
         )
-    whitened = split(whitened_ref[...])
-    for slab, r0 in zip(slabs, range(0, local_rows, step)):
-        r1 = r0 + step
-        factor = jnp.concatenate(
-            [
-                dot3(
-                    tuple(v[:, : j0 + step] for v in slab),
-                    tuple(v[j0 : j0 + step, : j0 + step] for v in inverse),
-                    NT,
-                )
-                for j0 in range(0, width, step)
-            ],
-            axis=1,
-        )
-        factor = split(factor)
-        residual_ref[:, r0:r1] = own_ref[:, r0:r1] - dot3(whitened, factor, NT)
-        weights = jnp.concatenate(
-            [
-                dot3(
-                    tuple(v[:, j0:] for v in factor),
-                    tuple(v[j0:, j0 : j0 + step] for v in inverse),
-                    NN,
-                )
-                for j0 in range(0, width, step)
-            ],
-            axis=1,
-        )
-        parts = split(weights)
+    for (r0, r1), parts in zip(chunks, weights):
         both = jnp.concatenate([panel[...], panel[...]], axis=0)
         explained = dot1(jnp.concatenate(parts, axis=1), both, NN)
         change[r0:r1, :] = (rows[r0:r1, :].astype(F32) - explained).astype(BF16)
-        cond_ref[r0:r1, :] = weights
+    whitened = split(whitened_ref[...])
+    for (r0, r1), factor in zip(chunks, factors):
+        residual_ref[:, r0:r1] = own_ref[:, r0:r1] - dot3(whitened, factor, NT)
 
     @pl.when(cols_own)
     def _():
@@ -361,8 +373,7 @@
             c.wait()
 
     row_first, col_first = facts[3], facts[4]
-    for r0 in range(0, local_rows, step):
-        r1 = r0 + step
+    for r0, r1 in chunks:
         part = dot1(change[r0:r1, :], cols[...], NT) / samples_all
         at = lax.broadcasted_iota(jnp.int32, part.shape, 0) + (row_first + r0)
         across = lax.broadcasted_iota(jnp.int32, part.shape, 1) + col_first

time: 114 us -> 110 us (0.965)
  Pallas kernels: 55.2 us -> 50.9 us
    pallas_call x1, Pallas kernels: 32.6 us -> 29.7 us  [panel_step(): pl.pallas_call(functools.partial(panel_kernel, plan, samples_all), out_sh...]
    pallas_call x1, Pallas kernels: 22.6 us -> 21.2 us  [tile_step(): pl.pallas_call(functools.partial(tile_kernel, samples_all, n_places, len(...]
  transfers between devices with their start and end apart: 25 -> 25, of which waited for: 11 -> 11; matrix products, arithmetic and copies ran while one was open for 1% -> 1% of each run, Pallas kernels for 29% -> 27%
where the time goes in v1:
time: 110 us; the launch traced here: 109 us
  Pallas kernels  50.9 us (46%)
  starting transfers between devices  25.3 us (23%)
  waiting for transfers between devices  25.1 us (23%)
  local copies, waits for them, and re-layouts  4.48 us (4%)
  between operations  1.8 us (2%)
  other arithmetic  1.18 us (1%)
    pallas_call x1, Pallas kernels, panel_step(): pl.pallas_call(functools.partial(panel_kernel, plan, samples_all), out_sh...  29.7 us
    pallas_call x1, Pallas kernels, tile_step(): pl.pallas_call(functools.partial(tile_kernel, samples_all, n_places, len(...  21.2 us
    ppermute x6, starting transfers between devices, along_samp(): return [lax.ppermute(v, 'samp', pairs) for pairs in steps]  11.1 us
    ppermute x6, waiting for transfers between devices, along_samp(): return [lax.ppermute(v, 'samp', pairs) for pairs in steps]  5.81 us
    ppermute x1, waiting for transfers between devices, on_device(): far_a = lax.ppermute(by_pan[:2], 'mem', swap)  5.61 us
    ppermute x1, waiting for transfers between devices, on_device(): lax.ppermute(own, 'pan', swap)  4.66 us
    ppermute x1, waiting for transfers between devices, on_device(): lax.ppermute(part(1 - pan, col), 'pan', swap)  3.51 us
    unnamed x37, local copies, waits for them, and re-layouts  3.16 us
  transfers between devices with their start and end apart: 25, of which 11 were waited for; matrix products, arithmetic and copies ran while one was open for 1% of the time, Pallas kernels for 27%

profile of v1, /device:TPU:0, one launch (start us, length us, event | category | flops | bytes accessed | tf_op | source)
XLA Modules:
  0.0 108.7 jit_solution(2089520204417853990)
XLA Ops:
  0.7 0.7 broadcast_multiply_fusion.1
  1.4 1.6 %copy.8 = s32[512,512]{0,1:T(8,128)S(1)} copy(s32[512,512]{1,0:T(8,128)} %param.5) | data formatting | bytes 2097152 | tf_op args[0]
  3.0 0.2 divide_convert_fusion
  3.2 3.0 %collective-permute-start = (bf16[128,512]{1,0:T(8,128)(2,1)S(1)}, bf16[128,512]{1,0:T(8,128)(2,1)S(1)}, u32[]{:S(2)}, u32[]{:S(2)}) collective-permute-start(bf16[128,512]{1,0:T(8,128)(2,1)S(1)} %dynamic-slice_bitcast_fusion), channel_id=1, source_target_pairs={{0,4},{4,0},{1,5},{5,1},{2,6},{6,2},{3,7},{7,3},{8,12},{12,8},{9,1... | collective-permute-start | bytes 393224 | tf_op jit(solution)/shard_map/ppermute | solution.py:434
  6.3 0.1 collective-permute-start.4
  7.1 3.5 %collective-permute-done = bf16[128,512]{1,0:T(8,128)(2,1)S(1)} collective-permute-done((bf16[128,512]{1,0:T(8,128)(2,1)S(1)}, bf16[128,512]{1,0:T(8,128)(2,1)S(1)}, u32[]{:S(2)}, u32[]{:S(2)}) %collective-permute-start) | collective-permute-done | bytes 131104 | tf_op jit(solution)/shard_map/ppermute | solution.py:434
  10.6 0.1 bitcast_select_fusion
  10.6 2.2 %collective-permute-start.1 = (bf16[128,512]{1,0:T(8,128)(2,1)S(1)}, bf16[128,512]{1,0:T(8,128)(2,1)S(1)}, u32[]{:S(2)}, u32[]{:S(2)}) collective-permute-start(bf16[128,512]{1,0:T(8,128)(2,1)S(1)} %get-tuple-element.32), channel_id=1, source_target_pairs={{0,8},{8,16},{16,24},{24,0},{1,9},{9,17},{17,25},{25,1},{2,10},{10... | collective-permute-start | bytes 393224 | tf_op jit(solution)/shard_map/ppermute | solution.py:440
  12.8 2.6 %collective-permute-start.2 = (bf16[128,512]{1,0:T(8,128)(2,1)S(1)}, bf16[128,512]{1,0:T(8,128)(2,1)S(1)}, u32[]{:S(2)}, u32[]{:S(2)}) collective-permute-start(bf16[128,512]{1,0:T(8,128)(2,1)S(1)} %get-tuple-element.32), channel_id=1, source_target_pairs={{0,16},{8,24},{16,0},{24,8},{1,17},{9,25},{17,1},{25,9},{2,18},{10... | collective-permute-start | bytes 393224 | tf_op jit(solution)/shard_map/ppermute | solution.py:440
  15.4 1.3 %collective-permute-start.3 = (bf16[128,512]{1,0:T(8,128)(2,1)S(1)}, bf16[128,512]{1,0:T(8,128)(2,1)S(1)}, u32[]{:S(2)}, u32[]{:S(2)}) collective-permute-start(bf16[128,512]{1,0:T(8,128)(2,1)S(1)} %get-tuple-element.32), channel_id=1, source_target_pairs={{0,24},{8,0},{16,8},{24,16},{1,25},{9,1},{17,9},{25,17},{2,26},{10... | collective-permute-start | bytes 393224 | tf_op jit(solution)/shard_map/ppermute | solution.py:440
  16.7 0.0 collective-permute-done.4
  16.8 2.5 %collective-permute-done.1 = bf16[128,512]{1,0:T(8,128)(2,1)S(1)} collective-permute-done((bf16[128,512]{1,0:T(8,128)(2,1)S(1)}, bf16[128,512]{1,0:T(8,128)(2,1)S(1)}, u32[]{:S(2)}, u32[]{:S(2)}) %collective-permute-start.1) | collective-permute-done | bytes 131104 | tf_op jit(solution)/shard_map/ppermute | solution.py:440
  19.3 3.3 %collective-permute-done.2 = bf16[128,512]{1,0:T(8,128)(2,1)S(1)} collective-permute-done((bf16[128,512]{1,0:T(8,128)(2,1)S(1)}, bf16[128,512]{1,0:T(8,128)(2,1)S(1)}, u32[]{:S(2)}, u32[]{:S(2)}) %collective-permute-start.2) | collective-permute-done | bytes 131104 | tf_op jit(solution)/shard_map/ppermute | solution.py:440
  22.6 0.0 collective-permute-done.3
  22.6 0.1 pad_maximum_fusion.refs_0_
  22.6 0.0 copy-start
  22.7 1.7 %collective-permute-start.6 = (bf16[4,128,512]{2,1,0:T(8,128)(2,1)S(1)}, bf16[4,128,512]{2,1,0:T(8,128)(2,1)S(1)}, u32[]{:S(2)}, u32[]{:S(2)}) collective-permute-start(bf16[4,128,512]{2,1,0:T(8,128)(2,1)S(1)} %pad_maximum_fusion.refs_0_), channel_id=1, source_target_pairs={{0,4},{4,0},{1,5},{5,1},{2,6},{6,2},{3,7},{7,3},{8,12},{12,8},{9,1... | collective-permute-start | bytes 1572872 | tf_op jit(solution)/shard_map/ppermute | solution.py:446
  24.3 1.5 %collective-permute-start.5 = (bf16[4,128,512]{2,1,0:T(8,128)(2,1)S(1)}, bf16[4,128,512]{2,1,0:T(8,128)(2,1)S(1)}, u32[]{:S(2)}, u32[]{:S(2)}) collective-permute-start(bf16[4,128,512]{2,1,0:T(8,128)(2,1)S(1)} %pad_maximum_fusion.refs_0_), channel_id=1, source_target_pairs={{0,2},{2,0},{1,3},{3,1},{4,6},{6,4},{5,7},{7,5},{8,10},{10,8},{9,1... | collective-permute-start | bytes 1572872 | tf_op jit(solution)/shard_map/ppermute | solution.py:446
  25.8 2.7 %collective-permute-start.14 = (bf16[128,512]{1,0:T(8,128)(2,1)S(1)}, bf16[128,512]{1,0:T(8,128)(2,1)S(1)}, u32[]{:S(2)}, u32[]{:S(2)}) collective-permute-start(bf16[128,512]{1,0:T(8,128)(2,1)S(1)} %get-tuple-element.22), channel_id=1, source_target_pairs={{0,8},{8,16},{16,24},{24,0},{1,9},{9,17},{17,25},{25,1},{2,10},{10... | collective-permute-start | bytes 393224 | tf_op jit(solution)/shard_map/ppermute | solution.py:440
  28.5 1.6 %collective-permute-start.15 = (bf16[128,512]{1,0:T(8,128)(2,1)S(1)}, bf16[128,512]{1,0:T(8,128)(2,1)S(1)}, u32[]{:S(2)}, u32[]{:S(2)}) collective-permute-start(bf16[128,512]{1,0:T(8,128)(2,1)S(1)} %get-tuple-element.22), channel_id=1, source_target_pairs={{0,16},{8,24},{16,0},{24,8},{1,17},{9,25},{17,1},{25,9},{2,18},{10... | collective-permute-start | bytes 393224 | tf_op jit(solution)/shard_map/ppermute | solution.py:440
  30.1 0.8 collective-permute-start.16
  30.9 4.7 %collective-permute-done.6.refs_2_ = bf16[4,128,512]{2,1,0:T(8,128)(2,1)S(1)} collective-permute-done((bf16[4,128,512]{2,1,0:T(8,128)(2,1)S(1)}, bf16[4,128,512]{2,1,0:T(8,128)(2,1)S(1)}, u32[]{:S(2)}, u32[]{:S(2)}) %collective-permute-start.6) | collective-permute-done | bytes 524320 | tf_op jit(solution)/shard_map/ppermute | solution.py:446
  35.5 1.3 %collective-permute-start.17 = (f32[64,512]{1,0:T(8,128)S(1)}, f32[64,512]{1,0:T(8,128)S(1)}, u32[]{:S(2)}, u32[]{:S(2)}) collective-permute-start(f32[64,512]{1,0:T(8,128)S(1)} %broadcast_select_fusion.refs_0_), channel_id=1, source_target_pairs={{0,2},{2,0},{1,3},{3,1},{4,6},{6,4},{5,7},{7,5},{8,10},{10,8},{9,1... | collective-permute-start | bytes 393224 | tf_op jit(solution)/shard_map/ppermute | solution.py:445
  36.9 0.1 collective-permute-done.5.refs_1_
  36.9 0.0 collective-permute-start.9
  37.0 0.0 collective-permute-done.14
  37.0 2.0 %collective-permute-start.7 = (bf16[2,128,512]{2,1,0:T(8,128)(2,1)S(1)}, bf16[2,128,512]{2,1,0:T(8,128)(2,1)}, u32[]{:S(2)}, u32[]{:S(2)}) collective-permute-start(bf16[2,128,512]{2,1,0:T(8,128)(2,1)S(1)} %slice.8), channel_id=1, source_target_pairs={{0,2},{2,0},{1,3},{3,1},{4,6},{6,4},{5,7},{7,5},{8,10},{10,8},{9,1... | collective-permute-start | bytes 786440 | tf_op jit(solution)/shard_map/ppermute | solution.py:447
  39.0 0.0 collective-permute-done.15
  39.0 0.1 collective-permute-start.8
  39.1 0.0 collective-permute-done.16
  39.1 0.2 collective-permute-start.10
  39.3 1.3 %collective-permute-done.17.refs_1_ = f32[64,512]{1,0:T(8,128)S(1)} collective-permute-done((f32[64,512]{1,0:T(8,128)S(1)}, f32[64,512]{1,0:T(8,128)S(1)}, u32[]{:S(2)}, u32[]{:S(2)}) %collective-permute-start.17) | collective-permute-done | bytes 131104 | tf_op jit(solution)/shard_map/ppermute | solution.py:445
  40.6 0.0 collective-permute-start.11
  40.6 5.6 %collective-permute-done.7.refs_3_ = bf16[2,128,512]{2,1,0:T(8,128)(2,1)} collective-permute-done((bf16[2,128,512]{2,1,0:T(8,128)(2,1)S(1)}, bf16[2,128,512]{2,1,0:T(8,128)(2,1)}, u32[]{:S(2)}, u32[]{:S(2)}) %collective-permute-start.7) | collective-permute-done | bytes 262176 | tf_op jit(solution)/shard_map/ppermute | solution.py:447
  46.2 0.0 collective-permute-start.12
  46.2 1.3 %collective-permute-done.8.refs_4_ = bf16[2,128,512]{2,1,0:T(8,128)(2,1)} collective-permute-done((bf16[2,128,512]{2,1,0:T(8,128)(2,1)S(1)}, bf16[2,128,512]{2,1,0:T(8,128)(2,1)}, u32[]{:S(2)}, u32[]{:S(2)}) %collective-permute-start.8) | collective-permute-done | bytes 262176 | tf_op jit(solution)/shard_map/ppermute | solution.py:448
  47.5 0.0 collective-permute-start.13
  47.5 0.6 stack.127.places
  48.1 0.7 stack.126.facts
  48.8 0.1 pad_maximum_fusion.1.refs_2_
  48.9 0.0 collective-permute-done.9.refs_5_
  48.9 0.9 collective-permute-start.18
  49.8 0.0 collective-permute-done.12.refs_8_
  49.8 1.2 %collective-permute-start.19 = (bf16[4,128,512]{2,1,0:T(8,128)(2,1)S(1)}, bf16[4,128,512]{2,1,0:T(8,128)(2,1)S(1)}, u32[]{:S(2)}, u32[]{:S(2)}) collective-permute-start(bf16[4,128,512]{2,1,0:T(8,128)(2,1)S(1)} %pad_maximum_fusion.1.refs_2_), channel_id=1, source_target_pairs={{0,4},{4,0},{1,5},{5,1},{2,6},{6,2},{3,7},{7,3},{8,12},{12,8},{9,1... | collective-permute-start | bytes 1572872 | tf_op jit(solution)/shard_map/ppermute | solution.py:468
  51.0 0.0 collective-permute-done.13.refs_9_
  51.0 1.5 %collective-permute-start.20 = (bf16[4,128,512]{2,1,0:T(8,128)(2,1)S(1)}, bf16[4,128,512]{2,1,0:T(8,128)(2,1)S(1)}, u32[]{:S(2)}, u32[]{:S(2)}) collective-permute-start(bf16[4,128,512]{2,1,0:T(8,128)(2,1)S(1)} %pad_maximum_fusion.1.refs_2_), channel_id=1, source_target_pairs={{0,6},{2,4},{4,2},{6,0},{1,7},{3,5},{5,3},{7,1},{8,14},{10,12},{12... | collective-permute-start | bytes 1572872 | tf_op jit(solution)/shard_map/ppermute | solution.py:469
  52.5 0.0 collective-permute-done.10.refs_6_
  52.5 0.0 collective-permute-start.21
  52.5 0.0 collective-permute-done.11.refs_7_
  52.5 0.8 copy-done.9
  53.3 29.7 %shard_map.76 = (bf16[1024,1024]{1,0:T(8,128)(2,1)}, bf16[1024,1024]{1,0:T(8,128)(2,1)}, bf16[1024,2048]{1,0:T(8,128)(2,1)}) custom-call(s32[14]{0:T(128)} %stack.127.places, bf16[4,128,512]{2,1,0:T(8,128)(2,1)} %copy-done, bf16[4,128,512]{2,1,0:T(8,128)(2,1)} %copy-done.4, bf16[4,128,512]{2,1,0:T(8,128)(2,1)} %copy-done.3, ...), custom_call_target="tpu_custom_call" | custom-call | flops 40000000000 | bytes 20971520 | tf_op jit(solution)/shard_map/pallas_call | solution.py:226
  83.0 0.0 collective-permute-done.18.refs_3_
  83.0 0.0 collective-permute-done.19.refs_4_
  83.0 0.0 collective-permute-done.20.refs_5_
  83.1 0.1 collective-permute-start.22
  83.1 0.5 collective-permute-start.23
  83.6 0.1 collective-permute-start.24
  83.7 0.0 collective-permute-done.21.refs_6_
  83.7 1.3 %collective-permute-done.22.refs_7_ = bf16[4,128,512]{2,1,0:T(8,128)(2,1)S(1)} collective-permute-done((bf16[4,128,512]{2,1,0:T(8,128)(2,1)S(1)}, bf16[4,128,512]{2,1,0:T(8,128)(2,1)S(1)}, u32[]{:S(2)}, u32[]{:S(2)}) %collective-permute-start.22) | collective-permute-done | bytes 524320 | tf_op jit(solution)/shard_map/ppermute | solution.py:500
  85.0 0.7 collective-permute-done.23.refs_8_
  85.8 0.7 collective-permute-done.24.refs_9_
  86.6 0.0 copy-done.15
  86.6 0.8 copy-done.16
  87.4 21.2 %shard_map.77 = (f32[512,1024]{1,0:T(8,128)}, f32[64,1024]{1,0:T(8,128)}, f32[64,512]{1,0:T(8,128)}) custom-call(s32[17]{0:T(128)} %stack.126.facts, bf16[1024,2048]{1,0:T(8,128)(2,1)} %get-tuple-element.20.panel_ref, bf16[1024,1024]{1,0:T(8,128)(2,1)} %get-tuple-element.25.high_ref, bf16[1024,1024]{1,0:T(8,128)(2,1)} %get-tuple-element.26.low_ref, ...), custom_call_target="tpu_custom_call" | custom-call | flops 20000000000 | bytes 20971520 | tf_op jit(solution)/shard_map/pallas_call | solution.py:390
  (38 shorter events, 0.2 us)
Async XLA Ops:
  0.6 5.6 %copy-start.7 = (s32[512]{0:T(512)S(1)}, s32[512]{0:T(512)}, u32[]{:S(2)}) copy-start(s32[512]{0:T(512)} %param.8) | copy-start | bytes 6148
  0.6 5.6 %copy-start.2 = (f32[64,512]{1,0:T(8,128)S(1)}, f32[64,512]{1,0:T(8,128)}, u32[]{:S(2)}) copy-start(f32[64,512]{1,0:T(8,128)} %param.7) | copy-start | bytes 393220
  3.2 7.4 %collective-permute-start = (bf16[128,512]{1,0:T(8,128)(2,1)S(1)}, bf16[128,512]{1,0:T(8,128)(2,1)S(1)}, u32[]{:S(2)}, u32[]{:S(2)}) collective-permute-start(bf16[128,512]{1,0:T(8,128)(2,1)S(1)} %dynamic-slice_bitcast_fusion), channel_id=1, source_target_pairs={{0,4},{4,0},{1,5},{5,1},{2,6},{6,2},{3,7},{7,3},{8,12},{12,8},{9,1... | collective-permute-start | bytes 393224 | tf_op jit(solution)/shard_map/ppermute | solution.py:434
  6.3 42.6 %copy-start.5 = (f32[64,512]{1,0:T(8,128)}, f32[64,512]{1,0:T(8,128)S(1)}, u32[]{:S(2)}) copy-start(f32[64,512]{1,0:T(8,128)S(1)} %broadcast_multiply_fusion.own_ref) | copy-start | bytes 393220
  6.3 10.5 %collective-permute-start.4 = (f32[64,512]{1,0:T(8,128)S(1)}, f32[64,512]{1,0:T(8,128)S(1)}, u32[]{:S(2)}, u32[]{:S(2)}) collective-permute-start(f32[64,512]{1,0:T(8,128)S(1)} %broadcast_multiply_fusion.own_ref), channel_id=1, source_target_pairs={{0,4},{4,0},{1,5},{5,1},{2,6},{6,2},{3,7},{7,3},{8,12},{12,8},{9,1... | collective-permute-start | bytes 393224 | tf_op jit(solution)/shard_map/ppermute | solution.py:443
  10.6 8.6 %collective-permute-start.1 = (bf16[128,512]{1,0:T(8,128)(2,1)S(1)}, bf16[128,512]{1,0:T(8,128)(2,1)S(1)}, u32[]{:S(2)}, u32[]{:S(2)}) collective-permute-start(bf16[128,512]{1,0:T(8,128)(2,1)S(1)} %get-tuple-element.32), channel_id=1, source_target_pairs={{0,8},{8,16},{16,24},{24,0},{1,9},{9,17},{17,25},{25,1},{2,10},{10... | collective-permute-start | bytes 393224 | tf_op jit(solution)/shard_map/ppermute | solution.py:440
  12.8 9.8 %collective-permute-start.2 = (bf16[128,512]{1,0:T(8,128)(2,1)S(1)}, bf16[128,512]{1,0:T(8,128)(2,1)S(1)}, u32[]{:S(2)}, u32[]{:S(2)}) collective-permute-start(bf16[128,512]{1,0:T(8,128)(2,1)S(1)} %get-tuple-element.32), channel_id=1, source_target_pairs={{0,16},{8,24},{16,0},{24,8},{1,17},{9,25},{17,1},{25,9},{2,18},{10... | collective-permute-start | bytes 393224 | tf_op jit(solution)/shard_map/ppermute | solution.py:440
  15.4 7.2 %collective-permute-start.3 = (bf16[128,512]{1,0:T(8,128)(2,1)S(1)}, bf16[128,512]{1,0:T(8,128)(2,1)S(1)}, u32[]{:S(2)}, u32[]{:S(2)}) collective-permute-start(bf16[128,512]{1,0:T(8,128)(2,1)S(1)} %get-tuple-element.32), channel_id=1, source_target_pairs={{0,24},{8,0},{16,8},{24,16},{1,25},{9,1},{17,9},{25,17},{2,26},{10... | collective-permute-start | bytes 393224 | tf_op jit(solution)/shard_map/ppermute | solution.py:440
  16.8 66.2 %copy-start.6 = (f32[64,512]{1,0:T(8,128)}, f32[64,512]{1,0:T(8,128)S(1)}, u32[]{:S(2)}) copy-start(f32[64,512]{1,0:T(8,128)S(1)} %broadcast_select_fusion.refs_0_) | copy-start | bytes 393220
  22.6 29.9 %copy-start = (bf16[4,128,512]{2,1,0:T(8,128)(2,1)}, bf16[4,128,512]{2,1,0:T(8,128)(2,1)S(1)}, u32[]{:S(2)}) copy-start(bf16[4,128,512]{2,1,0:T(8,128)(2,1)S(1)} %pad_maximum_fusion.refs_0_) | copy-start | bytes 1572868
  22.7 12.9 %collective-permute-start.6 = (bf16[4,128,512]{2,1,0:T(8,128)(2,1)S(1)}, bf16[4,128,512]{2,1,0:T(8,128)(2,1)S(1)}, u32[]{:S(2)}, u32[]{:S(2)}) collective-permute-start(bf16[4,128,512]{2,1,0:T(8,128)(2,1)S(1)} %pad_maximum_fusion.refs_0_), channel_id=1, source_target_pairs={{0,4},{4,0},{1,5},{5,1},{2,6},{6,2},{3,7},{7,3},{8,12},{12,8},{9,1... | collective-permute-start | bytes 1572872 | tf_op jit(solution)/shard_map/ppermute | solution.py:446
  24.3 12.6 %collective-permute-start.5 = (bf16[4,128,512]{2,1,0:T(8,128)(2,1)S(1)}, bf16[4,128,512]{2,1,0:T(8,128)(2,1)S(1)}, u32[]{:S(2)}, u32[]{:S(2)}) collective-permute-start(bf16[4,128,512]{2,1,0:T(8,128)(2,1)S(1)} %pad_maximum_fusion.refs_0_), channel_id=1, source_target_pairs={{0,2},{2,0},{1,3},{3,1},{4,6},{6,4},{5,7},{7,5},{8,10},{10,8},{9,1... | collective-permute-start | bytes 1572872 | tf_op jit(solution)/shard_map/ppermute | solution.py:446
  25.8 11.1 %collective-permute-start.14 = (bf16[128,512]{1,0:T(8,128)(2,1)S(1)}, bf16[128,512]{1,0:T(8,128)(2,1)S(1)}, u32[]{:S(2)}, u32[]{:S(2)}) collective-permute-start(bf16[128,512]{1,0:T(8,128)(2,1)S(1)} %get-tuple-element.22), channel_id=1, source_target_pairs={{0,8},{8,16},{16,24},{24,0},{1,9},{9,17},{17,25},{25,1},{2,10},{10... | collective-permute-start | bytes 393224 | tf_op jit(solution)/shard_map/ppermute | solution.py:440
  28.5 10.5 %collective-permute-start.15 = (bf16[128,512]{1,0:T(8,128)(2,1)S(1)}, bf16[128,512]{1,0:T(8,128)(2,1)S(1)}, u32[]{:S(2)}, u32[]{:S(2)}) collective-permute-start(bf16[128,512]{1,0:T(8,128)(2,1)S(1)} %get-tuple-element.22), channel_id=1, source_target_pairs={{0,16},{8,24},{16,0},{24,8},{1,17},{9,25},{17,1},{25,9},{2,18},{10... | collective-permute-start | bytes 393224 | tf_op jit(solution)/shard_map/ppermute | solution.py:440
  30.1 9.0 %collective-permute-start.16 = (bf16[128,512]{1,0:T(8,128)(2,1)S(1)}, bf16[128,512]{1,0:T(8,128)(2,1)S(1)}, u32[]{:S(2)}, u32[]{:S(2)}) collective-permute-start(bf16[128,512]{1,0:T(8,128)(2,1)S(1)} %get-tuple-element.22), channel_id=1, source_target_pairs={{0,24},{8,0},{16,8},{24,16},{1,25},{9,1},{17,9},{25,17},{2,26},{10... | collective-permute-start | bytes 393224 | tf_op jit(solution)/shard_map/ppermute | solution.py:440
  35.5 17.0 %copy-start.3 = (bf16[4,128,512]{2,1,0:T(8,128)(2,1)}, bf16[4,128,512]{2,1,0:T(8,128)(2,1)S(1)}, u32[]{:S(2)}) copy-start(bf16[4,128,512]{2,1,0:T(8,128)(2,1)S(1)} %collective-permute-done.6.refs_2_) | copy-start | bytes 1572868
  35.5 5.1 %collective-permute-start.17 = (f32[64,512]{1,0:T(8,128)S(1)}, f32[64,512]{1,0:T(8,128)S(1)}, u32[]{:S(2)}, u32[]{:S(2)}) collective-permute-start(f32[64,512]{1,0:T(8,128)S(1)} %broadcast_select_fusion.refs_0_), channel_id=1, source_target_pairs={{0,2},{2,0},{1,3},{3,1},{4,6},{6,4},{5,7},{7,5},{8,10},{10,8},{9,1... | collective-permute-start | bytes 393224 | tf_op jit(solution)/shard_map/ppermute | solution.py:445
  36.9 15.6 %copy-start.4 = (bf16[4,128,512]{2,1,0:T(8,128)(2,1)}, bf16[4,128,512]{2,1,0:T(8,128)(2,1)S(1)}, u32[]{:S(2)}) copy-start(bf16[4,128,512]{2,1,0:T(8,128)(2,1)S(1)} %collective-permute-done.5.refs_1_) | copy-start | bytes 1572868
  36.9 12.0 %collective-permute-start.9 = (bf16[4,128,512]{2,1,0:T(8,128)(2,1)S(1)}, bf16[4,128,512]{2,1,0:T(8,128)(2,1)S(1)}, u32[]{:S(2)}, u32[]{:S(2)}) collective-permute-start(bf16[4,128,512]{2,1,0:T(8,128)(2,1)S(1)} %pad_maximum_fusion.refs_0_), channel_id=1, source_target_pairs={{0,1},{1,0},{2,3},{3,2},{4,5},{5,4},{6,7},{7,6},{8,9},{9,8},{10,11... | collective-permute-start | bytes 1572872 | tf_op jit(solution)/shard_map/ppermute | solution.py:450
  37.0 9.2 %collective-permute-start.7 = (bf16[2,128,512]{2,1,0:T(8,128)(2,1)S(1)}, bf16[2,128,512]{2,1,0:T(8,128)(2,1)}, u32[]{:S(2)}, u32[]{:S(2)}) collective-permute-start(bf16[2,128,512]{2,1,0:T(8,128)(2,1)S(1)} %slice.8), channel_id=1, source_target_pairs={{0,2},{2,0},{1,3},{3,1},{4,6},{6,4},{5,7},{7,5},{8,10},{10,8},{9,1... | collective-permute-start | bytes 786440 | tf_op jit(solution)/shard_map/ppermute | solution.py:447
  39.0 8.5 %collective-permute-start.8 = (bf16[2,128,512]{2,1,0:T(8,128)(2,1)S(1)}, bf16[2,128,512]{2,1,0:T(8,128)(2,1)}, u32[]{:S(2)}, u32[]{:S(2)}) collective-permute-start(bf16[2,128,512]{2,1,0:T(8,128)(2,1)S(1)} %slice.9), channel_id=1, source_target_pairs={{0,4},{4,0},{1,5},{5,1},{2,6},{6,2},{3,7},{7,3},{8,12},{12,8},{9,1... | collective-permute-start | bytes 786440 | tf_op jit(solution)/shard_map/ppermute | solution.py:448
  39.1 13.4 %collective-permute-start.10 = (bf16[4,128,512]{2,1,0:T(8,128)(2,1)S(1)}, bf16[4,128,512]{2,1,0:T(8,128)(2,1)S(1)}, u32[]{:S(2)}, u32[]{:S(2)}) collective-permute-start(bf16[4,128,512]{2,1,0:T(8,128)(2,1)S(1)} %collective-permute-done.5.refs_1_), channel_id=1, source_target_pairs={{0,1},{1,0},{2,3},{3,2},{4,5},{5,4},{6,7},{7,6},{8,9},{9,8},{10,11... | collective-permute-start | bytes 1572872 | tf_op jit(solution)/shard_map/ppermute | solution.py:450
  40.6 42.4 %copy-start.17 = (f32[64,512]{1,0:T(8,128)}, f32[64,512]{1,0:T(8,128)S(1)}, u32[]{:S(2)}) copy-start(f32[64,512]{1,0:T(8,128)S(1)} %collective-permute-done.17.refs_1_) | copy-start | bytes 393220
  40.6 11.9 %collective-permute-start.11 = (bf16[4,128,512]{2,1,0:T(8,128)(2,1)S(1)}, bf16[4,128,512]{2,1,0:T(8,128)(2,1)}, u32[]{:S(2)}, u32[]{:S(2)}) collective-permute-start(bf16[4,128,512]{2,1,0:T(8,128)(2,1)S(1)} %collective-permute-done.6.refs_2_), channel_id=1, source_target_pairs={{0,1},{1,0},{2,3},{3,2},{4,5},{5,4},{6,7},{7,6},{8,9},{9,8},{10,11... | collective-permute-start | bytes 1572872 | tf_op jit(solution)/shard_map/ppermute | solution.py:450
  46.2 3.6 %collective-permute-start.12 = (bf16[2,128,512]{2,1,0:T(8,128)(2,1)}, bf16[2,128,512]{2,1,0:T(8,128)(2,1)}, u32[]{:S(2)}, u32[]{:S(2)}) collective-permute-start(bf16[2,128,512]{2,1,0:T(8,128)(2,1)} %collective-permute-done.7.refs_3_), channel_id=1, source_target_pairs={{0,1},{1,0},{2,3},{3,2},{4,5},{5,4},{6,7},{7,6},{8,9},{9,8},{10,11... | collective-permute-start | bytes 786440 | tf_op jit(solution)/shard_map/ppermute | solution.py:450
  47.5 3.5 %collective-permute-start.13 = (bf16[2,128,512]{2,1,0:T(8,128)(2,1)}, bf16[2,128,512]{2,1,0:T(8,128)(2,1)}, u32[]{:S(2)}, u32[]{:S(2)}) collective-permute-start(bf16[2,128,512]{2,1,0:T(8,128)(2,1)} %collective-permute-done.8.refs_4_), channel_id=1, source_target_pairs={{0,1},{1,0},{2,3},{3,2},{4,5},{5,4},{6,7},{7,6},{8,9},{9,8},{10,11... | collective-permute-start | bytes 786440 | tf_op jit(solution)/shard_map/ppermute | solution.py:450
  48.9 34.1 %copy-start.1 = (bf16[4,128,512]{2,1,0:T(8,128)(2,1)}, bf16[4,128,512]{2,1,0:T(8,128)(2,1)S(1)}, u32[]{:S(2)}) copy-start(bf16[4,128,512]{2,1,0:T(8,128)(2,1)S(1)} %pad_maximum_fusion.1.refs_2_) | copy-start | bytes 1572868
  48.9 3.6 %copy-start.8 = (bf16[4,128,512]{2,1,0:T(8,128)(2,1)}, bf16[4,128,512]{2,1,0:T(8,128)(2,1)S(1)}, u32[]{:S(2)}) copy-start(bf16[4,128,512]{2,1,0:T(8,128)(2,1)S(1)} %collective-permute-done.9.refs_5_) | copy-start | bytes 1572868
  48.9 34.1 %collective-permute-start.18 = (bf16[4,128,512]{2,1,0:T(8,128)(2,1)S(1)}, bf16[4,128,512]{2,1,0:T(8,128)(2,1)S(1)}, u32[]{:S(2)}, u32[]{:S(2)}) collective-permute-start(bf16[4,128,512]{2,1,0:T(8,128)(2,1)S(1)} %pad_maximum_fusion.1.refs_2_), channel_id=1, source_target_pairs={{0,2},{2,0},{1,3},{3,1},{4,6},{6,4},{5,7},{7,5},{8,10},{10,8},{9,1... | collective-permute-start | bytes 1572872 | tf_op jit(solution)/shard_map/ppermute | solution.py:467
  49.8 33.3 %collective-permute-start.19 = (bf16[4,128,512]{2,1,0:T(8,128)(2,1)S(1)}, bf16[4,128,512]{2,1,0:T(8,128)(2,1)S(1)}, u32[]{:S(2)}, u32[]{:S(2)}) collective-permute-start(bf16[4,128,512]{2,1,0:T(8,128)(2,1)S(1)} %pad_maximum_fusion.1.refs_2_), channel_id=1, source_target_pairs={{0,4},{4,0},{1,5},{5,1},{2,6},{6,2},{3,7},{7,3},{8,12},{12,8},{9,1... | collective-permute-start | bytes 1572872 | tf_op jit(solution)/shard_map/ppermute | solution.py:468
  51.0 32.0 %collective-permute-start.20 = (bf16[4,128,512]{2,1,0:T(8,128)(2,1)S(1)}, bf16[4,128,512]{2,1,0:T(8,128)(2,1)S(1)}, u32[]{:S(2)}, u32[]{:S(2)}) collective-permute-start(bf16[4,128,512]{2,1,0:T(8,128)(2,1)S(1)} %pad_maximum_fusion.1.refs_2_), channel_id=1, source_target_pairs={{0,6},{2,4},{4,2},{6,0},{1,7},{3,5},{5,3},{7,1},{8,14},{10,12},{12... | collective-permute-start | bytes 1572872 | tf_op jit(solution)/shard_map/ppermute | solution.py:469
  52.5 0.8 copy-start.9
  52.5 31.2 %collective-permute-start.21 = (bf16[4,128,512]{2,1,0:T(8,128)(2,1)S(1)}, bf16[4,128,512]{2,1,0:T(8,128)(2,1)S(1)}, u32[]{:S(2)}, u32[]{:S(2)}) collective-permute-start(bf16[4,128,512]{2,1,0:T(8,128)(2,1)S(1)} %pad_maximum_fusion.1.refs_2_), channel_id=1, source_target_pairs={{0,1},{1,0},{2,3},{3,2},{4,5},{5,4},{6,7},{7,6},{8,9},{9,8},{10,11... | collective-permute-start | bytes 1572872 | tf_op jit(solution)/shard_map/ppermute | solution.py:471
  83.0 3.5 %copy-start.10 = (bf16[4,128,512]{2,1,0:T(8,128)(2,1)}, bf16[4,128,512]{2,1,0:T(8,128)(2,1)S(1)}, u32[]{:S(2)}) copy-start(bf16[4,128,512]{2,1,0:T(8,128)(2,1)S(1)} %collective-permute-done.18.refs_3_) | copy-start | bytes 1572868
  83.0 3.5 %copy-start.11 = (bf16[4,128,512]{2,1,0:T(8,128)(2,1)}, bf16[4,128,512]{2,1,0:T(8,128)(2,1)S(1)}, u32[]{:S(2)}) copy-start(bf16[4,128,512]{2,1,0:T(8,128)(2,1)S(1)} %collective-permute-done.19.refs_4_) | copy-start | bytes 1572868
  83.1 3.5 %copy-start.12 = (bf16[4,128,512]{2,1,0:T(8,128)(2,1)}, bf16[4,128,512]{2,1,0:T(8,128)(2,1)S(1)}, u32[]{:S(2)}) copy-start(bf16[4,128,512]{2,1,0:T(8,128)(2,1)S(1)} %collective-permute-done.20.refs_5_) | copy-start | bytes 1572868
  83.1 2.0 %collective-permute-start.22 = (bf16[4,128,512]{2,1,0:T(8,128)(2,1)S(1)}, bf16[4,128,512]{2,1,0:T(8,128)(2,1)S(1)}, u32[]{:S(2)}, u32[]{:S(2)}) collective-permute-start(bf16[4,128,512]{2,1,0:T(8,128)(2,1)S(1)} %collective-permute-done.18.refs_3_), channel_id=1, source_target_pairs={{0,1},{1,0},{2,3},{3,2},{4,5},{5,4},{6,7},{7,6},{8,9},{9,8},{10,11... | collective-permute-start | bytes 1572872 | tf_op jit(solution)/shard_map/ppermute | solution.py:500
  83.1 2.6 %collective-permute-start.23 = (bf16[4,128,512]{2,1,0:T(8,128)(2,1)S(1)}, bf16[4,128,512]{2,1,0:T(8,128)(2,1)S(1)}, u32[]{:S(2)}, u32[]{:S(2)}) collective-permute-start(bf16[4,128,512]{2,1,0:T(8,128)(2,1)S(1)} %collective-permute-done.19.refs_4_), channel_id=1, source_target_pairs={{0,1},{1,0},{2,3},{3,2},{4,5},{5,4},{6,7},{7,6},{8,9},{9,8},{10,11... | collective-permute-start | bytes 1572872 | tf_op jit(solution)/shard_map/ppermute | solution.py:500
  83.6 2.9 %collective-permute-start.24 = (bf16[4,128,512]{2,1,0:T(8,128)(2,1)S(1)}, bf16[4,128,512]{2,1,0:T(8,128)(2,1)S(1)}, u32[]{:S(2)}, u32[]{:S(2)}) collective-permute-start(bf16[4,128,512]{2,1,0:T(8,128)(2,1)S(1)} %collective-permute-done.20.refs_5_), channel_id=1, source_target_pairs={{0,1},{1,0},{2,3},{3,2},{4,5},{5,4},{6,7},{7,6},{8,9},{9,8},{10,11... | collective-permute-start | bytes 1572872 | tf_op jit(solution)/shard_map/ppermute | solution.py:500
  83.7 2.8 %copy-start.13 = (bf16[4,128,512]{2,1,0:T(8,128)(2,1)}, bf16[4,128,512]{2,1,0:T(8,128)(2,1)S(1)}, u32[]{:S(2)}) copy-start(bf16[4,128,512]{2,1,0:T(8,128)(2,1)S(1)} %collective-permute-done.21.refs_6_) | copy-start | bytes 1572868
  85.0 1.5 %copy-start.14 = (bf16[4,128,512]{2,1,0:T(8,128)(2,1)}, bf16[4,128,512]{2,1,0:T(8,128)(2,1)S(1)}, u32[]{:S(2)}) copy-start(bf16[4,128,512]{2,1,0:T(8,128)(2,1)S(1)} %collective-permute-done.22.refs_7_) | copy-start | bytes 1572868
  85.8 0.8 copy-start.15
  86.5 0.8 copy-start.16

commit v2 on v1

--- a/solution.py
+++ b/solution.py
@@ -15,7 +15,8 @@
 NT = (((1,), (1,)), ((), ()))
 block = 128
 sublanes = 8
-vmem_bytes = 58 * 2**20
+panel_vmem = 30 * 2**20
+tile_vmem = 36 * 2**20
 
 
 def dot1(a, b, dims):
@@ -242,7 +243,7 @@
             pltpu.SemaphoreType.DMA,
             pltpu.SemaphoreType.DMA,
         ],
-        compiler_params=pltpu.CompilerParams(vmem_limit_bytes=vmem_bytes),
+        compiler_params=pltpu.CompilerParams(vmem_limit_bytes=panel_vmem),
         cost_estimate=pl.CostEstimate(flops=40 * 10**9, bytes_accessed=20 * 2**20, transcendentals=0),
     )(places, *pieces)
 
@@ -405,12 +406,16 @@
             pltpu.VMEM((local_rows, samples), BF16),
             pltpu.SemaphoreType.DMA((4,)),
         ],
-        compiler_params=pltpu.CompilerParams(vmem_limit_bytes=vmem_bytes),
+        compiler_params=pltpu.CompilerParams(vmem_limit_bytes=tile_vmem),
         cost_estimate=pl.CostEstimate(flops=20 * 10**9, bytes_accessed=20 * 2**20, transcendentals=0),
     )(facts, panel, high, low, own, *scores, *pieces, *extra)
 
 
 swap = [(0, 1), (1, 0)]
+
+
+def numbers(values):
+    return jnp.stack([jnp.asarray(v).astype(jnp.int32) for v in values])
 
 
 def on_device(genotypes, frequencies, trait_scores, typed_mask, panel_index):
@@ -425,6 +430,7 @@
     masked = trait_scores * typed_mask.astype(F32)
     own_panel = pan == q
     rest = []
+    common = [col == q, own_panel, mem * local_rows, (pan * n_mem + mem) * local_rows, col * width]
     if n_pan == 2 and n_mem == 2 and n_col == 2 and n_samp == 4:
         quarter = local_rows // 4
 
@@ -441,7 +447,15 @@
 
         own = jnp.stack([piece] + along_samp(piece))
         panel_masked = jnp.where(own_panel, masked, lax.ppermute(masked, "pan", swap))
-        own, panel_masked = lax.optimization_barrier((own, panel_masked))
+        corners = ((mem, pan), (1 - mem, pan), (mem, 1 - pan), (1 - mem, 1 - pan))
+        slots = [(samp - d) % n_samp for d in range(n_samp)]
+
+        def place(m, a, c):
+            return (m * 4 + a * 2 + c) * quarter
+
+        places = numbers([place(m, a, c) for c in (col, 1 - col) for m, a in corners + corners[3:]] + slots)
+        facts = numbers(common + [place(m, a, c) for c in (col, 1 - col) for m, a in corners] + slots)
+        own, panel_masked, places, facts = lax.optimization_barrier((own, panel_masked, places, facts))
         beside = lax.ppermute(panel_masked, "mem", swap)
         by_mem, by_pan = lax.ppermute(own, "mem", swap), lax.ppermute(own, "pan", swap)
         far_a = lax.ppermute(by_pan[:2], "mem", swap)
@@ -451,13 +465,6 @@
         pieces = near + twin
         plan = [(0, 1, 2, 3)] * 3 + [(0, 1), (2, 3)]
         plan = plan + plan
-
-        def place(m, a, c):
-            return (m * 4 + a * 2 + c) * quarter
-
-        slots = [(samp - d) % n_samp for d in range(n_samp)]
-        corners = ((mem, pan), (1 - mem, pan), (mem, 1 - pan), (1 - mem, 1 - pan))
-        places = [place(m, a, c) for c in (col, 1 - col) for m, a in corners + corners[3:]] + slots
         rest_piece, _ = lax.optimization_barrier((rest_piece, own))
         rest_own = jnp.stack([rest_piece] + along_samp(rest_piece))
         rest_own, _, _, beside = lax.optimization_barrier((rest_own, by_mem, by_pan, beside))
@@ -472,7 +479,6 @@
         col_plan = [[(d, t + 4 * c, d) for d in range(4)] for c in range(2) for t in range(4)]
         row_plan = [plan if i % 2 == 0 else [] for i, plan in enumerate(col_plan)]
         extra, n_places = [], 8
-        col_places = [place(m, a, c) for c in (col, 1 - col) for m, a in corners] + slots
         panel_scores = [panel_masked, beside]
     else:
         chosen = lax.psum(jnp.where(own_panel, standard, jnp.zeros_like(standard)), "pan")
@@ -485,13 +491,10 @@
         extra, n_places = [lax.all_gather(standard, "samp")], 1
         col_plan = [[(s, 0, s) for s in range(n_samp)]]
         row_plan = [[(s, -1, s) for s in range(n_samp)]]
-        col_places = places
+        facts = numbers(common + places)
+        places = numbers(places)
         panel_masked = lax.psum(jnp.where(own_panel, masked, jnp.zeros_like(masked)), "pan")
         panel_scores = [lax.all_gather(panel_masked, "mem", axis=1, tiled=True)]
-    places = jnp.stack([jnp.asarray(v).astype(jnp.int32) for v in places])
-    facts = [col == q, own_panel, mem * local_rows, (pan * n_mem + mem) * local_rows, col * width, *col_places]
-    facts = jnp.stack([jnp.asarray(f).astype(jnp.int32) for f in facts])
-    facts, places = lax.optimization_barrier((facts, places))
     high, low, panel_data = panel_step(pieces, plan, places, width, samples_all, samples_all)
     if rest:
         held = lax.optimization_barrier((high, *rest[1:]))

time: 110 us -> 103 us (0.936)
  Pallas kernels: 50.9 us -> 47 us
  local copies, waits for them, and re-layouts: 4.48 us -> 1.81 us
    pallas_call x1, Pallas kernels: 21.2 us -> 18.9 us  [tile_step(): pl.pallas_call(functools.partial(tile_kernel, samples_all, n_places, len(...]
    pallas_call x1, Pallas kernels: 29.7 us -> 28.1 us  [panel_step(): pl.pallas_call(functools.partial(panel_kernel, plan, samples_all), out_sh...]
    unnamed x37 -> x5, local copies, waits for them, and re-layouts: 3.16 us -> 1.57 us
  transfers between devices with their start and end apart: 25 -> 25, of which waited for: 11 -> 11; matrix products, arithmetic and copies ran while one was open for 1% -> 0% of each run, Pallas kernels for 27% -> 28%
where the time goes in v2:
time: 103 us; the launch traced here: 102 us
  Pallas kernels  47 us (46%)
  starting transfers between devices  25.7 us (25%)
  waiting for transfers between devices  24.5 us (24%)
  local copies, waits for them, and re-layouts  1.81 us (2%)
  between operations  1.73 us (2%)
  other arithmetic  1.18 us (1%)
    pallas_call x1, Pallas kernels, panel_step(): pl.pallas_call(functools.partial(panel_kernel, plan, samples_all), out_sh...  28.1 us
    pallas_call x1, Pallas kernels, tile_step(): pl.pallas_call(functools.partial(tile_kernel, samples_all, n_places, len(...  18.9 us
    ppermute x6, starting transfers between devices, along_samp(): return [lax.ppermute(v, 'samp', pairs) for pairs in steps]  11.1 us
    ppermute x6, waiting for transfers between devices, along_samp(): return [lax.ppermute(v, 'samp', pairs) for pairs in steps]  5.81 us
    ppermute x1, waiting for transfers between devices, on_device(): far_a = lax.ppermute(by_pan[:2], 'mem', swap)  5.51 us
    ppermute x1, waiting for transfers between devices, on_device(): lax.ppermute(own, 'pan', swap)  4.66 us
    ppermute x1, waiting for transfers between devices, on_device(): lax.ppermute(part(1 - pan, col), 'pan', swap)  3.22 us
    ppermute x1, starting transfers between devices, on_device(): lax.ppermute(part(1 - pan, col), 'pan', swap)  3.03 us
  transfers between devices with their start and end apart: 25, of which 11 were waited for; matrix products, arithmetic and copies ran while one was open for 0% of the time, Pallas kernels for 28%

profile of v2, /device:TPU:0, one launch (start us, length us, event | category | flops | bytes accessed | tf_op | source)
XLA Modules:
  0.0 101.9 jit_solution(5088262519504215552)
XLA Ops:
  0.6 0.0 copy-start.1
  0.6 0.0 copy-start
  0.7 0.7 broadcast_multiply_fusion.1
  1.4 1.6 %copy.8 = s32[512,512]{0,1:T(8,128)S(1)} copy(s32[512,512]{1,0:T(8,128)} %param.5) | data formatting | bytes 2097152 | tf_op args[0]
  3.0 0.2 divide_convert_fusion
  3.2 3.0 %collective-permute-start = (bf16[128,512]{1,0:T(8,128)(2,1)S(1)}, bf16[128,512]{1,0:T(8,128)(2,1)S(1)}, u32[]{:S(2)}, u32[]{:S(2)}) collective-permute-start(bf16[128,512]{1,0:T(8,128)(2,1)S(1)} %dynamic-slice_bitcast_fusion), channel_id=1, source_target_pairs={{0,4},{4,0},{1,5},{5,1},{2,6},{6,2},{3,7},{7,3},{8,12},{12,8},{9,1... | collective-permute-start | bytes 393224 | tf_op jit(solution)/shard_map/ppermute | solution.py:440
  6.2 0.0 copy-done.1
  6.2 0.0 copy-done
  6.3 0.1 collective-permute-start.4
  7.1 0.1 stack.124.places
  7.2 0.1 stack.132.facts
  7.3 3.2 %collective-permute-done = bf16[128,512]{1,0:T(8,128)(2,1)S(1)} collective-permute-done((bf16[128,512]{1,0:T(8,128)(2,1)S(1)}, bf16[128,512]{1,0:T(8,128)(2,1)S(1)}, u32[]{:S(2)}, u32[]{:S(2)}) %collective-permute-start) | collective-permute-done | bytes 131104 | tf_op jit(solution)/shard_map/ppermute | solution.py:440
  10.6 0.1 bitcast_select_fusion
  10.6 2.2 %collective-permute-start.1 = (bf16[128,512]{1,0:T(8,128)(2,1)S(1)}, bf16[128,512]{1,0:T(8,128)(2,1)S(1)}, u32[]{:S(2)}, u32[]{:S(2)}) collective-permute-start(bf16[128,512]{1,0:T(8,128)(2,1)S(1)} %get-tuple-element.32), channel_id=1, source_target_pairs={{0,8},{8,16},{16,24},{24,0},{1,9},{9,17},{17,25},{25,1},{2,10},{10... | collective-permute-start | bytes 393224 | tf_op jit(solution)/shard_map/ppermute | solution.py:446
  12.8 2.6 %collective-permute-start.2 = (bf16[128,512]{1,0:T(8,128)(2,1)S(1)}, bf16[128,512]{1,0:T(8,128)(2,1)S(1)}, u32[]{:S(2)}, u32[]{:S(2)}) collective-permute-start(bf16[128,512]{1,0:T(8,128)(2,1)S(1)} %get-tuple-element.32), channel_id=1, source_target_pairs={{0,16},{8,24},{16,0},{24,8},{1,17},{9,25},{17,1},{25,9},{2,18},{10... | collective-permute-start | bytes 393224 | tf_op jit(solution)/shard_map/ppermute | solution.py:446
  15.4 1.3 %collective-permute-start.3 = (bf16[128,512]{1,0:T(8,128)(2,1)S(1)}, bf16[128,512]{1,0:T(8,128)(2,1)S(1)}, u32[]{:S(2)}, u32[]{:S(2)}) collective-permute-start(bf16[128,512]{1,0:T(8,128)(2,1)S(1)} %get-tuple-element.32), channel_id=1, source_target_pairs={{0,24},{8,0},{16,8},{24,16},{1,25},{9,1},{17,9},{25,17},{2,26},{10... | collective-permute-start | bytes 393224 | tf_op jit(solution)/shard_map/ppermute | solution.py:446
  16.7 0.0 collective-permute-done.4
  16.8 2.5 %collective-permute-done.1 = bf16[128,512]{1,0:T(8,128)(2,1)S(1)} collective-permute-done((bf16[128,512]{1,0:T(8,128)(2,1)S(1)}, bf16[128,512]{1,0:T(8,128)(2,1)S(1)}, u32[]{:S(2)}, u32[]{:S(2)}) %collective-permute-start.1) | collective-permute-done | bytes 131104 | tf_op jit(solution)/shard_map/ppermute | solution.py:446
  19.3 3.3 %collective-permute-done.2 = bf16[128,512]{1,0:T(8,128)(2,1)S(1)} collective-permute-done((bf16[128,512]{1,0:T(8,128)(2,1)S(1)}, bf16[128,512]{1,0:T(8,128)(2,1)S(1)}, u32[]{:S(2)}, u32[]{:S(2)}) %collective-permute-start.2) | collective-permute-done | bytes 131104 | tf_op jit(solution)/shard_map/ppermute | solution.py:446
  22.6 0.0 collective-permute-done.3
  22.6 0.1 pad_maximum_fusion.refs_0_
  22.6 1.7 %collective-permute-start.6 = (bf16[4,128,512]{2,1,0:T(8,128)(2,1)S(1)}, bf16[4,128,512]{2,1,0:T(8,128)(2,1)S(1)}, u32[]{:S(2)}, u32[]{:S(2)}) collective-permute-start(bf16[4,128,512]{2,1,0:T(8,128)(2,1)S(1)} %pad_maximum_fusion.refs_0_), channel_id=1, source_target_pairs={{0,4},{4,0},{1,5},{5,1},{2,6},{6,2},{3,7},{7,3},{8,12},{12,8},{9,1... | collective-permute-start | bytes 1572872 | tf_op jit(solution)/shard_map/ppermute | solution.py:460
  24.3 1.5 %collective-permute-start.5 = (bf16[4,128,512]{2,1,0:T(8,128)(2,1)S(1)}, bf16[4,128,512]{2,1,0:T(8,128)(2,1)S(1)}, u32[]{:S(2)}, u32[]{:S(2)}) collective-permute-start(bf16[4,128,512]{2,1,0:T(8,128)(2,1)S(1)} %pad_maximum_fusion.refs_0_), channel_id=1, source_target_pairs={{0,2},{2,0},{1,3},{3,1},{4,6},{6,4},{5,7},{7,5},{8,10},{10,8},{9,1... | collective-permute-start | bytes 1572872 | tf_op jit(solution)/shard_map/ppermute | solution.py:460
  25.8 2.7 %collective-permute-start.14 = (bf16[128,512]{1,0:T(8,128)(2,1)S(1)}, bf16[128,512]{1,0:T(8,128)(2,1)S(1)}, u32[]{:S(2)}, u32[]{:S(2)}) collective-permute-start(bf16[128,512]{1,0:T(8,128)(2,1)S(1)} %get-tuple-element.22), channel_id=1, source_target_pairs={{0,8},{8,16},{16,24},{24,0},{1,9},{9,17},{17,25},{25,1},{2,10},{10... | collective-permute-start | bytes 393224 | tf_op jit(solution)/shard_map/ppermute | solution.py:446
  28.5 1.6 %collective-permute-start.15 = (bf16[128,512]{1,0:T(8,128)(2,1)S(1)}, bf16[128,512]{1,0:T(8,128)(2,1)S(1)}, u32[]{:S(2)}, u32[]{:S(2)}) collective-permute-start(bf16[128,512]{1,0:T(8,128)(2,1)S(1)} %get-tuple-element.22), channel_id=1, source_target_pairs={{0,16},{8,24},{16,0},{24,8},{1,17},{9,25},{17,1},{25,9},{2,18},{10... | collective-permute-start | bytes 393224 | tf_op jit(solution)/shard_map/ppermute | solution.py:446
  30.1 0.8 collective-permute-start.16
  30.8 4.7 %collective-permute-done.6.refs_2_ = bf16[4,128,512]{2,1,0:T(8,128)(2,1)S(1)} collective-permute-done((bf16[4,128,512]{2,1,0:T(8,128)(2,1)S(1)}, bf16[4,128,512]{2,1,0:T(8,128)(2,1)S(1)}, u32[]{:S(2)}, u32[]{:S(2)}) %collective-permute-start.6) | collective-permute-done | bytes 524320 | tf_op jit(solution)/shard_map/ppermute | solution.py:460
  35.5 1.3 %collective-permute-start.17 = (f32[64,512]{1,0:T(8,128)S(1)}, f32[64,512]{1,0:T(8,128)S(1)}, u32[]{:S(2)}, u32[]{:S(2)}) collective-permute-start(f32[64,512]{1,0:T(8,128)S(1)} %broadcast_select_fusion.refs_0_), channel_id=1, source_target_pairs={{0,2},{2,0},{1,3},{3,1},{4,6},{6,4},{5,7},{7,5},{8,10},{10,8},{9,1... | collective-permute-start | bytes 393224 | tf_op jit(solution)/shard_map/ppermute | solution.py:459
  36.8 0.1 collective-permute-done.5.refs_1_
  36.9 0.0 collective-permute-start.9
  37.0 0.0 collective-permute-done.14
  37.0 2.0 %collective-permute-start.7 = (bf16[2,128,512]{2,1,0:T(8,128)(2,1)S(1)}, bf16[2,128,512]{2,1,0:T(8,128)(2,1)S(1)}, u32[]{:S(2)}, u32[]{:S(2)}) collective-permute-start(bf16[2,128,512]{2,1,0:T(8,128)(2,1)S(1)} %slice.8), channel_id=1, source_target_pairs={{0,2},{2,0},{1,3},{3,1},{4,6},{6,4},{5,7},{7,5},{8,10},{10,8},{9,1... | collective-permute-start | bytes 786440 | tf_op jit(solution)/shard_map/ppermute | solution.py:461
  39.0 0.0 collective-permute-done.15
  39.0 0.1 collective-permute-start.8
  39.1 0.0 collective-permute-done.16
  39.1 0.2 collective-permute-start.10
  39.3 1.3 %collective-permute-done.17.refs_1_ = f32[64,512]{1,0:T(8,128)S(1)} collective-permute-done((f32[64,512]{1,0:T(8,128)S(1)}, f32[64,512]{1,0:T(8,128)S(1)}, u32[]{:S(2)}, u32[]{:S(2)}) %collective-permute-start.17) | collective-permute-done | bytes 131104 | tf_op jit(solution)/shard_map/ppermute | solution.py:459
  40.6 0.0 collective-permute-start.11
  40.6 5.5 %collective-permute-done.7.refs_3_ = bf16[2,128,512]{2,1,0:T(8,128)(2,1)S(1)} collective-permute-done((bf16[2,128,512]{2,1,0:T(8,128)(2,1)S(1)}, bf16[2,128,512]{2,1,0:T(8,128)(2,1)S(1)}, u32[]{:S(2)}, u32[]{:S(2)}) %collective-permute-start.7) | collective-permute-done | bytes 262176 | tf_op jit(solution)/shard_map/ppermute | solution.py:461
  46.1 0.0 collective-permute-start.12
  46.1 1.3 %collective-permute-done.8.refs_4_ = bf16[2,128,512]{2,1,0:T(8,128)(2,1)S(1)} collective-permute-done((bf16[2,128,512]{2,1,0:T(8,128)(2,1)S(1)}, bf16[2,128,512]{2,1,0:T(8,128)(2,1)S(1)}, u32[]{:S(2)}, u32[]{:S(2)}) %collective-permute-start.8) | collective-permute-done | bytes 262176 | tf_op jit(solution)/shard_map/ppermute | solution.py:462
  47.4 0.0 collective-permute-start.13
  47.4 0.1 pad_maximum_fusion.1.refs_2_
  47.5 0.0 collective-permute-done.9.refs_5_
  47.5 0.9 collective-permute-start.18
  48.4 0.0 collective-permute-done.12.refs_8_
  48.4 1.2 %collective-permute-start.19 = (bf16[4,128,512]{2,1,0:T(8,128)(2,1)S(1)}, bf16[4,128,512]{2,1,0:T(8,128)(2,1)S(1)}, u32[]{:S(2)}, u32[]{:S(2)}) collective-permute-start(bf16[4,128,512]{2,1,0:T(8,128)(2,1)S(1)} %pad_maximum_fusion.1.refs_2_), channel_id=1, source_target_pairs={{0,4},{4,0},{1,5},{5,1},{2,6},{6,2},{3,7},{7,3},{8,12},{12,8},{9,1... | collective-permute-start | bytes 1572872 | tf_op jit(solution)/shard_map/ppermute | solution.py:475
  49.6 0.0 collective-permute-done.13.refs_9_
  49.6 1.5 %collective-permute-start.20 = (bf16[4,128,512]{2,1,0:T(8,128)(2,1)S(1)}, bf16[4,128,512]{2,1,0:T(8,128)(2,1)S(1)}, u32[]{:S(2)}, u32[]{:S(2)}) collective-permute-start(bf16[4,128,512]{2,1,0:T(8,128)(2,1)S(1)} %pad_maximum_fusion.1.refs_2_), channel_id=1, source_target_pairs={{0,6},{2,4},{4,2},{6,0},{1,7},{3,5},{5,3},{7,1},{8,14},{10,12},{12... | collective-permute-start | bytes 1572872 | tf_op jit(solution)/shard_map/ppermute | solution.py:476
  51.1 0.0 collective-permute-done.10.refs_6_
  51.1 0.0 collective-permute-start.21
  51.1 0.0 collective-permute-done.11.refs_7_
  51.1 28.1 %shard_map.76 = (bf16[1024,1024]{1,0:T(8,128)(2,1)S(1)}, bf16[1024,1024]{1,0:T(8,128)(2,1)S(1)}, bf16[1024,2048]{1,0:T(8,128)(2,1)S(1)}) custom-call(s32[14]{0:T(128)S(1)} %stack.124.places, bf16[4,128,512]{2,1,0:T(8,128)(2,1)S(1)} %pad_maximum_fusion.refs_0_, bf16[4,128,512]{2,1,0:T(8,128)(2,1)S(1)} %collective-permute-done.5.refs_1_, ...), custom_call_target="tpu_custom_call" | custom-call | flops 40000000000 | bytes 20971520 | tf_op jit(solution)/shard_map/pallas_call | solution.py:227
  79.2 0.0 collective-permute-done.18.refs_3_
  79.2 0.0 collective-permute-done.19.refs_4_
  79.2 0.0 collective-permute-done.20.refs_5_
  79.2 0.6 collective-permute-start.22
  79.8 0.1 collective-permute-start.23
  79.8 0.4 collective-permute-start.24
  80.3 0.0 collective-permute-done.21.refs_6_
  80.3 1.0 %collective-permute-done.22.refs_7_ = bf16[4,128,512]{2,1,0:T(8,128)(2,1)S(1)} collective-permute-done((bf16[4,128,512]{2,1,0:T(8,128)(2,1)S(1)}, bf16[4,128,512]{2,1,0:T(8,128)(2,1)S(1)}, u32[]{:S(2)}, u32[]{:S(2)}) %collective-permute-start.22) | collective-permute-done | bytes 524320 | tf_op jit(solution)/shard_map/ppermute | solution.py:503
  81.3 0.7 collective-permute-done.23.refs_8_
  82.0 0.7 collective-permute-done.24.refs_9_
  82.8 18.9 %shard_map.77 = (f32[512,1024]{1,0:T(8,128)}, f32[64,1024]{1,0:T(8,128)}, f32[64,512]{1,0:T(8,128)}) custom-call(s32[17]{0:T(128)S(1)} %stack.132.facts, bf16[1024,2048]{1,0:T(8,128)(2,1)S(1)} %get-tuple-element.20.panel_ref, bf16[1024,1024]{1,0:T(8,128)(2,1)S(1)} %get-tuple-element.25.high_ref, bf16[1024,1024]{1,0:T(8,128)(2,1)S(1)} %get-tuple-element.26.low_ref, ...), custom_call_target="tpu_custom_call" | custom-call | flops 20000000000 | bytes 20971520 | tf_op jit(solution)/shard_map/pallas_call | solution.py:391
  (6 shorter events, 0.1 us)
Async XLA Ops:
  0.6 5.6 %copy-start.1 = (s32[512]{0:T(512)S(1)}, s32[512]{0:T(512)}, u32[]{:S(2)}) copy-start(s32[512]{0:T(512)} %param.8) | copy-start | bytes 6148
  0.6 5.6 %copy-start = (f32[64,512]{1,0:T(8,128)S(1)}, f32[64,512]{1,0:T(8,128)}, u32[]{:S(2)}) copy-start(f32[64,512]{1,0:T(8,128)} %param.7) | copy-start | bytes 393220
  3.2 7.4 %collective-permute-start = (bf16[128,512]{1,0:T(8,128)(2,1)S(1)}, bf16[128,512]{1,0:T(8,128)(2,1)S(1)}, u32[]{:S(2)}, u32[]{:S(2)}) collective-permute-start(bf16[128,512]{1,0:T(8,128)(2,1)S(1)} %dynamic-slice_bitcast_fusion), channel_id=1, source_target_pairs={{0,4},{4,0},{1,5},{5,1},{2,6},{6,2},{3,7},{7,3},{8,12},{12,8},{9,1... | collective-permute-start | bytes 393224 | tf_op jit(solution)/shard_map/ppermute | solution.py:440
  6.3 10.5 %collective-permute-start.4 = (f32[64,512]{1,0:T(8,128)S(1)}, f32[64,512]{1,0:T(8,128)S(1)}, u32[]{:S(2)}, u32[]{:S(2)}) collective-permute-start(f32[64,512]{1,0:T(8,128)S(1)} %broadcast_multiply_fusion.own_ref), channel_id=1, source_target_pairs={{0,4},{4,0},{1,5},{5,1},{2,6},{6,2},{3,7},{7,3},{8,12},{12,8},{9,1... | collective-permute-start | bytes 393224 | tf_op jit(solution)/shard_map/ppermute | solution.py:449
  10.6 8.6 %collective-permute-start.1 = (bf16[128,512]{1,0:T(8,128)(2,1)S(1)}, bf16[128,512]{1,0:T(8,128)(2,1)S(1)}, u32[]{:S(2)}, u32[]{:S(2)}) collective-permute-start(bf16[128,512]{1,0:T(8,128)(2,1)S(1)} %get-tuple-element.32), channel_id=1, source_target_pairs={{0,8},{8,16},{16,24},{24,0},{1,9},{9,17},{17,25},{25,1},{2,10},{10... | collective-permute-start | bytes 393224 | tf_op jit(solution)/shard_map/ppermute | solution.py:446
  12.8 9.8 %collective-permute-start.2 = (bf16[128,512]{1,0:T(8,128)(2,1)S(1)}, bf16[128,512]{1,0:T(8,128)(2,1)S(1)}, u32[]{:S(2)}, u32[]{:S(2)}) collective-permute-start(bf16[128,512]{1,0:T(8,128)(2,1)S(1)} %get-tuple-element.32), channel_id=1, source_target_pairs={{0,16},{8,24},{16,0},{24,8},{1,17},{9,25},{17,1},{25,9},{2,18},{10... | collective-permute-start | bytes 393224 | tf_op jit(solution)/shard_map/ppermute | solution.py:446
  15.4 7.2 %collective-permute-start.3 = (bf16[128,512]{1,0:T(8,128)(2,1)S(1)}, bf16[128,512]{1,0:T(8,128)(2,1)S(1)}, u32[]{:S(2)}, u32[]{:S(2)}) collective-permute-start(bf16[128,512]{1,0:T(8,128)(2,1)S(1)} %get-tuple-element.32), channel_id=1, source_target_pairs={{0,24},{8,0},{16,8},{24,16},{1,25},{9,1},{17,9},{25,17},{2,26},{10... | collective-permute-start | bytes 393224 | tf_op jit(solution)/shard_map/ppermute | solution.py:446
  22.6 12.9 %collective-permute-start.6 = (bf16[4,128,512]{2,1,0:T(8,128)(2,1)S(1)}, bf16[4,128,512]{2,1,0:T(8,128)(2,1)S(1)}, u32[]{:S(2)}, u32[]{:S(2)}) collective-permute-start(bf16[4,128,512]{2,1,0:T(8,128)(2,1)S(1)} %pad_maximum_fusion.refs_0_), channel_id=1, source_target_pairs={{0,4},{4,0},{1,5},{5,1},{2,6},{6,2},{3,7},{7,3},{8,12},{12,8},{9,1... | collective-permute-start | bytes 1572872 | tf_op jit(solution)/shard_map/ppermute | solution.py:460
  24.3 12.6 %collective-permute-start.5 = (bf16[4,128,512]{2,1,0:T(8,128)(2,1)S(1)}, bf16[4,128,512]{2,1,0:T(8,128)(2,1)S(1)}, u32[]{:S(2)}, u32[]{:S(2)}) collective-permute-start(bf16[4,128,512]{2,1,0:T(8,128)(2,1)S(1)} %pad_maximum_fusion.refs_0_), channel_id=1, source_target_pairs={{0,2},{2,0},{1,3},{3,1},{4,6},{6,4},{5,7},{7,5},{8,10},{10,8},{9,1... | collective-permute-start | bytes 1572872 | tf_op jit(solution)/shard_map/ppermute | solution.py:460
  25.8 11.1 %collective-permute-start.14 = (bf16[128,512]{1,0:T(8,128)(2,1)S(1)}, bf16[128,512]{1,0:T(8,128)(2,1)S(1)}, u32[]{:S(2)}, u32[]{:S(2)}) collective-permute-start(bf16[128,512]{1,0:T(8,128)(2,1)S(1)} %get-tuple-element.22), channel_id=1, source_target_pairs={{0,8},{8,16},{16,24},{24,0},{1,9},{9,17},{17,25},{25,1},{2,10},{10... | collective-permute-start | bytes 393224 | tf_op jit(solution)/shard_map/ppermute | solution.py:446
  28.5 10.5 %collective-permute-start.15 = (bf16[128,512]{1,0:T(8,128)(2,1)S(1)}, bf16[128,512]{1,0:T(8,128)(2,1)S(1)}, u32[]{:S(2)}, u32[]{:S(2)}) collective-permute-start(bf16[128,512]{1,0:T(8,128)(2,1)S(1)} %get-tuple-element.22), channel_id=1, source_target_pairs={{0,16},{8,24},{16,0},{24,8},{1,17},{9,25},{17,1},{25,9},{2,18},{10... | collective-permute-start | bytes 393224 | tf_op jit(solution)/shard_map/ppermute | solution.py:446
  30.1 9.0 %collective-permute-start.16 = (bf16[128,512]{1,0:T(8,128)(2,1)S(1)}, bf16[128,512]{1,0:T(8,128)(2,1)S(1)}, u32[]{:S(2)}, u32[]{:S(2)}) collective-permute-start(bf16[128,512]{1,0:T(8,128)(2,1)S(1)} %get-tuple-element.22), channel_id=1, source_target_pairs={{0,24},{8,0},{16,8},{24,16},{1,25},{9,1},{17,9},{25,17},{2,26},{10... | collective-permute-start | bytes 393224 | tf_op jit(solution)/shard_map/ppermute | solution.py:446
  35.5 5.1 %collective-permute-start.17 = (f32[64,512]{1,0:T(8,128)S(1)}, f32[64,512]{1,0:T(8,128)S(1)}, u32[]{:S(2)}, u32[]{:S(2)}) collective-permute-start(f32[64,512]{1,0:T(8,128)S(1)} %broadcast_select_fusion.refs_0_), channel_id=1, source_target_pairs={{0,2},{2,0},{1,3},{3,1},{4,6},{6,4},{5,7},{7,5},{8,10},{10,8},{9,1... | collective-permute-start | bytes 393224 | tf_op jit(solution)/shard_map/ppermute | solution.py:459
  36.9 10.6 %collective-permute-start.9 = (bf16[4,128,512]{2,1,0:T(8,128)(2,1)S(1)}, bf16[4,128,512]{2,1,0:T(8,128)(2,1)S(1)}, u32[]{:S(2)}, u32[]{:S(2)}) collective-permute-start(bf16[4,128,512]{2,1,0:T(8,128)(2,1)S(1)} %pad_maximum_fusion.refs_0_), channel_id=1, source_target_pairs={{0,1},{1,0},{2,3},{3,2},{4,5},{5,4},{6,7},{7,6},{8,9},{9,8},{10,11... | collective-permute-start | bytes 1572872 | tf_op jit(solution)/shard_map/ppermute | solution.py:464
  37.0 9.1 %collective-permute-start.7 = (bf16[2,128,512]{2,1,0:T(8,128)(2,1)S(1)}, bf16[2,128,512]{2,1,0:T(8,128)(2,1)S(1)}, u32[]{:S(2)}, u32[]{:S(2)}) collective-permute-start(bf16[2,128,512]{2,1,0:T(8,128)(2,1)S(1)} %slice.8), channel_id=1, source_target_pairs={{0,2},{2,0},{1,3},{3,1},{4,6},{6,4},{5,7},{7,5},{8,10},{10,8},{9,1... | collective-permute-start | bytes 786440 | tf_op jit(solution)/shard_map/ppermute | solution.py:461
  39.0 8.4 %collective-permute-start.8 = (bf16[2,128,512]{2,1,0:T(8,128)(2,1)S(1)}, bf16[2,128,512]{2,1,0:T(8,128)(2,1)S(1)}, u32[]{:S(2)}, u32[]{:S(2)}) collective-permute-start(bf16[2,128,512]{2,1,0:T(8,128)(2,1)S(1)} %slice.9), channel_id=1, source_target_pairs={{0,4},{4,0},{1,5},{5,1},{2,6},{6,2},{3,7},{7,3},{8,12},{12,8},{9,1... | collective-permute-start | bytes 786440 | tf_op jit(solution)/shard_map/ppermute | solution.py:462
  39.1 12.0 %collective-permute-start.10 = (bf16[4,128,512]{2,1,0:T(8,128)(2,1)S(1)}, bf16[4,128,512]{2,1,0:T(8,128)(2,1)S(1)}, u32[]{:S(2)}, u32[]{:S(2)}) collective-permute-start(bf16[4,128,512]{2,1,0:T(8,128)(2,1)S(1)} %collective-permute-done.5.refs_1_), channel_id=1, source_target_pairs={{0,1},{1,0},{2,3},{3,2},{4,5},{5,4},{6,7},{7,6},{8,9},{9,8},{10,11... | collective-permute-start | bytes 1572872 | tf_op jit(solution)/shard_map/ppermute | solution.py:464
  40.6 10.5 %collective-permute-start.11 = (bf16[4,128,512]{2,1,0:T(8,128)(2,1)S(1)}, bf16[4,128,512]{2,1,0:T(8,128)(2,1)S(1)}, u32[]{:S(2)}, u32[]{:S(2)}) collective-permute-start(bf16[4,128,512]{2,1,0:T(8,128)(2,1)S(1)} %collective-permute-done.6.refs_2_), channel_id=1, source_target_pairs={{0,1},{1,0},{2,3},{3,2},{4,5},{5,4},{6,7},{7,6},{8,9},{9,8},{10,11... | collective-permute-start | bytes 1572872 | tf_op jit(solution)/shard_map/ppermute | solution.py:464
  46.1 2.3 %collective-permute-start.12 = (bf16[2,128,512]{2,1,0:T(8,128)(2,1)S(1)}, bf16[2,128,512]{2,1,0:T(8,128)(2,1)S(1)}, u32[]{:S(2)}, u32[]{:S(2)}) collective-permute-start(bf16[2,128,512]{2,1,0:T(8,128)(2,1)S(1)} %collective-permute-done.7.refs_3_), channel_id=1, source_target_pairs={{0,1},{1,0},{2,3},{3,2},{4,5},{5,4},{6,7},{7,6},{8,9},{9,8},{10,11... | collective-permute-start | bytes 786440 | tf_op jit(solution)/shard_map/ppermute | solution.py:464
  47.4 2.2 %collective-permute-start.13 = (bf16[2,128,512]{2,1,0:T(8,128)(2,1)S(1)}, bf16[2,128,512]{2,1,0:T(8,128)(2,1)S(1)}, u32[]{:S(2)}, u32[]{:S(2)}) collective-permute-start(bf16[2,128,512]{2,1,0:T(8,128)(2,1)S(1)} %collective-permute-done.8.refs_4_), channel_id=1, source_target_pairs={{0,1},{1,0},{2,3},{3,2},{4,5},{5,4},{6,7},{7,6},{8,9},{9,8},{10,11... | collective-permute-start | bytes 786440 | tf_op jit(solution)/shard_map/ppermute | solution.py:464
  47.5 31.6 %collective-permute-start.18 = (bf16[4,128,512]{2,1,0:T(8,128)(2,1)S(1)}, bf16[4,128,512]{2,1,0:T(8,128)(2,1)S(1)}, u32[]{:S(2)}, u32[]{:S(2)}) collective-permute-start(bf16[4,128,512]{2,1,0:T(8,128)(2,1)S(1)} %pad_maximum_fusion.1.refs_2_), channel_id=1, source_target_pairs={{0,2},{2,0},{1,3},{3,1},{4,6},{6,4},{5,7},{7,5},{8,10},{10,8},{9,1... | collective-permute-start | bytes 1572872 | tf_op jit(solution)/shard_map/ppermute | solution.py:474
  48.4 30.8 %collective-permute-start.19 = (bf16[4,128,512]{2,1,0:T(8,128)(2,1)S(1)}, bf16[4,128,512]{2,1,0:T(8,128)(2,1)S(1)}, u32[]{:S(2)}, u32[]{:S(2)}) collective-permute-start(bf16[4,128,512]{2,1,0:T(8,128)(2,1)S(1)} %pad_maximum_fusion.1.refs_2_), channel_id=1, source_target_pairs={{0,4},{4,0},{1,5},{5,1},{2,6},{6,2},{3,7},{7,3},{8,12},{12,8},{9,1... | collective-permute-start | bytes 1572872 | tf_op jit(solution)/shard_map/ppermute | solution.py:475
  49.6 29.6 %collective-permute-start.20 = (bf16[4,128,512]{2,1,0:T(8,128)(2,1)S(1)}, bf16[4,128,512]{2,1,0:T(8,128)(2,1)S(1)}, u32[]{:S(2)}, u32[]{:S(2)}) collective-permute-start(bf16[4,128,512]{2,1,0:T(8,128)(2,1)S(1)} %pad_maximum_fusion.1.refs_2_), channel_id=1, source_target_pairs={{0,6},{2,4},{4,2},{6,0},{1,7},{3,5},{5,3},{7,1},{8,14},{10,12},{12... | collective-permute-start | bytes 1572872 | tf_op jit(solution)/shard_map/ppermute | solution.py:476
  51.1 29.2 %collective-permute-start.21 = (bf16[4,128,512]{2,1,0:T(8,128)(2,1)S(1)}, bf16[4,128,512]{2,1,0:T(8,128)(2,1)S(1)}, u32[]{:S(2)}, u32[]{:S(2)}) collective-permute-start(bf16[4,128,512]{2,1,0:T(8,128)(2,1)S(1)} %pad_maximum_fusion.1.refs_2_), channel_id=1, source_target_pairs={{0,1},{1,0},{2,3},{3,2},{4,5},{5,4},{6,7},{7,6},{8,9},{9,8},{10,11... | collective-permute-start | bytes 1572872 | tf_op jit(solution)/shard_map/ppermute | solution.py:478
  79.2 2.1 %collective-permute-start.22 = (bf16[4,128,512]{2,1,0:T(8,128)(2,1)S(1)}, bf16[4,128,512]{2,1,0:T(8,128)(2,1)S(1)}, u32[]{:S(2)}, u32[]{:S(2)}) collective-permute-start(bf16[4,128,512]{2,1,0:T(8,128)(2,1)S(1)} %collective-permute-done.18.refs_3_), channel_id=1, source_target_pairs={{0,1},{1,0},{2,3},{3,2},{4,5},{5,4},{6,7},{7,6},{8,9},{9,8},{10,11... | collective-permute-start | bytes 1572872 | tf_op jit(solution)/shard_map/ppermute | solution.py:503
  79.8 2.3 %collective-permute-start.23 = (bf16[4,128,512]{2,1,0:T(8,128)(2,1)S(1)}, bf16[4,128,512]{2,1,0:T(8,128)(2,1)S(1)}, u32[]{:S(2)}, u32[]{:S(2)}) collective-permute-start(bf16[4,128,512]{2,1,0:T(8,128)(2,1)S(1)} %collective-permute-done.19.refs_4_), channel_id=1, source_target_pairs={{0,1},{1,0},{2,3},{3,2},{4,5},{5,4},{6,7},{7,6},{8,9},{9,8},{10,11... | collective-permute-start | bytes 1572872 | tf_op jit(solution)/shard_map/ppermute | solution.py:503
  79.8 3.0 %collective-permute-start.24 = (bf16[4,128,512]{2,1,0:T(8,128)(2,1)S(1)}, bf16[4,128,512]{2,1,0:T(8,128)(2,1)S(1)}, u32[]{:S(2)}, u32[]{:S(2)}) collective-permute-start(bf16[4,128,512]{2,1,0:T(8,128)(2,1)S(1)} %collective-permute-done.20.refs_5_), channel_id=1, source_target_pairs={{0,1},{1,0},{2,3},{3,2},{4,5},{5,4},{6,7},{7,6},{8,9},{9,8},{10,11... | collective-permute-start | bytes 1572872 | tf_op jit(solution)/shard_map/ppermute | solution.py:503

commit v3 on v2

--- a/solution.py
+++ b/solution.py
@@ -418,6 +418,11 @@
     return jnp.stack([jnp.asarray(v).astype(jnp.int32) for v in values])
 
 
+def standardized(genotypes, frequencies):
+    spread = jnp.sqrt(2.0 * frequencies * (1.0 - frequencies))
+    return ((genotypes.astype(F32) - 2.0 * frequencies) / spread).astype(BF16).T
+
+
 def on_device(genotypes, frequencies, trait_scores, typed_mask, panel_index):
     n_samp, n_pan, n_mem, n_col = (lax.axis_size(a) for a in ("samp", "pan", "mem", "col"))
     samp, pan, mem, col = (lax.axis_index(a) for a in ("samp", "pan", "mem", "col"))
@@ -425,8 +430,6 @@
     width = local_rows * n_mem
     samples_all = depth * n_samp
     q = panel_index[0] % n_col
-    spread = jnp.sqrt(2.0 * frequencies * (1.0 - frequencies))
-    standard = ((genotypes.astype(F32) - 2.0 * frequencies) / spread).astype(BF16).T
     masked = trait_scores * typed_mask.astype(F32)
     own_panel = pan == q
     rest = []
@@ -435,7 +438,10 @@
         quarter = local_rows // 4
 
         def part(i, j):
-            return lax.dynamic_slice_in_dim(standard, (2 * i + j) * quarter, quarter, 0)
+            at = (2 * i + j) * quarter
+            return standardized(
+                lax.dynamic_slice_in_dim(genotypes, at, quarter, 1), lax.dynamic_slice_in_dim(frequencies, at, quarter, 0)
+            )
 
         mine, other = part(pan, col), lax.ppermute(part(1 - pan, col), "pan", swap)
         piece = jnp.where(own_panel, mine, other)
@@ -481,6 +487,7 @@
         extra, n_places = [], 8
         panel_scores = [panel_masked, beside]
     else:
+        standard = standardized(genotypes, frequencies)
         chosen = lax.psum(jnp.where(own_panel, standard, jnp.zeros_like(standard)), "pan")
         gathered = lax.all_gather(chosen, ("samp", "mem")).reshape(n_samp, width, depth)
         pieces, plan = [gathered], [tuple(range(n_samp))]

time: 103 us -> 103 us (level)
  waiting for transfers between devices: 24.5 us -> 22.8 us
    unnamed x5 -> x4, local copies, waits for them, and re-layouts: 1.57 us -> 0.26 us
    ppermute x1, waiting for transfers between devices: 1.32 us -> 0.08 us  [on_device(): far_b = lax.ppermute(by_mem[2:], 'pan', swap)]
    ppermute x1, starting transfers between devices: 2.01 us -> 0.78 us  [on_device(): far_a = lax.ppermute(by_pan[:2], 'mem', swap)]
    ppermute x1, waiting for transfers between devices: 3.22 us -> 2.09 us  [on_device(): lax.ppermute(part(1 - pan, col), 'pan', swap)]
    dynamic_slice x1, local copies, waits for them, and re-layouts: 0.02 us -> 1.07 us  [part(): lax.dynamic_slice_in_dim(genotypes, at, quarter, 1)]
    ppermute x1, starting transfers between devices: 0.11 us -> 1.15 us  [on_device(): far_b = lax.ppermute(by_mem[2:], 'pan', swap)]
  transfers between devices with their start and end apart: 25 -> 25, of which waited for: 11 -> 10; matrix products, arithmetic and copies ran while one was open for 0% -> 1% of each run, Pallas kernels for 28% -> 28%
where the time goes in v3:
time: 103 us; the launch traced here: 101 us
  Pallas kernels  47 us (46%)
  starting transfers between devices  26.3 us (26%)
  waiting for transfers between devices  22.8 us (22%)
  other arithmetic  1.95 us (2%)
  between operations  1.8 us (2%)
  local copies, waits for them, and re-layouts  1.56 us (2%)
    pallas_call x1, Pallas kernels, panel_step(): pl.pallas_call(functools.partial(panel_kernel, plan, samples_all), out_sh...  28.1 us
    pallas_call x1, Pallas kernels, tile_step(): pl.pallas_call(functools.partial(tile_kernel, samples_all, n_places, len(...  18.9 us
    ppermute x6, starting transfers between devices, along_samp(): return [lax.ppermute(v, 'samp', pairs) for pairs in steps]  11.1 us
    ppermute x6, waiting for transfers between devices, along_samp(): return [lax.ppermute(v, 'samp', pairs) for pairs in steps]  5.8 us
    ppermute x1, waiting for transfers between devices, on_device(): far_a = lax.ppermute(by_pan[:2], 'mem', swap)  5.26 us
    ppermute x1, waiting for transfers between devices, on_device(): lax.ppermute(own, 'pan', swap)  5.09 us
    ppermute x1, starting transfers between devices, on_device(): lax.ppermute(part(1 - pan, col), 'pan', swap)  3.03 us
    ppermute x3, waiting for transfers between devices, on_device(): lax.ppermute(v, 'col', swap)  2.52 us
  transfers between devices with their start and end apart: 25, of which 10 were waited for; matrix products, arithmetic and copies ran while one was open for 1% of the time, Pallas kernels for 28%

profile of v3, /device:TPU:0, one launch (start us, length us, event | category | flops | bytes accessed | tf_op | source)
XLA Modules:
  0.0 101.4 jit_solution(189158895273187971)
XLA Ops:
  0.6 0.0 copy-start
  0.7 0.8 broadcast_multiply_fusion.2
  1.5 1.1 %constant_dynamic-slice_fusion.1 = (s32[512,128]{1,0:T(8,128)S(1)}, s32[512,128]{1,0:T(8,128)S(1)}) fusion(s32[512,512]{1,0:T(8,128)} %param.5, s32[]{:T(128)S(6)} %select_n.53, s32[]{:T(128)S(6)} %select_n.54), kind=kLoop, calls=%fused_computation.12 | loop fusion | bytes 1048584 | tf_op jit(solution)/shard_map/dynamic_slice | solution.py:443
  2.6 0.1 copy.11
  2.7 0.1 fusion
  2.8 3.0 %collective-permute-start = (bf16[128,512]{1,0:T(8,128)(2,1)S(1)}, bf16[128,512]{1,0:T(8,128)(2,1)S(1)}, u32[]{:S(2)}, u32[]{:S(2)}) collective-permute-start(bf16[128,512]{1,0:T(8,128)(2,1)S(1)} %fusion), channel_id=1, source_target_pairs={{0,4},{4,0},{1,5},{5,1},{2,6},{6,2},{3,7},{7,3},{8,12},{12,8},{9,1... | collective-permute-start | bytes 393224 | tf_op jit(solution)/shard_map/ppermute | solution.py:446
  5.9 0.7 convert_element_type.21
  6.6 0.1 collective-permute-start.4
  7.4 0.1 copy.10
  7.6 0.1 stack.124.places
  7.7 0.1 stack.132.facts
  7.8 2.1 %collective-permute-done = bf16[128,512]{1,0:T(8,128)(2,1)S(1)} collective-permute-done((bf16[128,512]{1,0:T(8,128)(2,1)S(1)}, bf16[128,512]{1,0:T(8,128)(2,1)S(1)}, u32[]{:S(2)}, u32[]{:S(2)}) %collective-permute-start) | collective-permute-done | bytes 131104 | tf_op jit(solution)/shard_map/ppermute | solution.py:446
  9.9 0.1 bitcast_select_fusion
  10.0 2.1 %collective-permute-start.1 = (bf16[128,512]{1,0:T(8,128)(2,1)S(1)}, bf16[128,512]{1,0:T(8,128)(2,1)S(1)}, u32[]{:S(2)}, u32[]{:S(2)}) collective-permute-start(bf16[128,512]{1,0:T(8,128)(2,1)S(1)} %bitcast_select_fusion.1), channel_id=1, source_target_pairs={{0,8},{8,16},{16,24},{24,0},{1,9},{9,17},{17,25},{25,1},{2,10},{10... | collective-permute-start | bytes 393224 | tf_op jit(solution)/shard_map/ppermute | solution.py:452
  12.2 2.6 %collective-permute-start.2 = (bf16[128,512]{1,0:T(8,128)(2,1)S(1)}, bf16[128,512]{1,0:T(8,128)(2,1)S(1)}, u32[]{:S(2)}, u32[]{:S(2)}) collective-permute-start(bf16[128,512]{1,0:T(8,128)(2,1)S(1)} %bitcast_select_fusion.1), channel_id=1, source_target_pairs={{0,16},{8,24},{16,0},{24,8},{1,17},{9,25},{17,1},{25,9},{2,18},{10... | collective-permute-start | bytes 393224 | tf_op jit(solution)/shard_map/ppermute | solution.py:452
  14.8 1.3 %collective-permute-start.3 = (bf16[128,512]{1,0:T(8,128)(2,1)S(1)}, bf16[128,512]{1,0:T(8,128)(2,1)S(1)}, u32[]{:S(2)}, u32[]{:S(2)}) collective-permute-start(bf16[128,512]{1,0:T(8,128)(2,1)S(1)} %bitcast_select_fusion.1), channel_id=1, source_target_pairs={{0,24},{8,0},{16,8},{24,16},{1,25},{9,1},{17,9},{25,17},{2,26},{10... | collective-permute-start | bytes 393224 | tf_op jit(solution)/shard_map/ppermute | solution.py:452
  16.1 0.0 collective-permute-done.4
  16.2 2.5 %collective-permute-done.1 = bf16[128,512]{1,0:T(8,128)(2,1)S(1)} collective-permute-done((bf16[128,512]{1,0:T(8,128)(2,1)S(1)}, bf16[128,512]{1,0:T(8,128)(2,1)S(1)}, u32[]{:S(2)}, u32[]{:S(2)}) %collective-permute-start.1) | collective-permute-done | bytes 131104 | tf_op jit(solution)/shard_map/ppermute | solution.py:452
  18.7 3.3 %collective-permute-done.2 = bf16[128,512]{1,0:T(8,128)(2,1)S(1)} collective-permute-done((bf16[128,512]{1,0:T(8,128)(2,1)S(1)}, bf16[128,512]{1,0:T(8,128)(2,1)S(1)}, u32[]{:S(2)}, u32[]{:S(2)}) %collective-permute-start.2) | collective-permute-done | bytes 131104 | tf_op jit(solution)/shard_map/ppermute | solution.py:452
  21.9 0.0 collective-permute-done.3
  21.9 0.1 pad_maximum_fusion.refs_0_
  22.0 2.0 %collective-permute-start.6 = (bf16[4,128,512]{2,1,0:T(8,128)(2,1)S(1)}, bf16[4,128,512]{2,1,0:T(8,128)(2,1)S(1)}, u32[]{:S(2)}, u32[]{:S(2)}) collective-permute-start(bf16[4,128,512]{2,1,0:T(8,128)(2,1)S(1)} %pad_maximum_fusion.refs_0_), channel_id=1, source_target_pairs={{0,4},{4,0},{1,5},{5,1},{2,6},{6,2},{3,7},{7,3},{8,12},{12,8},{9,1... | collective-permute-start | bytes 1572872 | tf_op jit(solution)/shard_map/ppermute | solution.py:466
  24.1 1.5 %collective-permute-start.5 = (bf16[4,128,512]{2,1,0:T(8,128)(2,1)S(1)}, bf16[4,128,512]{2,1,0:T(8,128)(2,1)S(1)}, u32[]{:S(2)}, u32[]{:S(2)}) collective-permute-start(bf16[4,128,512]{2,1,0:T(8,128)(2,1)S(1)} %pad_maximum_fusion.refs_0_), channel_id=1, source_target_pairs={{0,2},{2,0},{1,3},{3,1},{4,6},{6,4},{5,7},{7,5},{8,10},{10,8},{9,1... | collective-permute-start | bytes 1572872 | tf_op jit(solution)/shard_map/ppermute | solution.py:466
  25.5 2.7 %collective-permute-start.14 = (bf16[128,512]{1,0:T(8,128)(2,1)S(1)}, bf16[128,512]{1,0:T(8,128)(2,1)S(1)}, u32[]{:S(2)}, u32[]{:S(2)}) collective-permute-start(bf16[128,512]{1,0:T(8,128)(2,1)S(1)} %get-tuple-element.22), channel_id=1, source_target_pairs={{0,8},{8,16},{16,24},{24,0},{1,9},{9,17},{17,25},{25,1},{2,10},{10... | collective-permute-start | bytes 393224 | tf_op jit(solution)/shard_map/ppermute | solution.py:452
  28.2 1.6 %collective-permute-start.15 = (bf16[128,512]{1,0:T(8,128)(2,1)S(1)}, bf16[128,512]{1,0:T(8,128)(2,1)S(1)}, u32[]{:S(2)}, u32[]{:S(2)}) collective-permute-start(bf16[128,512]{1,0:T(8,128)(2,1)S(1)} %get-tuple-element.22), channel_id=1, source_target_pairs={{0,16},{8,24},{16,0},{24,8},{1,17},{9,25},{17,1},{25,9},{2,18},{10... | collective-permute-start | bytes 393224 | tf_op jit(solution)/shard_map/ppermute | solution.py:452
  29.8 0.8 collective-permute-start.16
  30.6 5.1 %collective-permute-done.6.refs_2_ = bf16[4,128,512]{2,1,0:T(8,128)(2,1)S(1)} collective-permute-done((bf16[4,128,512]{2,1,0:T(8,128)(2,1)S(1)}, bf16[4,128,512]{2,1,0:T(8,128)(2,1)S(1)}, u32[]{:S(2)}, u32[]{:S(2)}) %collective-permute-start.6) | collective-permute-done | bytes 524320 | tf_op jit(solution)/shard_map/ppermute | solution.py:466
  35.7 1.3 %collective-permute-start.17 = (f32[64,512]{1,0:T(8,128)S(1)}, f32[64,512]{1,0:T(8,128)S(1)}, u32[]{:S(2)}, u32[]{:S(2)}) collective-permute-start(f32[64,512]{1,0:T(8,128)S(1)} %broadcast_select_fusion.refs_0_), channel_id=1, source_target_pairs={{0,2},{2,0},{1,3},{3,1},{4,6},{6,4},{5,7},{7,5},{8,10},{10,8},{9,1... | collective-permute-start | bytes 393224 | tf_op jit(solution)/shard_map/ppermute | solution.py:465
  37.0 0.0 collective-permute-done.5.refs_1_
  37.0 0.1 collective-permute-start.9
  37.1 0.0 collective-permute-done.14
  37.1 0.8 collective-permute-start.7
  37.9 0.0 collective-permute-done.15
  37.9 1.2 %collective-permute-start.8 = (bf16[2,128,512]{2,1,0:T(8,128)(2,1)S(1)}, bf16[2,128,512]{2,1,0:T(8,128)(2,1)S(1)}, u32[]{:S(2)}, u32[]{:S(2)}) collective-permute-start(bf16[2,128,512]{2,1,0:T(8,128)(2,1)S(1)} %slice.9), channel_id=1, source_target_pairs={{0,4},{4,0},{1,5},{5,1},{2,6},{6,2},{3,7},{7,3},{8,12},{12,8},{9,1... | collective-permute-start | bytes 786440 | tf_op jit(solution)/shard_map/ppermute | solution.py:468
  39.1 0.0 collective-permute-done.16
  39.1 0.0 collective-permute-start.10
  39.1 1.9 %collective-permute-done.17.refs_1_ = f32[64,512]{1,0:T(8,128)S(1)} collective-permute-done((f32[64,512]{1,0:T(8,128)S(1)}, f32[64,512]{1,0:T(8,128)S(1)}, u32[]{:S(2)}, u32[]{:S(2)}) %collective-permute-start.17) | collective-permute-done | bytes 131104 | tf_op jit(solution)/shard_map/ppermute | solution.py:465
  41.0 0.0 collective-permute-start.11
  41.0 5.3 %collective-permute-done.7.refs_3_ = bf16[2,128,512]{2,1,0:T(8,128)(2,1)S(1)} collective-permute-done((bf16[2,128,512]{2,1,0:T(8,128)(2,1)S(1)}, bf16[2,128,512]{2,1,0:T(8,128)(2,1)S(1)}, u32[]{:S(2)}, u32[]{:S(2)}) %collective-permute-start.7) | collective-permute-done | bytes 262176 | tf_op jit(solution)/shard_map/ppermute | solution.py:467
  46.2 0.0 collective-permute-start.12
  46.3 0.1 collective-permute-done.8.refs_4_
  46.3 0.4 collective-permute-start.13
  46.8 0.1 pad_maximum_fusion.1.refs_2_
  46.8 0.0 collective-permute-done.9.refs_5_
  46.8 1.4 %collective-permute-start.18 = (bf16[4,128,512]{2,1,0:T(8,128)(2,1)S(1)}, bf16[4,128,512]{2,1,0:T(8,128)(2,1)S(1)}, u32[]{:S(2)}, u32[]{:S(2)}) collective-permute-start(bf16[4,128,512]{2,1,0:T(8,128)(2,1)S(1)} %pad_maximum_fusion.1.refs_2_), channel_id=1, source_target_pairs={{0,2},{2,0},{1,3},{3,1},{4,6},{6,4},{5,7},{7,5},{8,10},{10,8},{9,1... | collective-permute-start | bytes 1572872 | tf_op jit(solution)/shard_map/ppermute | solution.py:480
  48.2 0.0 collective-permute-done.12.refs_8_
  48.2 1.1 %collective-permute-start.19 = (bf16[4,128,512]{2,1,0:T(8,128)(2,1)S(1)}, bf16[4,128,512]{2,1,0:T(8,128)(2,1)S(1)}, u32[]{:S(2)}, u32[]{:S(2)}) collective-permute-start(bf16[4,128,512]{2,1,0:T(8,128)(2,1)S(1)} %pad_maximum_fusion.1.refs_2_), channel_id=1, source_target_pairs={{0,4},{4,0},{1,5},{5,1},{2,6},{6,2},{3,7},{7,3},{8,12},{12,8},{9,1... | collective-permute-start | bytes 1572872 | tf_op jit(solution)/shard_map/ppermute | solution.py:481
  49.3 0.0 collective-permute-done.13.refs_9_
  49.3 1.2 %collective-permute-start.20 = (bf16[4,128,512]{2,1,0:T(8,128)(2,1)S(1)}, bf16[4,128,512]{2,1,0:T(8,128)(2,1)S(1)}, u32[]{:S(2)}, u32[]{:S(2)}) collective-permute-start(bf16[4,128,512]{2,1,0:T(8,128)(2,1)S(1)} %pad_maximum_fusion.1.refs_2_), channel_id=1, source_target_pairs={{0,6},{2,4},{4,2},{6,0},{1,7},{3,5},{5,3},{7,1},{8,14},{10,12},{12... | collective-permute-start | bytes 1572872 | tf_op jit(solution)/shard_map/ppermute | solution.py:482
  50.6 0.0 collective-permute-done.10.refs_6_
  50.6 0.0 collective-permute-start.21
  50.6 0.0 collective-permute-done.11.refs_7_
  50.6 28.1 %shard_map.76 = (bf16[1024,1024]{1,0:T(8,128)(2,1)S(1)}, bf16[1024,1024]{1,0:T(8,128)(2,1)S(1)}, bf16[1024,2048]{1,0:T(8,128)(2,1)S(1)}) custom-call(s32[14]{0:T(128)S(1)} %stack.124.places, bf16[4,128,512]{2,1,0:T(8,128)(2,1)S(1)} %pad_maximum_fusion.refs_0_, bf16[4,128,512]{2,1,0:T(8,128)(2,1)S(1)} %collective-permute-done.5.refs_1_, ...), custom_call_target="tpu_custom_call" | custom-call | flops 40000000000 | bytes 20971520 | tf_op jit(solution)/shard_map/pallas_call | solution.py:227
  78.6 0.0 collective-permute-done.18.refs_3_
  78.7 0.0 collective-permute-done.19.refs_4_
  78.7 0.0 collective-permute-done.20.refs_5_
  78.7 0.6 collective-permute-start.22
  79.2 0.1 collective-permute-start.23
  79.3 0.4 collective-permute-start.24
  79.8 0.0 collective-permute-done.21.refs_6_
  79.8 1.0 %collective-permute-done.22.refs_7_ = bf16[4,128,512]{2,1,0:T(8,128)(2,1)S(1)} collective-permute-done((bf16[4,128,512]{2,1,0:T(8,128)(2,1)S(1)}, bf16[4,128,512]{2,1,0:T(8,128)(2,1)S(1)}, u32[]{:S(2)}, u32[]{:S(2)}) %collective-permute-start.22) | collective-permute-done | bytes 524320 | tf_op jit(solution)/shard_map/ppermute | solution.py:510
  80.8 0.7 collective-permute-done.23.refs_8_
  81.5 0.7 collective-permute-done.24.refs_9_
  82.3 18.9 %shard_map.77 = (f32[512,1024]{1,0:T(8,128)}, f32[64,1024]{1,0:T(8,128)}, f32[64,512]{1,0:T(8,128)}) custom-call(s32[17]{0:T(128)S(1)} %stack.132.facts, bf16[1024,2048]{1,0:T(8,128)(2,1)S(1)} %get-tuple-element.20.panel_ref, bf16[1024,1024]{1,0:T(8,128)(2,1)S(1)} %get-tuple-element.25.high_ref, bf16[1024,1024]{1,0:T(8,128)(2,1)S(1)} %get-tuple-element.26.low_ref, ...), custom_call_target="tpu_custom_call" | custom-call | flops 20000000000 | bytes 20971520 | tf_op jit(solution)/shard_map/pallas_call | solution.py:391
  (6 shorter events, 0.1 us)
Async XLA Ops:
  0.6 5.9 %copy-start = (f32[64,512]{1,0:T(8,128)S(1)}, f32[64,512]{1,0:T(8,128)}, u32[]{:S(2)}) copy-start(f32[64,512]{1,0:T(8,128)} %param.7) | copy-start | bytes 393220
  2.8 7.1 %collective-permute-start = (bf16[128,512]{1,0:T(8,128)(2,1)S(1)}, bf16[128,512]{1,0:T(8,128)(2,1)S(1)}, u32[]{:S(2)}, u32[]{:S(2)}) collective-permute-start(bf16[128,512]{1,0:T(8,128)(2,1)S(1)} %fusion), channel_id=1, source_target_pairs={{0,4},{4,0},{1,5},{5,1},{2,6},{6,2},{3,7},{7,3},{8,12},{12,8},{9,1... | collective-permute-start | bytes 393224 | tf_op jit(solution)/shard_map/ppermute | solution.py:446
  6.6 9.6 %collective-permute-start.4 = (f32[64,512]{1,0:T(8,128)S(1)}, f32[64,512]{1,0:T(8,128)S(1)}, u32[]{:S(2)}, u32[]{:S(2)}) collective-permute-start(f32[64,512]{1,0:T(8,128)S(1)} %broadcast_multiply_fusion.own_ref), channel_id=1, source_target_pairs={{0,4},{4,0},{1,5},{5,1},{2,6},{6,2},{3,7},{7,3},{8,12},{12,8},{9,1... | collective-permute-start | bytes 393224 | tf_op jit(solution)/shard_map/ppermute | solution.py:455
  10.0 8.6 %collective-permute-start.1 = (bf16[128,512]{1,0:T(8,128)(2,1)S(1)}, bf16[128,512]{1,0:T(8,128)(2,1)S(1)}, u32[]{:S(2)}, u32[]{:S(2)}) collective-permute-start(bf16[128,512]{1,0:T(8,128)(2,1)S(1)} %bitcast_select_fusion.1), channel_id=1, source_target_pairs={{0,8},{8,16},{16,24},{24,0},{1,9},{9,17},{17,25},{25,1},{2,10},{10... | collective-permute-start | bytes 393224 | tf_op jit(solution)/shard_map/ppermute | solution.py:452
  12.2 9.8 %collective-permute-start.2 = (bf16[128,512]{1,0:T(8,128)(2,1)S(1)}, bf16[128,512]{1,0:T(8,128)(2,1)S(1)}, u32[]{:S(2)}, u32[]{:S(2)}) collective-permute-start(bf16[128,512]{1,0:T(8,128)(2,1)S(1)} %bitcast_select_fusion.1), channel_id=1, source_target_pairs={{0,16},{8,24},{16,0},{24,8},{1,17},{9,25},{17,1},{25,9},{2,18},{10... | collective-permute-start | bytes 393224 | tf_op jit(solution)/shard_map/ppermute | solution.py:452
  14.8 7.2 %collective-permute-start.3 = (bf16[128,512]{1,0:T(8,128)(2,1)S(1)}, bf16[128,512]{1,0:T(8,128)(2,1)S(1)}, u32[]{:S(2)}, u32[]{:S(2)}) collective-permute-start(bf16[128,512]{1,0:T(8,128)(2,1)S(1)} %bitcast_select_fusion.1), channel_id=1, source_target_pairs={{0,24},{8,0},{16,8},{24,16},{1,25},{9,1},{17,9},{25,17},{2,26},{10... | collective-permute-start | bytes 393224 | tf_op jit(solution)/shard_map/ppermute | solution.py:452
  22.0 13.6 %collective-permute-start.6 = (bf16[4,128,512]{2,1,0:T(8,128)(2,1)S(1)}, bf16[4,128,512]{2,1,0:T(8,128)(2,1)S(1)}, u32[]{:S(2)}, u32[]{:S(2)}) collective-permute-start(bf16[4,128,512]{2,1,0:T(8,128)(2,1)S(1)} %pad_maximum_fusion.refs_0_), channel_id=1, source_target_pairs={{0,4},{4,0},{1,5},{5,1},{2,6},{6,2},{3,7},{7,3},{8,12},{12,8},{9,1... | collective-permute-start | bytes 1572872 | tf_op jit(solution)/shard_map/ppermute | solution.py:466
  24.1 12.9 %collective-permute-start.5 = (bf16[4,128,512]{2,1,0:T(8,128)(2,1)S(1)}, bf16[4,128,512]{2,1,0:T(8,128)(2,1)S(1)}, u32[]{:S(2)}, u32[]{:S(2)}) collective-permute-start(bf16[4,128,512]{2,1,0:T(8,128)(2,1)S(1)} %pad_maximum_fusion.refs_0_), channel_id=1, source_target_pairs={{0,2},{2,0},{1,3},{3,1},{4,6},{6,4},{5,7},{7,5},{8,10},{10,8},{9,1... | collective-permute-start | bytes 1572872 | tf_op jit(solution)/shard_map/ppermute | solution.py:466
  25.5 11.6 %collective-permute-start.14 = (bf16[128,512]{1,0:T(8,128)(2,1)S(1)}, bf16[128,512]{1,0:T(8,128)(2,1)S(1)}, u32[]{:S(2)}, u32[]{:S(2)}) collective-permute-start(bf16[128,512]{1,0:T(8,128)(2,1)S(1)} %get-tuple-element.22), channel_id=1, source_target_pairs={{0,8},{8,16},{16,24},{24,0},{1,9},{9,17},{17,25},{25,1},{2,10},{10... | collective-permute-start | bytes 393224 | tf_op jit(solution)/shard_map/ppermute | solution.py:452
  28.2 9.7 %collective-permute-start.15 = (bf16[128,512]{1,0:T(8,128)(2,1)S(1)}, bf16[128,512]{1,0:T(8,128)(2,1)S(1)}, u32[]{:S(2)}, u32[]{:S(2)}) collective-permute-start(bf16[128,512]{1,0:T(8,128)(2,1)S(1)} %get-tuple-element.22), channel_id=1, source_target_pairs={{0,16},{8,24},{16,0},{24,8},{1,17},{9,25},{17,1},{25,9},{2,18},{10... | collective-permute-start | bytes 393224 | tf_op jit(solution)/shard_map/ppermute | solution.py:452
  29.8 9.3 %collective-permute-start.16 = (bf16[128,512]{1,0:T(8,128)(2,1)S(1)}, bf16[128,512]{1,0:T(8,128)(2,1)S(1)}, u32[]{:S(2)}, u32[]{:S(2)}) collective-permute-start(bf16[128,512]{1,0:T(8,128)(2,1)S(1)} %get-tuple-element.22), channel_id=1, source_target_pairs={{0,24},{8,0},{16,8},{24,16},{1,25},{9,1},{17,9},{25,17},{2,26},{10... | collective-permute-start | bytes 393224 | tf_op jit(solution)/shard_map/ppermute | solution.py:452
  35.7 5.3 %collective-permute-start.17 = (f32[64,512]{1,0:T(8,128)S(1)}, f32[64,512]{1,0:T(8,128)S(1)}, u32[]{:S(2)}, u32[]{:S(2)}) collective-permute-start(f32[64,512]{1,0:T(8,128)S(1)} %broadcast_select_fusion.refs_0_), channel_id=1, source_target_pairs={{0,2},{2,0},{1,3},{3,1},{4,6},{6,4},{5,7},{7,5},{8,10},{10,8},{9,1... | collective-permute-start | bytes 393224 | tf_op jit(solution)/shard_map/ppermute | solution.py:465
  37.0 9.8 %collective-permute-start.9 = (bf16[4,128,512]{2,1,0:T(8,128)(2,1)S(1)}, bf16[4,128,512]{2,1,0:T(8,128)(2,1)S(1)}, u32[]{:S(2)}, u32[]{:S(2)}) collective-permute-start(bf16[4,128,512]{2,1,0:T(8,128)(2,1)S(1)} %pad_maximum_fusion.refs_0_), channel_id=1, source_target_pairs={{0,1},{1,0},{2,3},{3,2},{4,5},{5,4},{6,7},{7,6},{8,9},{9,8},{10,11... | collective-permute-start | bytes 1572872 | tf_op jit(solution)/shard_map/ppermute | solution.py:470
  37.1 9.1 %collective-permute-start.7 = (bf16[2,128,512]{2,1,0:T(8,128)(2,1)S(1)}, bf16[2,128,512]{2,1,0:T(8,128)(2,1)S(1)}, u32[]{:S(2)}, u32[]{:S(2)}) collective-permute-start(bf16[2,128,512]{2,1,0:T(8,128)(2,1)S(1)} %slice.8), channel_id=1, source_target_pairs={{0,2},{2,0},{1,3},{3,1},{4,6},{6,4},{5,7},{7,5},{8,10},{10,8},{9,1... | collective-permute-start | bytes 786440 | tf_op jit(solution)/shard_map/ppermute | solution.py:467
  37.9 8.4 %collective-permute-start.8 = (bf16[2,128,512]{2,1,0:T(8,128)(2,1)S(1)}, bf16[2,128,512]{2,1,0:T(8,128)(2,1)S(1)}, u32[]{:S(2)}, u32[]{:S(2)}) collective-permute-start(bf16[2,128,512]{2,1,0:T(8,128)(2,1)S(1)} %slice.9), channel_id=1, source_target_pairs={{0,4},{4,0},{1,5},{5,1},{2,6},{6,2},{3,7},{7,3},{8,12},{12,8},{9,1... | collective-permute-start | bytes 786440 | tf_op jit(solution)/shard_map/ppermute | solution.py:468
  39.1 11.5 %collective-permute-start.10 = (bf16[4,128,512]{2,1,0:T(8,128)(2,1)S(1)}, bf16[4,128,512]{2,1,0:T(8,128)(2,1)S(1)}, u32[]{:S(2)}, u32[]{:S(2)}) collective-permute-start(bf16[4,128,512]{2,1,0:T(8,128)(2,1)S(1)} %collective-permute-done.5.refs_1_), channel_id=1, source_target_pairs={{0,1},{1,0},{2,3},{3,2},{4,5},{5,4},{6,7},{7,6},{8,9},{9,8},{10,11... | collective-permute-start | bytes 1572872 | tf_op jit(solution)/shard_map/ppermute | solution.py:470
  41.0 9.6 %collective-permute-start.11 = (bf16[4,128,512]{2,1,0:T(8,128)(2,1)S(1)}, bf16[4,128,512]{2,1,0:T(8,128)(2,1)S(1)}, u32[]{:S(2)}, u32[]{:S(2)}) collective-permute-start(bf16[4,128,512]{2,1,0:T(8,128)(2,1)S(1)} %collective-permute-done.6.refs_2_), channel_id=1, source_target_pairs={{0,1},{1,0},{2,3},{3,2},{4,5},{5,4},{6,7},{7,6},{8,9},{9,8},{10,11... | collective-permute-start | bytes 1572872 | tf_op jit(solution)/shard_map/ppermute | solution.py:470
  46.2 2.0 %collective-permute-start.12 = (bf16[2,128,512]{2,1,0:T(8,128)(2,1)S(1)}, bf16[2,128,512]{2,1,0:T(8,128)(2,1)S(1)}, u32[]{:S(2)}, u32[]{:S(2)}) collective-permute-start(bf16[2,128,512]{2,1,0:T(8,128)(2,1)S(1)} %collective-permute-done.7.refs_3_), channel_id=1, source_target_pairs={{0,1},{1,0},{2,3},{3,2},{4,5},{5,4},{6,7},{7,6},{8,9},{9,8},{10,11... | collective-permute-start | bytes 786440 | tf_op jit(solution)/shard_map/ppermute | solution.py:470
  46.3 3.0 %collective-permute-start.13 = (bf16[2,128,512]{2,1,0:T(8,128)(2,1)S(1)}, bf16[2,128,512]{2,1,0:T(8,128)(2,1)S(1)}, u32[]{:S(2)}, u32[]{:S(2)}) collective-permute-start(bf16[2,128,512]{2,1,0:T(8,128)(2,1)S(1)} %collective-permute-done.8.refs_4_), channel_id=1, source_target_pairs={{0,1},{1,0},{2,3},{3,2},{4,5},{5,4},{6,7},{7,6},{8,9},{9,8},{10,11... | collective-permute-start | bytes 786440 | tf_op jit(solution)/shard_map/ppermute | solution.py:470
  46.8 31.8 %collective-permute-start.18 = (bf16[4,128,512]{2,1,0:T(8,128)(2,1)S(1)}, bf16[4,128,512]{2,1,0:T(8,128)(2,1)S(1)}, u32[]{:S(2)}, u32[]{:S(2)}) collective-permute-start(bf16[4,128,512]{2,1,0:T(8,128)(2,1)S(1)} %pad_maximum_fusion.1.refs_2_), channel_id=1, source_target_pairs={{0,2},{2,0},{1,3},{3,1},{4,6},{6,4},{5,7},{7,5},{8,10},{10,8},{9,1... | collective-permute-start | bytes 1572872 | tf_op jit(solution)/shard_map/ppermute | solution.py:480
  48.2 30.4 %collective-permute-start.19 = (bf16[4,128,512]{2,1,0:T(8,128)(2,1)S(1)}, bf16[4,128,512]{2,1,0:T(8,128)(2,1)S(1)}, u32[]{:S(2)}, u32[]{:S(2)}) collective-permute-start(bf16[4,128,512]{2,1,0:T(8,128)(2,1)S(1)} %pad_maximum_fusion.1.refs_2_), channel_id=1, source_target_pairs={{0,4},{4,0},{1,5},{5,1},{2,6},{6,2},{3,7},{7,3},{8,12},{12,8},{9,1... | collective-permute-start | bytes 1572872 | tf_op jit(solution)/shard_map/ppermute | solution.py:481
  49.3 29.4 %collective-permute-start.20 = (bf16[4,128,512]{2,1,0:T(8,128)(2,1)S(1)}, bf16[4,128,512]{2,1,0:T(8,128)(2,1)S(1)}, u32[]{:S(2)}, u32[]{:S(2)}) collective-permute-start(bf16[4,128,512]{2,1,0:T(8,128)(2,1)S(1)} %pad_maximum_fusion.1.refs_2_), channel_id=1, source_target_pairs={{0,6},{2,4},{4,2},{6,0},{1,7},{3,5},{5,3},{7,1},{8,14},{10,12},{12... | collective-permute-start | bytes 1572872 | tf_op jit(solution)/shard_map/ppermute | solution.py:482
  50.6 29.2 %collective-permute-start.21 = (bf16[4,128,512]{2,1,0:T(8,128)(2,1)S(1)}, bf16[4,128,512]{2,1,0:T(8,128)(2,1)S(1)}, u32[]{:S(2)}, u32[]{:S(2)}) collective-permute-start(bf16[4,128,512]{2,1,0:T(8,128)(2,1)S(1)} %pad_maximum_fusion.1.refs_2_), channel_id=1, source_target_pairs={{0,1},{1,0},{2,3},{3,2},{4,5},{5,4},{6,7},{7,6},{8,9},{9,8},{10,11... | collective-permute-start | bytes 1572872 | tf_op jit(solution)/shard_map/ppermute | solution.py:484
  78.7 2.1 %collective-permute-start.22 = (bf16[4,128,512]{2,1,0:T(8,128)(2,1)S(1)}, bf16[4,128,512]{2,1,0:T(8,128)(2,1)S(1)}, u32[]{:S(2)}, u32[]{:S(2)}) collective-permute-start(bf16[4,128,512]{2,1,0:T(8,128)(2,1)S(1)} %collective-permute-done.18.refs_3_), channel_id=1, source_target_pairs={{0,1},{1,0},{2,3},{3,2},{4,5},{5,4},{6,7},{7,6},{8,9},{9,8},{10,11... | collective-permute-start | bytes 1572872 | tf_op jit(solution)/shard_map/ppermute | solution.py:510
  79.2 2.3 %collective-permute-start.23 = (bf16[4,128,512]{2,1,0:T(8,128)(2,1)S(1)}, bf16[4,128,512]{2,1,0:T(8,128)(2,1)S(1)}, u32[]{:S(2)}, u32[]{:S(2)}) collective-permute-start(bf16[4,128,512]{2,1,0:T(8,128)(2,1)S(1)} %collective-permute-done.19.refs_4_), channel_id=1, source_target_pairs={{0,1},{1,0},{2,3},{3,2},{4,5},{5,4},{6,7},{7,6},{8,9},{9,8},{10,11... | collective-permute-start | bytes 1572872 | tf_op jit(solution)/shard_map/ppermute | solution.py:510
  79.3 3.0 %collective-permute-start.24 = (bf16[4,128,512]{2,1,0:T(8,128)(2,1)S(1)}, bf16[4,128,512]{2,1,0:T(8,128)(2,1)S(1)}, u32[]{:S(2)}, u32[]{:S(2)}) collective-permute-start(bf16[4,128,512]{2,1,0:T(8,128)(2,1)S(1)} %collective-permute-done.20.refs_5_), channel_id=1, source_target_pairs={{0,1},{1,0},{2,3},{3,2},{4,5},{5,4},{6,7},{7,6},{8,9},{9,8},{10,11... | collective-permute-start | bytes 1572872 | tf_op jit(solution)/shard_map/ppermute | solution.py:510

commit v4 on v3

--- a/solution.py
+++ b/solution.py
@@ -459,22 +459,20 @@
         def place(m, a, c):
             return (m * 4 + a * 2 + c) * quarter
 
-        places = numbers([place(m, a, c) for c in (col, 1 - col) for m, a in corners + corners[3:]] + slots)
+        places = numbers([place(m, a, c) for c in (col, 1 - col) for m, a in corners] + slots)
         facts = numbers(common + [place(m, a, c) for c in (col, 1 - col) for m, a in corners] + slots)
         own, panel_masked, places, facts = lax.optimization_barrier((own, panel_masked, places, facts))
         beside = lax.ppermute(panel_masked, "mem", swap)
         by_mem, by_pan = lax.ppermute(own, "mem", swap), lax.ppermute(own, "pan", swap)
-        far_a = lax.ppermute(by_pan[:2], "mem", swap)
-        far_b = lax.ppermute(by_mem[2:], "pan", swap)
-        near = [own, by_mem, by_pan, far_a, far_b]
+        cross = [(2 * i + j, 2 * (1 - i) + 1 - j) for i in range(2) for j in range(2)]
+        far = lax.ppermute(own, ("pan", "mem"), cross)
+        near = [own, by_mem, by_pan, far]
         twin = [lax.ppermute(v, "col", swap) for v in near]
         pieces = near + twin
-        plan = [(0, 1, 2, 3)] * 3 + [(0, 1), (2, 3)]
-        plan = plan + plan
+        plan = [(0, 1, 2, 3)] * 8
         rest_piece, _ = lax.optimization_barrier((rest_piece, own))
         rest_own = jnp.stack([rest_piece] + along_samp(rest_piece))
         rest_own, _, _, beside = lax.optimization_barrier((rest_own, by_mem, by_pan, beside))
-        cross = [(2 * i + j, 2 * (1 - i) + 1 - j) for i in range(2) for j in range(2)]
         rest = [
             rest_own,
             lax.ppermute(rest_own, "mem", swap),

time: 103 us -> 123 us (1.19); the launches traced: 101 us -> 123 us
  waiting for transfers between devices: 22.8 us -> 40.2 us
  starting transfers between devices: 26.3 us -> 30.6 us
    ppermute x1, waiting for transfers between devices: 5.09 us -> 18.1 us  [on_device(): lax.ppermute(own, 'pan', swap)]
    ppermute x6, waiting for transfers between devices: 5.8 us -> 13.1 us  [along_samp(): return [lax.ppermute(v, 'samp', pairs) for pairs in steps]]
    ppermute x6, starting transfers between devices: 11.1 us -> 17.5 us  [along_samp(): return [lax.ppermute(v, 'samp', pairs) for pairs in steps]]
    ppermute x2 -> x1, waiting for transfers between devices: 5.34 us -> 0.01 us  [on_device(): far = lax.ppermute(own, ('pan', 'mem'), cross)]
    ppermute x1, waiting for transfers between devices: 1.91 us -> 3.59 us  [on_device(): beside = lax.ppermute(panel_masked, 'mem', swap)]
  transfers between devices with their start and end apart: 25 -> 23, of which waited for: 10 -> 11; matrix products, arithmetic and copies ran while one was open for 1% -> 1% of each run, Pallas kernels for 28% -> 23%
where the time goes in v4:
time: 123 us
  Pallas kernels  47 us (38%)
  waiting for transfers between devices  40.2 us (33%)
  starting transfers between devices  30.6 us (25%)
  other arithmetic  1.95 us (2%)
  between operations  1.75 us (1%)
  local copies, waits for them, and re-layouts  1.52 us (1%)
    pallas_call x1, Pallas kernels, panel_step(): pl.pallas_call(functools.partial(panel_kernel, plan, samples_all), out_sh...  28.1 us
    pallas_call x1, Pallas kernels, tile_step(): pl.pallas_call(functools.partial(tile_kernel, samples_all, n_places, len(...  18.9 us
    ppermute x1, waiting for transfers between devices, on_device(): lax.ppermute(own, 'pan', swap)  18.1 us
    ppermute x6, starting transfers between devices, along_samp(): return [lax.ppermute(v, 'samp', pairs) for pairs in steps]  17.5 us
    ppermute x6, waiting for transfers between devices, along_samp(): return [lax.ppermute(v, 'samp', pairs) for pairs in steps]  13.1 us
    ppermute x1, waiting for transfers between devices, on_device(): beside = lax.ppermute(panel_masked, 'mem', swap)  3.59 us
    ppermute x1, starting transfers between devices, on_device(): lax.ppermute(part(1 - pan, col), 'pan', swap)  3.03 us
    ppermute x3, waiting for transfers between devices, on_device(): lax.ppermute(v, 'col', swap)  2.52 us
  transfers between devices with their start and end apart: 23, of which 11 were waited for; matrix products, arithmetic and copies ran while one was open for 1% of the time, Pallas kernels for 23%

profile of v4, /device:TPU:0, one launch (start us, length us, event | category | flops | bytes accessed | tf_op | source)
XLA Modules:
  0.0 123.0 jit_solution(6241388957292516598)
XLA Ops:
  0.6 0.0 copy-start
  0.7 0.8 broadcast_multiply_fusion.2
  1.5 1.1 constant_dynamic-slice_fusion.1
  2.6 0.1 copy.11
  2.7 0.1 fusion
  2.8 3.0 %collective-permute-start = (bf16[128,512]{1,0:T(8,128)(2,1)S(1)}, bf16[128,512]{1,0:T(8,128)(2,1)S(1)}, u32[]{:S(2)}, u32[]{:S(2)}) collective-permute-start(bf16[128,512]{1,0:T(8,128)(2,1)S(1)} %fusion), channel_id=1, source_target_pairs={{0,4},{4,0},{1,5},{5,1},{2,6},{6,2},{3,7},{7,3},{8,12},{12,8},{9,1... | collective-permute-start | bytes 393224 | tf_op jit(solution)/shard_map/ppermute | solution.py:446
  5.9 0.7 convert_element_type.21
  6.5 0.0 copy-done
  6.6 0.1 collective-permute-start.4
  7.4 0.1 copy.10
  7.6 0.1 stack.122.places
  7.7 0.1 stack.130.facts
  7.8 2.1 %collective-permute-done = bf16[128,512]{1,0:T(8,128)(2,1)S(1)} collective-permute-done((bf16[128,512]{1,0:T(8,128)(2,1)S(1)}, bf16[128,512]{1,0:T(8,128)(2,1)S(1)}, u32[]{:S(2)}, u32[]{:S(2)}) %collective-permute-start) | collective-permute-done | bytes 131104 | tf_op jit(solution)/shard_map/ppermute | solution.py:446
  9.9 0.1 bitcast_select_fusion
  10.0 2.1 %collective-permute-start.1 = (bf16[128,512]{1,0:T(8,128)(2,1)S(1)}, bf16[128,512]{1,0:T(8,128)(2,1)S(1)}, u32[]{:S(2)}, u32[]{:S(2)}) collective-permute-start(bf16[128,512]{1,0:T(8,128)(2,1)S(1)} %bitcast_select_fusion.1), channel_id=1, source_target_pairs={{0,8},{8,16},{16,24},{24,0},{1,9},{9,17},{17,25},{25,1},{2,10},{10... | collective-permute-start | bytes 393224 | tf_op jit(solution)/shard_map/ppermute | solution.py:452
  12.2 2.6 %collective-permute-start.2 = (bf16[128,512]{1,0:T(8,128)(2,1)S(1)}, bf16[128,512]{1,0:T(8,128)(2,1)S(1)}, u32[]{:S(2)}, u32[]{:S(2)}) collective-permute-start(bf16[128,512]{1,0:T(8,128)(2,1)S(1)} %bitcast_select_fusion.1), channel_id=1, source_target_pairs={{0,16},{8,24},{16,0},{24,8},{1,17},{9,25},{17,1},{25,9},{2,18},{10... | collective-permute-start | bytes 393224 | tf_op jit(solution)/shard_map/ppermute | solution.py:452
  14.8 1.3 %collective-permute-start.3 = (bf16[128,512]{1,0:T(8,128)(2,1)S(1)}, bf16[128,512]{1,0:T(8,128)(2,1)S(1)}, u32[]{:S(2)}, u32[]{:S(2)}) collective-permute-start(bf16[128,512]{1,0:T(8,128)(2,1)S(1)} %bitcast_select_fusion.1), channel_id=1, source_target_pairs={{0,24},{8,0},{16,8},{24,16},{1,25},{9,1},{17,9},{25,17},{2,26},{10... | collective-permute-start | bytes 393224 | tf_op jit(solution)/shard_map/ppermute | solution.py:452
  16.1 0.0 collective-permute-done.4
  16.2 2.5 %collective-permute-done.1 = bf16[128,512]{1,0:T(8,128)(2,1)S(1)} collective-permute-done((bf16[128,512]{1,0:T(8,128)(2,1)S(1)}, bf16[128,512]{1,0:T(8,128)(2,1)S(1)}, u32[]{:S(2)}, u32[]{:S(2)}) %collective-permute-start.1) | collective-permute-done | bytes 131104 | tf_op jit(solution)/shard_map/ppermute | solution.py:452
  18.7 3.3 %collective-permute-done.2 = bf16[128,512]{1,0:T(8,128)(2,1)S(1)} collective-permute-done((bf16[128,512]{1,0:T(8,128)(2,1)S(1)}, bf16[128,512]{1,0:T(8,128)(2,1)S(1)}, u32[]{:S(2)}, u32[]{:S(2)}) %collective-permute-start.2) | collective-permute-done | bytes 131104 | tf_op jit(solution)/shard_map/ppermute | solution.py:452
  21.9 0.0 collective-permute-done.3
  21.9 0.1 pad_maximum_fusion.refs_0_
  22.0 2.0 %collective-permute-start.6 = (bf16[4,128,512]{2,1,0:T(8,128)(2,1)S(1)}, bf16[4,128,512]{2,1,0:T(8,128)(2,1)S(1)}, u32[]{:S(2)}, u32[]{:S(2)}) collective-permute-start(bf16[4,128,512]{2,1,0:T(8,128)(2,1)S(1)} %pad_maximum_fusion.refs_0_), channel_id=1, source_target_pairs={{0,4},{4,0},{1,5},{5,1},{2,6},{6,2},{3,7},{7,3},{8,12},{12,8},{9,1... | collective-permute-start | bytes 1572872 | tf_op jit(solution)/shard_map/ppermute | solution.py:466
  24.1 1.1 collective-permute-start.7
  25.1 0.5 collective-permute-start.5
  25.6 3.2 %collective-permute-start.12 = (bf16[128,512]{1,0:T(8,128)(2,1)S(1)}, bf16[128,512]{1,0:T(8,128)(2,1)S(1)}, u32[]{:S(2)}, u32[]{:S(2)}) collective-permute-start(bf16[128,512]{1,0:T(8,128)(2,1)S(1)} %get-tuple-element.22), channel_id=1, source_target_pairs={{0,8},{8,16},{16,24},{24,0},{1,9},{9,17},{17,25},{25,1},{2,10},{10... | collective-permute-start | bytes 393224 | tf_op jit(solution)/shard_map/ppermute | solution.py:452
  28.8 0.0 collective-permute-start.8
  28.8 18.1 %collective-permute-done.6.refs_2_ = bf16[4,128,512]{2,1,0:T(8,128)(2,1)S(1)} collective-permute-done((bf16[4,128,512]{2,1,0:T(8,128)(2,1)S(1)}, bf16[4,128,512]{2,1,0:T(8,128)(2,1)S(1)}, u32[]{:S(2)}, u32[]{:S(2)}) %collective-permute-start.6) | collective-permute-done | bytes 524320 | tf_op jit(solution)/shard_map/ppermute | solution.py:466
  46.9 0.0 collective-permute-start.10
  46.9 0.0 collective-permute-done.7.refs_3_
  46.9 0.5 collective-permute-start.11
  47.4 0.7 collective-permute-done.5.refs_1_
  48.1 0.0 collective-permute-start.9
  48.1 0.0 collective-permute-done.12
  48.1 2.4 %collective-permute-start.13 = (bf16[128,512]{1,0:T(8,128)(2,1)S(1)}, bf16[128,512]{1,0:T(8,128)(2,1)S(1)}, u32[]{:S(2)}, u32[]{:S(2)}) collective-permute-start(bf16[128,512]{1,0:T(8,128)(2,1)S(1)} %get-tuple-element.22), channel_id=1, source_target_pairs={{0,16},{8,24},{16,0},{24,8},{1,17},{9,25},{17,1},{25,9},{2,18},{10... | collective-permute-start | bytes 393224 | tf_op jit(solution)/shard_map/ppermute | solution.py:452
  50.5 4.5 %collective-permute-done.13 = bf16[128,512]{1,0:T(8,128)(2,1)S(1)} collective-permute-done((bf16[128,512]{1,0:T(8,128)(2,1)S(1)}, bf16[128,512]{1,0:T(8,128)(2,1)S(1)}, u32[]{:S(2)}, u32[]{:S(2)}) %collective-permute-start.13) | collective-permute-done | bytes 131104 | tf_op jit(solution)/shard_map/ppermute | solution.py:452
  54.9 5.9 %collective-permute-start.14 = (bf16[128,512]{1,0:T(8,128)(2,1)S(1)}, bf16[128,512]{1,0:T(8,128)(2,1)S(1)}, u32[]{:S(2)}, u32[]{:S(2)}) collective-permute-start(bf16[128,512]{1,0:T(8,128)(2,1)S(1)} %get-tuple-element.22), channel_id=1, source_target_pairs={{0,24},{8,0},{16,8},{24,16},{1,25},{9,1},{17,9},{25,17},{2,26},{10... | collective-permute-start | bytes 393224 | tf_op jit(solution)/shard_map/ppermute | solution.py:452
  60.8 2.9 %collective-permute-done.14 = bf16[128,512]{1,0:T(8,128)(2,1)S(1)} collective-permute-done((bf16[128,512]{1,0:T(8,128)(2,1)S(1)}, bf16[128,512]{1,0:T(8,128)(2,1)S(1)}, u32[]{:S(2)}, u32[]{:S(2)}) %collective-permute-start.14) | collective-permute-done | bytes 131104 | tf_op jit(solution)/shard_map/ppermute | solution.py:452
  63.7 1.3 %collective-permute-start.15 = (f32[64,512]{1,0:T(8,128)S(1)}, f32[64,512]{1,0:T(8,128)S(1)}, u32[]{:S(2)}, u32[]{:S(2)}) collective-permute-start(f32[64,512]{1,0:T(8,128)S(1)} %broadcast_select_fusion.refs_0_), channel_id=1, source_target_pairs={{0,2},{2,0},{1,3},{3,1},{4,6},{6,4},{5,7},{7,5},{8,10},{10,8},{9,1... | collective-permute-start | bytes 393224 | tf_op jit(solution)/shard_map/ppermute | solution.py:465
  65.0 0.1 pad_maximum_fusion.1.refs_2_
  65.1 3.6 %collective-permute-done.15.refs_1_ = f32[64,512]{1,0:T(8,128)S(1)} collective-permute-done((f32[64,512]{1,0:T(8,128)S(1)}, f32[64,512]{1,0:T(8,128)S(1)}, u32[]{:S(2)}, u32[]{:S(2)}) %collective-permute-start.15) | collective-permute-done | bytes 131104 | tf_op jit(solution)/shard_map/ppermute | solution.py:465
  68.7 1.3 %collective-permute-start.16 = (bf16[4,128,512]{2,1,0:T(8,128)(2,1)S(1)}, bf16[4,128,512]{2,1,0:T(8,128)(2,1)S(1)}, u32[]{:S(2)}, u32[]{:S(2)}) collective-permute-start(bf16[4,128,512]{2,1,0:T(8,128)(2,1)S(1)} %pad_maximum_fusion.1.refs_2_), channel_id=1, source_target_pairs={{0,2},{2,0},{1,3},{3,1},{4,6},{6,4},{5,7},{7,5},{8,10},{10,8},{9,1... | collective-permute-start | bytes 1572872 | tf_op jit(solution)/shard_map/ppermute | solution.py:478
  70.0 0.0 collective-permute-done.8.refs_4_
  70.0 1.1 collective-permute-start.17
  71.1 0.0 collective-permute-done.10.refs_6_
  71.1 1.1 collective-permute-start.18
  72.2 0.0 collective-permute-done.11.refs_7_
  72.2 0.0 collective-permute-start.19
  72.2 0.0 collective-permute-done.9.refs_5_
  72.2 28.1 %shard_map.76 = (bf16[1024,1024]{1,0:T(8,128)(2,1)S(1)}, bf16[1024,1024]{1,0:T(8,128)(2,1)S(1)}, bf16[1024,2048]{1,0:T(8,128)(2,1)S(1)}) custom-call(s32[12]{0:T(128)S(1)} %stack.122.places, bf16[4,128,512]{2,1,0:T(8,128)(2,1)S(1)} %pad_maximum_fusion.refs_0_, bf16[4,128,512]{2,1,0:T(8,128)(2,1)S(1)} %collective-permute-done.5.refs_1_, ...), custom_call_target="tpu_custom_call" | custom-call | flops 40000000000 | bytes 20971520 | tf_op jit(solution)/shard_map/pallas_call | solution.py:227
  100.2 0.0 collective-permute-done.16.refs_3_
  100.3 0.0 collective-permute-done.17.refs_4_
  100.3 0.0 collective-permute-done.18.refs_5_
  100.3 0.6 collective-permute-start.20
  100.9 0.1 collective-permute-start.21
  100.9 0.4 collective-permute-start.22
  101.4 0.0 collective-permute-done.19.refs_6_
  101.4 1.0 collective-permute-done.20.refs_7_
  102.4 0.7 collective-permute-done.21.refs_8_
  103.1 0.7 collective-permute-done.22.refs_9_
  103.9 18.9 %shard_map.77 = (f32[512,1024]{1,0:T(8,128)}, f32[64,1024]{1,0:T(8,128)}, f32[64,512]{1,0:T(8,128)}) custom-call(s32[17]{0:T(128)S(1)} %stack.130.facts, bf16[1024,2048]{1,0:T(8,128)(2,1)S(1)} %get-tuple-element.20.panel_ref, bf16[1024,1024]{1,0:T(8,128)(2,1)S(1)} %get-tuple-element.25.high_ref, bf16[1024,1024]{1,0:T(8,128)(2,1)S(1)} %get-tuple-element.26.low_ref, ...), custom_call_target="tpu_custom_call" | custom-call | flops 20000000000 | bytes 20971520 | tf_op jit(solution)/shard_map/pallas_call | solution.py:391
  (3 shorter events, 0.0 us)
Async XLA Ops:
  0.6 5.9 %copy-start = (f32[64,512]{1,0:T(8,128)S(1)}, f32[64,512]{1,0:T(8,128)}, u32[]{:S(2)}) copy-start(f32[64,512]{1,0:T(8,128)} %param.7) | copy-start | bytes 393220
  2.8 7.1 %collective-permute-start = (bf16[128,512]{1,0:T(8,128)(2,1)S(1)}, bf16[128,512]{1,0:T(8,128)(2,1)S(1)}, u32[]{:S(2)}, u32[]{:S(2)}) collective-permute-start(bf16[128,512]{1,0:T(8,128)(2,1)S(1)} %fusion), channel_id=1, source_target_pairs={{0,4},{4,0},{1,5},{5,1},{2,6},{6,2},{3,7},{7,3},{8,12},{12,8},{9,1... | collective-permute-start | bytes 393224 | tf_op jit(solution)/shard_map/ppermute | solution.py:446
  6.6 9.6 %collective-permute-start.4 = (f32[64,512]{1,0:T(8,128)S(1)}, f32[64,512]{1,0:T(8,128)S(1)}, u32[]{:S(2)}, u32[]{:S(2)}) collective-permute-start(f32[64,512]{1,0:T(8,128)S(1)} %broadcast_multiply_fusion.own_ref), channel_id=1, source_target_pairs={{0,4},{4,0},{1,5},{5,1},{2,6},{6,2},{3,7},{7,3},{8,12},{12,8},{9,1... | collective-permute-start | bytes 393224 | tf_op jit(solution)/shard_map/ppermute | solution.py:455
  10.0 8.6 %collective-permute-start.1 = (bf16[128,512]{1,0:T(8,128)(2,1)S(1)}, bf16[128,512]{1,0:T(8,128)(2,1)S(1)}, u32[]{:S(2)}, u32[]{:S(2)}) collective-permute-start(bf16[128,512]{1,0:T(8,128)(2,1)S(1)} %bitcast_select_fusion.1), channel_id=1, source_target_pairs={{0,8},{8,16},{16,24},{24,0},{1,9},{9,17},{17,25},{25,1},{2,10},{10... | collective-permute-start | bytes 393224 | tf_op jit(solution)/shard_map/ppermute | solution.py:452
  12.2 9.8 %collective-permute-start.2 = (bf16[128,512]{1,0:T(8,128)(2,1)S(1)}, bf16[128,512]{1,0:T(8,128)(2,1)S(1)}, u32[]{:S(2)}, u32[]{:S(2)}) collective-permute-start(bf16[128,512]{1,0:T(8,128)(2,1)S(1)} %bitcast_select_fusion.1), channel_id=1, source_target_pairs={{0,16},{8,24},{16,0},{24,8},{1,17},{9,25},{17,1},{25,9},{2,18},{10... | collective-permute-start | bytes 393224 | tf_op jit(solution)/shard_map/ppermute | solution.py:452
  14.8 7.2 %collective-permute-start.3 = (bf16[128,512]{1,0:T(8,128)(2,1)S(1)}, bf16[128,512]{1,0:T(8,128)(2,1)S(1)}, u32[]{:S(2)}, u32[]{:S(2)}) collective-permute-start(bf16[128,512]{1,0:T(8,128)(2,1)S(1)} %bitcast_select_fusion.1), channel_id=1, source_target_pairs={{0,24},{8,0},{16,8},{24,16},{1,25},{9,1},{17,9},{25,17},{2,26},{10... | collective-permute-start | bytes 393224 | tf_op jit(solution)/shard_map/ppermute | solution.py:452
  22.0 24.9 %collective-permute-start.6 = (bf16[4,128,512]{2,1,0:T(8,128)(2,1)S(1)}, bf16[4,128,512]{2,1,0:T(8,128)(2,1)S(1)}, u32[]{:S(2)}, u32[]{:S(2)}) collective-permute-start(bf16[4,128,512]{2,1,0:T(8,128)(2,1)S(1)} %pad_maximum_fusion.refs_0_), channel_id=1, source_target_pairs={{0,4},{4,0},{1,5},{5,1},{2,6},{6,2},{3,7},{7,3},{8,12},{12,8},{9,1... | collective-permute-start | bytes 1572872 | tf_op jit(solution)/shard_map/ppermute | solution.py:466
  24.1 22.8 %collective-permute-start.7 = (bf16[4,128,512]{2,1,0:T(8,128)(2,1)S(1)}, bf16[4,128,512]{2,1,0:T(8,128)(2,1)S(1)}, u32[]{:S(2)}, u32[]{:S(2)}) collective-permute-start(bf16[4,128,512]{2,1,0:T(8,128)(2,1)S(1)} %pad_maximum_fusion.refs_0_), channel_id=1, source_target_pairs={{0,6},{2,4},{4,2},{6,0},{1,7},{3,5},{5,3},{7,1},{8,14},{10,12},{12... | collective-permute-start | bytes 1572872 | tf_op jit(solution)/shard_map/ppermute | solution.py:468
  25.1 23.0 %collective-permute-start.5 = (bf16[4,128,512]{2,1,0:T(8,128)(2,1)S(1)}, bf16[4,128,512]{2,1,0:T(8,128)(2,1)S(1)}, u32[]{:S(2)}, u32[]{:S(2)}) collective-permute-start(bf16[4,128,512]{2,1,0:T(8,128)(2,1)S(1)} %pad_maximum_fusion.refs_0_), channel_id=1, source_target_pairs={{0,2},{2,0},{1,3},{3,1},{4,6},{6,4},{5,7},{7,5},{8,10},{10,8},{9,1... | collective-permute-start | bytes 1572872 | tf_op jit(solution)/shard_map/ppermute | solution.py:466
  25.6 22.5 %collective-permute-start.12 = (bf16[128,512]{1,0:T(8,128)(2,1)S(1)}, bf16[128,512]{1,0:T(8,128)(2,1)S(1)}, u32[]{:S(2)}, u32[]{:S(2)}) collective-permute-start(bf16[128,512]{1,0:T(8,128)(2,1)S(1)} %get-tuple-element.22), channel_id=1, source_target_pairs={{0,8},{8,16},{16,24},{24,0},{1,9},{9,17},{17,25},{25,1},{2,10},{10... | collective-permute-start | bytes 393224 | tf_op jit(solution)/shard_map/ppermute | solution.py:452
  28.8 41.2 %collective-permute-start.8 = (bf16[4,128,512]{2,1,0:T(8,128)(2,1)S(1)}, bf16[4,128,512]{2,1,0:T(8,128)(2,1)S(1)}, u32[]{:S(2)}, u32[]{:S(2)}) collective-permute-start(bf16[4,128,512]{2,1,0:T(8,128)(2,1)S(1)} %pad_maximum_fusion.refs_0_), channel_id=1, source_target_pairs={{0,1},{1,0},{2,3},{3,2},{4,5},{5,4},{6,7},{7,6},{8,9},{9,8},{10,11... | collective-permute-start | bytes 1572872 | tf_op jit(solution)/shard_map/ppermute | solution.py:470
  46.9 24.2 %collective-permute-start.10 = (bf16[4,128,512]{2,1,0:T(8,128)(2,1)S(1)}, bf16[4,128,512]{2,1,0:T(8,128)(2,1)S(1)}, u32[]{:S(2)}, u32[]{:S(2)}) collective-permute-start(bf16[4,128,512]{2,1,0:T(8,128)(2,1)S(1)} %collective-permute-done.6.refs_2_), channel_id=1, source_target_pairs={{0,1},{1,0},{2,3},{3,2},{4,5},{5,4},{6,7},{7,6},{8,9},{9,8},{10,11... | collective-permute-start | bytes 1572872 | tf_op jit(solution)/shard_map/ppermute | solution.py:470
  46.9 25.3 %collective-permute-start.11 = (bf16[4,128,512]{2,1,0:T(8,128)(2,1)S(1)}, bf16[4,128,512]{2,1,0:T(8,128)(2,1)S(1)}, u32[]{:S(2)}, u32[]{:S(2)}) collective-permute-start(bf16[4,128,512]{2,1,0:T(8,128)(2,1)S(1)} %collective-permute-done.7.refs_3_), channel_id=1, source_target_pairs={{0,1},{1,0},{2,3},{3,2},{4,5},{5,4},{6,7},{7,6},{8,9},{9,8},{10,11... | collective-permute-start | bytes 1572872 | tf_op jit(solution)/shard_map/ppermute | solution.py:470
  48.1 24.0 %collective-permute-start.9 = (bf16[4,128,512]{2,1,0:T(8,128)(2,1)S(1)}, bf16[4,128,512]{2,1,0:T(8,128)(2,1)S(1)}, u32[]{:S(2)}, u32[]{:S(2)}) collective-permute-start(bf16[4,128,512]{2,1,0:T(8,128)(2,1)S(1)} %collective-permute-done.5.refs_1_), channel_id=1, source_target_pairs={{0,1},{1,0},{2,3},{3,2},{4,5},{5,4},{6,7},{7,6},{8,9},{9,8},{10,11... | collective-permute-start | bytes 1572872 | tf_op jit(solution)/shard_map/ppermute | solution.py:470
  48.1 6.8 %collective-permute-start.13 = (bf16[128,512]{1,0:T(8,128)(2,1)S(1)}, bf16[128,512]{1,0:T(8,128)(2,1)S(1)}, u32[]{:S(2)}, u32[]{:S(2)}) collective-permute-start(bf16[128,512]{1,0:T(8,128)(2,1)S(1)} %get-tuple-element.22), channel_id=1, source_target_pairs={{0,16},{8,24},{16,0},{24,8},{1,17},{9,25},{17,1},{25,9},{2,18},{10... | collective-permute-start | bytes 393224 | tf_op jit(solution)/shard_map/ppermute | solution.py:452
  54.9 8.8 %collective-permute-start.14 = (bf16[128,512]{1,0:T(8,128)(2,1)S(1)}, bf16[128,512]{1,0:T(8,128)(2,1)S(1)}, u32[]{:S(2)}, u32[]{:S(2)}) collective-permute-start(bf16[128,512]{1,0:T(8,128)(2,1)S(1)} %get-tuple-element.22), channel_id=1, source_target_pairs={{0,24},{8,0},{16,8},{24,16},{1,25},{9,1},{17,9},{25,17},{2,26},{10... | collective-permute-start | bytes 393224 | tf_op jit(solution)/shard_map/ppermute | solution.py:452
  63.7 5.0 %collective-permute-start.15 = (f32[64,512]{1,0:T(8,128)S(1)}, f32[64,512]{1,0:T(8,128)S(1)}, u32[]{:S(2)}, u32[]{:S(2)}) collective-permute-start(f32[64,512]{1,0:T(8,128)S(1)} %broadcast_select_fusion.refs_0_), channel_id=1, source_target_pairs={{0,2},{2,0},{1,3},{3,1},{4,6},{6,4},{5,7},{7,5},{8,10},{10,8},{9,1... | collective-permute-start | bytes 393224 | tf_op jit(solution)/shard_map/ppermute | solution.py:465
  68.7 31.6 %collective-permute-start.16 = (bf16[4,128,512]{2,1,0:T(8,128)(2,1)S(1)}, bf16[4,128,512]{2,1,0:T(8,128)(2,1)S(1)}, u32[]{:S(2)}, u32[]{:S(2)}) collective-permute-start(bf16[4,128,512]{2,1,0:T(8,128)(2,1)S(1)} %pad_maximum_fusion.1.refs_2_), channel_id=1, source_target_pairs={{0,2},{2,0},{1,3},{3,1},{4,6},{6,4},{5,7},{7,5},{8,10},{10,8},{9,1... | collective-permute-start | bytes 1572872 | tf_op jit(solution)/shard_map/ppermute | solution.py:478
  70.0 30.3 %collective-permute-start.17 = (bf16[4,128,512]{2,1,0:T(8,128)(2,1)S(1)}, bf16[4,128,512]{2,1,0:T(8,128)(2,1)S(1)}, u32[]{:S(2)}, u32[]{:S(2)}) collective-permute-start(bf16[4,128,512]{2,1,0:T(8,128)(2,1)S(1)} %pad_maximum_fusion.1.refs_2_), channel_id=1, source_target_pairs={{0,4},{4,0},{1,5},{5,1},{2,6},{6,2},{3,7},{7,3},{8,12},{12,8},{9,1... | collective-permute-start | bytes 1572872 | tf_op jit(solution)/shard_map/ppermute | solution.py:479
  71.1 29.2 %collective-permute-start.18 = (bf16[4,128,512]{2,1,0:T(8,128)(2,1)S(1)}, bf16[4,128,512]{2,1,0:T(8,128)(2,1)S(1)}, u32[]{:S(2)}, u32[]{:S(2)}) collective-permute-start(bf16[4,128,512]{2,1,0:T(8,128)(2,1)S(1)} %pad_maximum_fusion.1.refs_2_), channel_id=1, source_target_pairs={{0,6},{2,4},{4,2},{6,0},{1,7},{3,5},{5,3},{7,1},{8,14},{10,12},{12... | collective-permute-start | bytes 1572872 | tf_op jit(solution)/shard_map/ppermute | solution.py:480
  72.2 29.2 %collective-permute-start.19 = (bf16[4,128,512]{2,1,0:T(8,128)(2,1)S(1)}, bf16[4,128,512]{2,1,0:T(8,128)(2,1)S(1)}, u32[]{:S(2)}, u32[]{:S(2)}) collective-permute-start(bf16[4,128,512]{2,1,0:T(8,128)(2,1)S(1)} %pad_maximum_fusion.1.refs_2_), channel_id=1, source_target_pairs={{0,1},{1,0},{2,3},{3,2},{4,5},{5,4},{6,7},{7,6},{8,9},{9,8},{10,11... | collective-permute-start | bytes 1572872 | tf_op jit(solution)/shard_map/ppermute | solution.py:482
  100.3 2.1 %collective-permute-start.20 = (bf16[4,128,512]{2,1,0:T(8,128)(2,1)S(1)}, bf16[4,128,512]{2,1,0:T(8,128)(2,1)S(1)}, u32[]{:S(2)}, u32[]{:S(2)}) collective-permute-start(bf16[4,128,512]{2,1,0:T(8,128)(2,1)S(1)} %collective-permute-done.16.refs_3_), channel_id=1, source_target_pairs={{0,1},{1,0},{2,3},{3,2},{4,5},{5,4},{6,7},{7,6},{8,9},{9,8},{10,11... | collective-permute-start | bytes 1572872 | tf_op jit(solution)/shard_map/ppermute | solution.py:508
  100.9 2.3 %collective-permute-start.21 = (bf16[4,128,512]{2,1,0:T(8,128)(2,1)S(1)}, bf16[4,128,512]{2,1,0:T(8,128)(2,1)S(1)}, u32[]{:S(2)}, u32[]{:S(2)}) collective-permute-start(bf16[4,128,512]{2,1,0:T(8,128)(2,1)S(1)} %collective-permute-done.17.refs_4_), channel_id=1, source_target_pairs={{0,1},{1,0},{2,3},{3,2},{4,5},{5,4},{6,7},{7,6},{8,9},{9,8},{10,11... | collective-permute-start | bytes 1572872 | tf_op jit(solution)/shard_map/ppermute | solution.py:508
  100.9 3.0 %collective-permute-start.22 = (bf16[4,128,512]{2,1,0:T(8,128)(2,1)S(1)}, bf16[4,128,512]{2,1,0:T(8,128)(2,1)S(1)}, u32[]{:S(2)}, u32[]{:S(2)}) collective-permute-start(bf16[4,128,512]{2,1,0:T(8,128)(2,1)S(1)} %collective-permute-done.18.refs_5_), channel_id=1, source_target_pairs={{0,1},{1,0},{2,3},{3,2},{4,5},{5,4},{6,7},{7,6},{8,9},{9,8},{10,11... | collective-permute-start | bytes 1572872 | tf_op jit(solution)/shard_map/ppermute | solution.py:508
